TPU v7x, 256 devices: a whole 4x4x8 slice. The times are simulated.
256 devices in a mesh: row: 16 (over z_lo, x, core), col: 16 (over z_hi, y).
Axes of the slice: x: 4, y: 4, z: 8 (z_hi: 4, z_lo: 2; z = z_hi * 2 + z_lo), core: 2. Of those that a mesh axis runs over, the one named last changes fastest.
Arguments:
- pair_input: bfloat16 [384, 384, 128], P('row', 'col'), may hold values from -6 to 6
- norm_mean: float32 [384, 384], P('row', 'col'), may hold values from -0.5 to 0.5
- norm_scale: float32 [384, 384], P('row', 'col'), may hold values from 0.5 to 2
- pair_mask: int32 [384, 384], P('row', 'col'), may hold values 0 or 1
- cotangent: bfloat16 [384, 384, 128], P('row', 'col'), may hold values from -6 to 6
- left_gate: bfloat16 [128, 128], replicated, may hold values from -0.5 to 0.5
- left_value: bfloat16 [128, 128], replicated, may hold values from -0.5 to 0.5
- right_gate: bfloat16 [128, 128], replicated, may hold values from -0.5 to 0.5
- right_value: bfloat16 [128, 128], replicated, may hold values from -0.5 to 0.5
- output_gate: bfloat16 [128, 128], replicated, may hold values from -0.5 to 0.5
- output_weight: bfloat16 [128, 128], replicated, may hold values from -0.5 to 0.5
Outputs:
- pair_grad: float32 [384, 384, 128], P('row', 'col')
Inputs may be any that keep to these rules, and one draw needn't show every extreme that they name: `pair_mask`: 1 marks a pair that takes part.
All inputs are finite; a program needn't handle non-finite values. No bound on the sum of `pair_mask` on one device may be relied on, other than what follows from the above.
Results may differ from a plain program's by a relative error of at most 0.0072.
Values may be sent and summed in bfloat16 or wider, within the bound.
No kernel may reach another device: no remote copies, remote signals or barrier semaphores. Data moves between devices by JAX's collectives and lax.ppermute only.
A program may use at most 128 MiB of HBM per device.

v0:
```python
import jax
import jax.numpy as jnp
from jax import lax
from jax.sharding import PartitionSpec as P

epsilon = 1e-05


def layer_back(grad, normed, scale):
    centre = jnp.mean(grad, axis=-1, keepdims=True)
    along = jnp.mean(grad * normed, axis=-1, keepdims=True)
    return scale * (grad - centre - normed * along)


def column_panel(right_edge):
    return lax.all_gather(right_edge, "row", axis=0, tiled=True)


def panel_right(right_edge):
    right_cols = column_panel(right_edge)
    return lax.all_to_all(right_cols, "col", split_axis=0, concat_axis=1, tiled=True)


def panel_grad_right(grad_mix, left_rows):
    partial_right = jnp.einsum(
        "ijh,ikh->jkh", grad_mix, left_rows, preferred_element_type=jnp.float32
    )
    moved_right = lax.all_to_all(partial_right, "col", split_axis=1, concat_axis=0, tiled=True)
    return lax.psum_scatter(moved_right, "row", scatter_dimension=0, tiled=True)


def per_device(
    pair_input,
    norm_mean,
    norm_scale,
    pair_mask,
    cotangent,
    left_gate,
    left_value,
    right_gate,
    right_value,
    output_gate,
    output_weight,
):
    rows_here, cols_here, width = pair_input.shape
    hidden = left_gate.shape[1]
    flat_rows = rows_here * cols_here
    normed = (pair_input.astype(jnp.float32) - norm_mean[:, :, None]) * norm_scale[:, :, None]
    normed_low = normed.astype(jnp.bfloat16)
    stacked = jnp.concatenate([left_gate, left_value, right_gate, right_value, output_gate], axis=1)
    projected = jnp.dot(
        normed_low.reshape(flat_rows, width), stacked, preferred_element_type=jnp.float32
    )
    keep = pair_mask.reshape(flat_rows, 1).astype(jnp.float32)
    left_sig = jax.nn.sigmoid(projected[:, :hidden])
    left_lin = projected[:, hidden : 2 * hidden]
    right_sig = jax.nn.sigmoid(projected[:, 2 * hidden : 3 * hidden])
    right_lin = projected[:, 3 * hidden : 4 * hidden]
    out_sig = jax.nn.sigmoid(projected[:, 4 * hidden :])
    left_edge = (
        (left_sig * left_lin * keep).astype(jnp.bfloat16).reshape(rows_here, cols_here, hidden)
    )
    right_edge = (
        (right_sig * right_lin * keep).astype(jnp.bfloat16).reshape(rows_here, cols_here, hidden)
    )
    left_rows = lax.all_gather(left_edge, "col", axis=1, tiled=True)
    right_mine = panel_right(right_edge)
    mixed = jnp.einsum("ikh,jkh->ijh", left_rows, right_mine, preferred_element_type=jnp.float32)
    centred = mixed - jnp.mean(mixed, axis=-1, keepdims=True)
    mix_scale = lax.rsqrt(jnp.mean(centred * centred, axis=-1, keepdims=True) + epsilon)
    mix_normed = centred * mix_scale
    out_lin = jnp.dot(
        mix_normed.astype(jnp.bfloat16).reshape(flat_rows, hidden),
        output_weight,
        preferred_element_type=jnp.float32,
    )
    upstream = cotangent.reshape(flat_rows, width).astype(jnp.float32)
    grad_y = (upstream * out_sig).astype(jnp.bfloat16)
    grad_gate = upstream * out_lin * out_sig * (1.0 - out_sig)
    grad_mixnorm = jnp.dot(grad_y, output_weight.T, preferred_element_type=jnp.float32).reshape(
        rows_here, cols_here, hidden
    )
    grad_mix = layer_back(grad_mixnorm, mix_normed, mix_scale).astype(jnp.bfloat16)
    partial_left = jnp.einsum(
        "ijh,jkh->ikh", grad_mix, right_mine, preferred_element_type=jnp.float32
    )
    grad_left = lax.psum_scatter(partial_left, "col", scatter_dimension=1, tiled=True)
    grad_right = panel_grad_right(grad_mix, left_rows)
    grad_left = grad_left.reshape(flat_rows, hidden) * keep
    grad_right = grad_right.reshape(flat_rows, hidden) * keep
    pre_grads = jnp.concatenate(
        [
            grad_left * left_lin * left_sig * (1.0 - left_sig),
            grad_left * left_sig,
            grad_right * right_lin * right_sig * (1.0 - right_sig),
            grad_right * right_sig,
            grad_gate,
        ],
        axis=1,
    ).astype(jnp.bfloat16)
    grad_normed = jnp.dot(pre_grads, stacked.T, preferred_element_type=jnp.float32).reshape(
        rows_here, cols_here, width
    )
    return layer_back(grad_normed, normed, norm_scale[:, :, None])


def solution(mesh):
    placed = (
        P("row", "col", None),
        P("row", "col"),
        P("row", "col"),
        P("row", "col"),
        P("row", "col", None),
        P(),
        P(),
        P(),
        P(),
        P(),
        P(),
    )
    return jax.shard_map(
        per_device, mesh=mesh, in_specs=placed, out_specs=P("row", "col", None), check_vma=False
    )
```

profile of v0, /device:TPU:32, one launch (start us, length us, event | category | flops | bytes accessed | tf_op | source)
XLA Modules:
  0.0 451.3 jit_solution(10674677785893327585)
XLA Ops:
  8.1 0.8 constant_dynamic-update-slice_fusion.3
  8.9 0.8 constant_dynamic-update-slice_fusion.2
  11.2 1.1 fusion.14
  12.7 1.1 multiply_convert_fusion.5
  14.5 38.6 %all-gather.3.cloned.1.call-done = bf16[384,24,128]{2,1,0:T(8,128)(2,1)} async-done(((bf16[24,24,128]{2,1,0:T(8,128)(2,1)}), bf16[384,24,128]{2,1,0:T(8,128)(2,1)}) %all-gather.3.cloned.1.call-update) | async-done | bytes 2359312 | tf_op jit(solution)/shard_map/all_gather | solution.py:16
  53.2 8.8 %all-to-all-start = ((bf16[384,24,128]{2,1,0:T(8,128)(2,1)}), bf16[384,24,128]{2,1,0:T(8,128)(2,1)}, u32[]{:S(2)}, u32[]{:S(2)}) async-start(bf16[384,24,128]{2,1,0:T(8,128)(2,1)} %all-gather.3.cloned.1.call-done), calls=%async_computation | async-start | bytes 4718592 | tf_op jit(solution)/shard_map/all_to_all | solution.py:21
  62.5 82.2 %all-gather.5.cloned.1.call-done = bf16[24,384,128]{2,0,1:T(8,128)(2,1)} async-done(((bf16[24,24,128]{2,0,1:T(8,128)(2,1)}), bf16[24,384,128]{2,0,1:T(8,128)(2,1)}) %all-gather.5.cloned.1.call-update) | async-done | bytes 2359312 | tf_op jit(solution)/shard_map/all_gather | solution.py:66
  144.7 3.7 copy.82
  148.4 3.8 copy.79
  152.2 4.5 %copy.90 = bf16[24,384,128]{1,0,2:T(8,128)(2,1)} copy(bf16[24,384,128]{2,1,0:T(8,128)(2,1)} %bitcast.61) | data formatting | bytes 4718592 | tf_op jit(solution)/shard_map/all_to_all | solution.py:21
  156.7 3.9 bitcast_reduce_fusion
  160.7 1.9 copy.83
  163.4 1.0 fusion.16
  164.9 4.8 %convolution_bitcast_fusion.1 = f32[24,384,128]{1,0,2:T(8,128)} fusion(bf16[24,384,128]{1,0,2:T(8,128)(2,1)} %copy.90, bf16[24,24,128]{0,1,2:T(8,128)(2,1)S(1)} %copy.95), kind=kOutput, calls=%fused_computation.1 | convolution fusion | flops 56623104 | bytes 7225344 | tf_op jit(solution)/shard_map/ijh,jkh->ikh/dot_general | solution.py:84
  169.8 6.1 %copy.92 = f32[24,384,128]{2,0,1:T(8,128)} copy(f32[24,384,128]{1,0,2:T(8,128)} %convolution_bitcast_fusion.1) | data formatting | bytes 9437184 | tf_op jit(solution)/shard_map/ijh,jkh->ikh/transpose | solution.py:84
  175.9 3.1 convolution_bitcast_fusion
  179.0 6.1 %copy.96 = f32[24,384,128]{2,0,1:T(8,128)} copy(f32[24,384,128]{1,0,2:T(8,128)} %convolution_bitcast_fusion) | data formatting | bytes 9437184 | tf_op jit(solution)/shard_map/ijh,ikh->jkh/transpose | solution.py:25
  185.1 145.2 %all_to_all.36 = f32[24,384,128]{2,0,1:T(8,128)S(1)} all-to-all(f32[24,384,128]{2,0,1:T(8,128)} %copy.96), channel_id=1, replica_groups=mesh['row'=16,'col'=16] {'col'}, dimensions={1} | all-to-all | bytes 9437184 | tf_op jit(solution)/shard_map/all_to_all | solution.py:28
  330.3 3.0 copy.98
  333.3 36.7 %reduce-scatter.3.cloned.1.call-done = f32[24,24,128]{2,0,1:T(8,128)} async-done(((f32[24,384,128]{2,0,1:T(8,128)}), f32[24,24,128]{2,0,1:T(8,128)}) %reduce-scatter.3.cloned.1.call-update) | async-done | bytes 294928 | tf_op jit(solution)/shard_map/reduce_scatter | solution.py:87
  370.0 1.0 copy.93
  371.1 69.8 %reduce-scatter.5.cloned.1.call-done = f32[24,24,128]{2,1,0:T(8,128)} async-done(((f32[384,24,128]{2,1,0:T(8,128)}), f32[24,24,128]{2,1,0:T(8,128)}) %reduce-scatter.5.cloned.1.call-update) | async-done | bytes 294928 | tf_op jit(solution)/shard_map/reduce_scatter | solution.py:29
  440.9 1.2 multiply_convert_fusion
  443.6 1.1 subtract_multiply_fusion
  (60 shorter events, 7.6 us)
Async XLA Ops:
  6.5 55.5 %copy-start = (bf16[128,128]{1,0:T(8,128)(2,1)S(1)}, bf16[128,128]{1,0:T(8,128)(2,1)}, u32[]{:S(2)}) copy-start(bf16[128,128]{1,0:T(8,128)(2,1)} %param.21) | copy-start | bytes 98308
  6.5 46.6 %all-gather.3.cloned.1.call-start = ((), (), s32[]{:S(2)}) async-start(), calls=%async_computation.4 | async-start | bytes 2506752 | tf_op jit(solution)/shard_map/all_gather | solution.py:16
  12.7 49.3 %copy-start.1 = (f32[576,640]{1,0:T(8,128)}, f32[576,640]{1,0:T(8,128)S(1)}, u32[]{:S(2)}) copy-start(f32[576,640]{1,0:T(8,128)S(1)} %fusion.23) | copy-start | bytes 4423684
  13.8 130.9 %all-gather.5.cloned.1.call-start = ((), (), s32[]{:S(2)}) async-start(), calls=%async_computation.5 | async-start | bytes 2506752 | tf_op jit(solution)/shard_map/all_gather | solution.py:66
  14.5 47.5 %copy-start.7 = (bf16[24,24,128]{2,1,0:T(8,128)(2,1)S(1)}, bf16[24,24,128]{2,1,0:T(8,128)(2,1)}, u32[]{:S(2)}) copy-start(bf16[24,24,128]{2,1,0:T(8,128)(2,1)} %param.15) | copy-start | bytes 442372
  53.2 95.2 %all-to-all-start = ((bf16[384,24,128]{2,1,0:T(8,128)(2,1)}), bf16[384,24,128]{2,1,0:T(8,128)(2,1)}, u32[]{:S(2)}, u32[]{:S(2)}) async-start(bf16[384,24,128]{2,1,0:T(8,128)(2,1)} %all-gather.3.cloned.1.call-done), calls=%async_computation | async-start | bytes 4718592 | tf_op jit(solution)/shard_map/all_to_all | solution.py:21
  61.9 308.1 %reduce-scatter.3.cloned.1.call-start = ((), (), s32[]{:S(2)}) async-start(), calls=%async_computation.6 | async-start | bytes 5013504 | tf_op jit(solution)/shard_map/reduce_scatter | solution.py:87
  175.8 265.0 %reduce-scatter.5.cloned.1.call-start = ((), (), s32[]{:S(2)}) async-start(), calls=%async_computation.7 | async-start | bytes 5013504 | tf_op jit(solution)/shard_map/reduce_scatter | solution.py:29
  333.3 107.6 %copy-start.2 = (f32[576,640]{1,0:T(8,128)S(1)}, f32[576,640]{1,0:T(8,128)}, u32[]{:S(2)}) copy-start(f32[576,640]{1,0:T(8,128)} %copy-done.1) | copy-start | bytes 4423684
  333.3 109.0 %copy-start.4 = (bf16[24,24,128]{2,1,0:T(8,128)(2,1)S(1)}, bf16[24,24,128]{2,1,0:T(8,128)(2,1)}, u32[]{:S(2)}) copy-start(bf16[24,24,128]{2,1,0:T(8,128)(2,1)} %get-tuple-element.13) | copy-start | bytes 442372
  333.3 109.0 %copy-start.8 = (bf16[24,24,128]{2,1,0:T(8,128)(2,1)S(1)}, bf16[24,24,128]{2,1,0:T(8,128)(2,1)}, u32[]{:S(2)}) copy-start(bf16[24,24,128]{2,1,0:T(8,128)(2,1)} %param.15) | copy-start | bytes 442372
  442.1 1.0 copy-start.3
  442.1 1.0 copy-start.5
  442.2 1.0 copy-start.6
Sparse Core Ops, SparseCore 0:
  13.9 39.2 all-gather.2
  55.6 89.0 all-gather.4
  176.0 194.0 reduce-scatter.2
  372.5 68.3 reduce-scatter.4
where the time goes:
time: 454 us; the launch traced here: 451 us
  waiting for transfers between devices  227 us (50%)
  blocking collectives  145 us (32%)
  local copies, waits for them, and re-layouts  35.9 us (8%)
  between operations  13.4 us (3%)
  matrix products  13.2 us (3%)
  starting transfers between devices  8.88 us (2%)
  other arithmetic  7.22 us (2%)
    all_to_all x1, blocking collectives, panel_grad_right(): lax.all_to_all(partial_right, 'col', split_axis=1, concat_axis=0, tiled=T...  145 us
    all_gather x1, waiting for transfers between devices, per_device(): left_rows = lax.all_gather(left_edge, 'col', axis=1, tiled=True)  82.2 us
    reduce_scatter x1, waiting for transfers between devices, panel_grad_right(): return lax.psum_scatter(moved_right, 'row', scatter_dimension=0, tiled=True)  69.8 us
    all_gather x1, waiting for transfers between devices, column_panel(): return lax.all_gather(right_edge, 'row', axis=0, tiled=True)  38.6 us
    reduce_scatter x1, waiting for transfers between devices, per_device(): lax.psum_scatter(partial_left, 'col', scatter_dimension=1, tiled=True)  36.7 us
  transfers between devices with their start and end apart: 5, of which 4 were waited for; matrix products, arithmetic and copies ran while one was open for 4% of the time, Pallas kernels for 0%

commit v1 on v0

v1 whole, which is shorter than its diff:
```python
import jax
import jax.numpy as jnp
from jax import lax
from jax.experimental import pallas as pl
from jax.experimental.pallas import tpu as pltpu
from jax.sharding import Mesh, PartitionSpec as P

epsilon = 1e-05
SIDE = 24
BLOCKS = 16
PAIRS = SIDE * SIDE
WIDTH = 128
HALF = 64
XS = 4
QUARTER = XS * SIDE
TOKENS = SIDE * BLOCKS
SPREAD = ("x", "z_hi", "y")
f32 = jnp.float32
bf16 = jnp.bfloat16


def dot(a, b, over=((1,), (0,))):
    return lax.dot_general(a, b, (over, ((), ())), preferred_element_type=f32)


def columns(ref):
    turned = jnp.transpose(ref[...].astype(f32))
    return jnp.concatenate([turned[:, i : i + 1] for i in range(SIDE)], axis=0)


def lanes(rows):
    return lax.broadcasted_iota(jnp.int32, (rows, WIDTH), 1)


def roll(value, by):
    by = by % WIDTH
    return value if by == 0 else pltpu.roll(value, by, 1)


def place(c):
    return ((c // 8) * 2 + c % 2) * XS + (c // 2) % XS


def layer_back(grad, normed, scale):
    centre = jnp.mean(grad, axis=-1, keepdims=True)
    along = jnp.mean(grad * normed, axis=-1, keepdims=True)
    return scale * (grad - centre - normed * along)


def spread_rows(parts, scratch):
    count = len(parts)
    step = count * SIDE
    per = WIDTH // step if count == 2 else 4
    low = lanes(HALF) < step
    for first in range(0, SIDE, per):
        stack = []
        for i in range(first, first + per):
            stack += [part[i * SIDE : (i + 1) * SIDE] for part in parts]
        stack.append(jnp.zeros((WIDTH - per * step, WIDTH), f32))
        turned = jnp.transpose(jnp.concatenate(stack, axis=0))
        for p in range(per):
            row = jnp.where(low, roll(turned[:HALF], -p * step), roll(turned[HALF:], step - p * step))
            scratch[pl.ds(first + p, HALF, stride=SIDE), :] = row


def gather_rows(scratch, combine):
    low = lanes(SIDE) < HALF
    found = []
    for first in range(0, SIDE, 2):
        stack = [scratch[pl.ds(first + p, HALF, stride=SIDE), :] for p in range(2)]
        pairs = combine(jnp.transpose(jnp.concatenate(stack, axis=0)))
        found.append([jnp.where(low, a, roll(b, HALF)) for a, b in pairs])
        found.append([jnp.where(low, roll(a, HALF), b) for a, b in pairs])
    return [jnp.concatenate([row[n] for row in found], axis=0) for n in range(len(found[0]))]


def assemble(messages, x, offset, spot):
    lane = lanes(SIDE)
    order = {spot(c): c for c in range(BLOCKS)}
    tiles = []
    for t in range(TOKENS // WIDTH):
        tile = None
        for at in range(BLOCKS):
            begin, end = at * SIDE - t * WIDTH, (at + 1) * SIDE - t * WIDTH
            if end <= 0 or begin >= WIDTH:
                continue
            piece = roll(messages(x * BLOCKS + order[at]), begin - offset)
            tile = piece if tile is None else jnp.where(lane >= begin, piece, tile)
        tiles.append(tile)
    return jnp.concatenate(tiles, axis=1)


def extract(wide, at, offset):
    begin = at * SIDE
    first, last = begin // WIDTH, (begin + SIDE - 1) // WIDTH
    shift = offset - begin
    piece = roll(wide[:, first * WIDTH : (first + 1) * WIDTH], shift)
    if last != first:
        other = roll(wide[:, last * WIDTH : (last + 1) * WIDTH], shift)
        piece = jnp.where(lanes(SIDE) < offset + last * WIDTH - begin, piece, other)
    return piece


def normalise(pair_ref, mean_ref, scale_ref):
    scale = columns(scale_ref)
    normed = (pair_ref[...].astype(f32) - columns(mean_ref)) * scale
    return normed, scale


def edges_kernel(pair_ref, mean_ref, scale_ref, mask_ref, lg, lv, rg, rv, out_ref, scratch):
    normed, _ = normalise(pair_ref, mean_ref, scale_ref)
    low = normed.astype(bf16)
    keep = columns(mask_ref)
    left = jax.nn.sigmoid(dot(low, lg[...])) * dot(low, lv[...]) * keep
    right = jax.nn.sigmoid(dot(low, rg[...])) * dot(low, rv[...]) * keep
    spread_rows([left, right], scratch)
    out_ref[...] = scratch[...].reshape(HALF, SIDE, WIDTH).astype(bf16)


def assemble_kernel(edge, in_ref, out_ref):
    for x in range(XS):
        for ch in range(2):
            wide = assemble(lambda n: in_ref[n].astype(f32), x, (2 * ch + edge) * SIDE, lambda c: c)
            out_ref[ch, x * SIDE : (x + 1) * SIDE, :] = wide.astype(bf16)


def mixed_kernel(left_ref, r0, r1, r2, r3, right_ref, out_ref):
    own = lax.axis_index("z_lo") * 2 + lax.axis_index("core")
    for p, part in enumerate((r0, r1, r2, r3)):
        right_ref[own ^ p] = part[...]
    mixed = []
    for ch in range(2):
        right = right_ref[:, ch].reshape(TOKENS, TOKENS)
        mixed.append(dot(left_ref[ch], right, ((1,), (1,))))
    lane = lanes(SIDE)
    for x in range(XS):
        rows = [m[x * SIDE : (x + 1) * SIDE] for m in mixed]
        for c in range(BLOCKS):
            both = jnp.where(lane < SIDE, extract(rows[0], place(c), 0), extract(rows[1], place(c), SIDE))
            high = both.astype(bf16).astype(f32)
            rest = roll(both - high, 2 * SIDE)
            out_ref[x * BLOCKS + c] = jnp.where(lane < 2 * SIDE, high, rest).astype(bf16)


def middle_kernel(
    in_ref, pair_ref, mean_ref, scale_ref, cot_ref, gate_ref, weight_ref, out_ref, grad_gate_ref, scratch
):
    scratch[...] = in_ref[...].astype(f32).reshape(HALF * SIDE, WIDTH)

    def combine(turned):
        both = turned[: 2 * SIDE] + turned[2 * SIDE : 4 * SIDE]
        return [(both[:SIDE], both[SIDE:])]

    (mixed,) = gather_rows(scratch, combine)
    normed, _ = normalise(pair_ref, mean_ref, scale_ref)
    out_sig = jax.nn.sigmoid(dot(normed.astype(bf16), gate_ref[...]))
    upstream = cot_ref[...].astype(f32)
    grad_y = (upstream * out_sig).astype(bf16)
    grad_mixnorm = dot(grad_y, weight_ref[...], ((1,), (1,)))
    centred = mixed - jnp.mean(mixed, axis=-1, keepdims=True)
    mix_scale = lax.rsqrt(jnp.mean(centred * centred, axis=-1, keepdims=True) + epsilon)
    mix_normed = centred * mix_scale
    out_lin = dot(mix_normed.astype(bf16), weight_ref[...])
    grad_gate_ref[...] = (upstream * out_lin * out_sig * (1.0 - out_sig)).astype(bf16)
    grad_mix = layer_back(grad_mixnorm, mix_normed, mix_scale)
    spread_rows([grad_mix], scratch)
    out_ref[...] = scratch[...].reshape(HALF, SIDE, WIDTH).astype(bf16)


def right_grad_kernel(in_ref, left_ref, grad_ref, own_ref, s1, s2, s3):
    for ch in range(2):
        for x in range(XS):
            wide = assemble(lambda n: in_ref[n].astype(f32), x, ch * SIDE, place)
            grad_ref[ch, x * SIDE : (x + 1) * SIDE, :] = wide.astype(bf16)
    own = lax.axis_index("z_lo") * 2 + lax.axis_index("core")
    for ch in range(2):
        turned = jnp.transpose(grad_ref[ch].astype(f32)).astype(bf16)
        s1_s = dot(turned, left_ref[ch])
        for q in range(4):
            rows = s1_s[q * QUARTER : (q + 1) * QUARTER]
            for p, ref in enumerate((own_ref, s1, s2, s3)):

                @pl.when((own ^ p) == q)
                def _(rows=rows, ref=ref, ch=ch):
                    ref[ch] = rows.astype(ref.dtype)


def left_grad_kernel(grad_ref, right_ref, out_ref):
    for ch in range(2):
        right = right_ref[:, ch].reshape(TOKENS, TOKENS)
        out_ref[ch] = dot(grad_ref[ch], right)


def return_kernel(left_ref, r0, r1, r2, r3, out_ref):
    lane = lanes(SIDE)
    for x in range(XS):
        here = slice(x * SIDE, (x + 1) * SIDE)
        wides = []
        for ch in range(2):
            total = r0[ch, here]
            for part in (r1, r2, r3):
                total = total + part[ch, here].astype(f32)
            wides += [left_ref[ch, here], total]
        for c in range(BLOCKS):
            tile = extract(wides[0], c, 0)
            for n in range(1, 4):
                tile = jnp.where(lane >= n * SIDE, extract(wides[n], c, n * SIDE), tile)
            out_ref[x * BLOCKS + c] = tile.astype(bf16)


def last_kernel(
    in_ref, pair_ref, mean_ref, scale_ref, mask_ref, grad_gate_ref, lg, lv, rg, rv, og, out_ref, scratch
):
    scratch[...] = in_ref[...].astype(f32).reshape(HALF * SIDE, WIDTH)

    def combine(turned):
        cut = [turned[n * SIDE : (n + 1) * SIDE] for n in range(4)]
        return [(cut[0], cut[2]), (cut[1], cut[3])]

    grad_left, grad_right = gather_rows(scratch, combine)
    normed, scale = normalise(pair_ref, mean_ref, scale_ref)
    low = normed.astype(bf16)
    keep = columns(mask_ref)
    over = ((1,), (1,))
    grad_normed = dot(grad_gate_ref[...], og[...], over)
    for grad, gate, value in ((grad_left, lg, lv), (grad_right, rg, rv)):
        sig = jax.nn.sigmoid(dot(low, gate[...]))
        lin = dot(low, value[...])
        kept = grad * keep
        grad_normed += dot((kept * lin * sig * (1.0 - sig)).astype(bf16), gate[...], over)
        grad_normed += dot((kept * sig).astype(bf16), value[...], over)
    out_ref[...] = layer_back(grad_normed, normed, scale)


def call(kernel, outs, *args, scratch=False, name=None):
    return pl.pallas_call(
        kernel,
        out_shape=[jax.ShapeDtypeStruct(shape, dtype) for shape, dtype in outs],
        in_specs=[pl.BlockSpec(memory_space=pltpu.VMEM) for _ in args],
        out_specs=[pl.BlockSpec(memory_space=pltpu.VMEM) for _ in outs],
        scratch_shapes=[pltpu.VMEM((HALF * SIDE, WIDTH), f32)] if scratch else [],
        compiler_params=pltpu.CompilerParams(vmem_limit_bytes=48 * 1024 * 1024),
        name=name,
    )(*args)


def spread(messages):
    return lax.all_to_all(messages, SPREAD, 0, 0, tiled=True)


def swap(value, axis):
    return lax.ppermute(value, axis, [(0, 1), (1, 0)])


def per_device(
    pair_input,
    norm_mean,
    norm_scale,
    pair_mask,
    cotangent,
    left_gate,
    left_value,
    right_gate,
    right_value,
    output_gate,
    output_weight,
):
    pair = pair_input.reshape(PAIRS, WIDTH)
    cot = cotangent.reshape(PAIRS, WIDTH)
    message = ((HALF, SIDE, WIDTH), bf16)
    panel = ((2, QUARTER, TOKENS), bf16)
    (sent,) = call(
        edges_kernel, [message], pair, norm_mean, norm_scale, pair_mask, left_gate, left_value, right_gate, right_value,
        scratch=True, name="edges",
    )
    came = spread(sent)
    (right_own,) = call(lambda *r: assemble_kernel(1, *r), [panel], came, name="take_right")
    right_z = swap(right_own, "z_lo")
    right_core = swap(right_own, "core")
    (left,) = call(lambda *r: assemble_kernel(0, *r), [panel], came, name="take_left")
    right_both = swap(right_z, "core")
    right, sent = call(
        mixed_kernel, [((4, 2, QUARTER, TOKENS), bf16), message], left, right_own, right_core, right_z, right_both,
        name="mix",
    )
    came = spread(sent)
    sent, grad_gate = call(
        middle_kernel, [message, ((PAIRS, WIDTH), bf16)], came, pair, norm_mean, norm_scale, cot, output_gate,
        output_weight, scratch=True, name="middle",
    )
    came = spread(sent)
    grad, own, s1, s2, s3 = call(
        right_grad_kernel, [panel, ((2, QUARTER, TOKENS), f32), panel, panel, panel], came, left, name="right_grad"
    )
    s3 = lax.ppermute(s3, ("z_lo", "core"), [(0, 3), (3, 0), (1, 2), (2, 1)])
    s2 = swap(s2, "z_lo")
    s1 = swap(s1, "core")
    (grad_left,) = call(left_grad_kernel, [((2, QUARTER, TOKENS), f32)], grad, right, name="left_grad")
    (sent,) = call(return_kernel, [message], grad_left, own, s1, s2, s3, name="return")
    came = spread(sent)
    (out,) = call(
        last_kernel, [((PAIRS, WIDTH), f32)], came, pair, norm_mean, norm_scale, pair_mask, grad_gate, left_gate,
        left_value, right_gate, right_value, output_gate, scratch=True, name="last",
    )
    return out.reshape(SIDE, SIDE, WIDTH)


def solution(mesh):
    fine = Mesh(mesh.devices.reshape(2, 4, 2, 4, 4), ("z_lo", "x", "core", "z_hi", "y"))
    row, col = ("z_lo", "x", "core"), ("z_hi", "y")
    placed = (P(row, col, None), P(row, col), P(row, col), P(row, col), P(row, col, None)) + (P(),) * 6
    return jax.shard_map(per_device, mesh=fine, in_specs=placed, out_specs=P(row, col, None), check_vma=False)
```

time: 454 us -> 131 us (0.29)
  waiting for transfers between devices: 227 us -> 12.2 us
  blocking collectives: 145 us -> 98.2 us
  local copies, waits for them, and re-layouts: 35.9 us -> 6.13 us
  matrix products: 13.2 us -> 0 us
  between operations: 13.4 us -> 0.23 us
  Pallas kernels: 0 us -> 9.43 us
  other arithmetic: 7.22 us -> 0 us
  starting transfers between devices: 8.88 us -> 3.6 us
    all_gather x2 -> x0, waiting for transfers between devices: 121 us -> none  [the longest x1 82.2 us: per_device(): left_rows = lax.all_gather(left_edge, 'col', axis=1, tiled=True)]
    reduce_scatter x2 -> x0, waiting for transfers between devices: 107 us -> none  [the longest x1 69.8 us: panel_grad_right(): return lax.psum_scatter(moved_right, 'row', scatter_dimension=0, tiled=True)]
    all_to_all x1 -> x4, blocking collectives: 145 us -> 98.2 us  [spread(): return lax.all_to_all(messages, SPREAD, 0, 0, tiled=True)]
    dot_general x7 -> x0, matrix products: 13.2 us -> none  [the longest x1 4.85 us: per_device(): jnp.einsum('ijh,jkh->ikh', grad_mix, right_mine, preferred_element_type=j...]
    ppermute x0 -> x6, waiting for transfers between devices: none -> 12.2 us  [the longest x5 9.63 us: swap(): return lax.ppermute(value, axis, [(0, 1), (1, 0)])]
    transpose x2 -> x0, local copies, waits for them, and re-layouts: 12.2 us -> none  [the longest x1 6.09 us: panel_grad_right(): jnp.einsum('ijh,ikh->jkh', grad_mix, left_rows, preferred_element_type=jn...]
    all_to_all x3 -> x0, local copies, waits for them, and re-layouts: 11.2 us -> none  [the longest x2 8.27 us: panel_right(): lax.all_to_all(right_cols, 'col', split_axis=0, concat_axis=1, tiled=True)]
    pallas_call x0 -> x9, Pallas kernels: none -> 9.43 us  [call(): pl.pallas_call(kernel, out_shape=[jax.ShapeDtypeStruct(shape, dtype) for...]
  transfers between devices with their start and end apart: 5 -> 6, of which waited for: 4 -> 4; matrix products, arithmetic and copies ran while one was open for 4% -> 0% of each run, Pallas kernels for 0% -> 0%
where the time goes in v1:
time: 131 us; the launch traced here: 130 us
  blocking collectives  98.2 us (75%)
  waiting for transfers between devices  12.2 us (9%)
  Pallas kernels  9.43 us (7%)
  local copies, waits for them, and re-layouts  6.13 us (5%)
  starting transfers between devices  3.6 us (3%)
    all_to_all x4, blocking collectives, spread(): return lax.all_to_all(messages, SPREAD, 0, 0, tiled=True)  98.2 us
    ppermute x5, waiting for transfers between devices, swap(): return lax.ppermute(value, axis, [(0, 1), (1, 0)])  9.63 us
    pallas_call x9, Pallas kernels, call(): pl.pallas_call(kernel, out_shape=[jax.ShapeDtypeStruct(shape, dtype) for...  9.43 us
    unnamed x38, local copies, waits for them, and re-layouts  6.13 us
    ppermute x5, starting transfers between devices, swap(): return lax.ppermute(value, axis, [(0, 1), (1, 0)])  3.55 us
  transfers between devices with their start and end apart: 6, of which 4 were waited for; matrix products, arithmetic and copies ran while one was open for 0% of the time, Pallas kernels for 0%

profile of v1, /device:TPU:32, one launch (start us, length us, event | category | flops | bytes accessed | tf_op | source)
XLA Modules:
  0.0 129.8 jit_solution(17230300189467847079)
XLA Ops:
  0.0 0.9 copy-done
  0.9 0.8 copy-done.3
  1.7 0.8 copy-done.5
  2.4 0.8 copy-done.7
  3.2 0.8 copy-done.9
  3.9 0.7 copy-done.12
  4.7 0.7 copy-done.14
  5.4 0.7 copy-done.16
  6.1 1.3 edges.1
  7.3 31.3 %all_to_all.20.r_0_ = bf16[64,24,128]{2,1,0:T(8,128)(2,1)S(1)} all-to-all(bf16[64,24,128]{2,1,0:T(8,128)(2,1)S(1)} %edges.1), channel_id=1, replica_groups=mesh['z_lo'=2,'x'=4,'core'=2,'z_hi'=4,'y'=4] {'x','z_hi','y'}, dimensions={0} | all-to-all | bytes 786432 | tf_op jit(solution)/shard_map/all_to_all | solution.py:248
  38.9 1.1 collective-permute-start.1
  40.0 4.2 %collective-permute-done.1.r2 = bf16[2,96,384]{2,1,0:T(8,128)(2,1)S(1)} collective-permute-done((bf16[2,96,384]{2,1,0:T(8,128)(2,1)S(1)}, bf16[2,96,384]{2,1,0:T(8,128)(2,1)S(1)}, u32[]{:S(2)}, u32[]{:S(2)}) %collective-permute-start.1) | collective-permute-done | bytes 147488 | tf_op jit(solution)/shard_map/ppermute | solution.py:252
  44.4 1.1 collective-permute-done.2.r3
  45.5 1.9 %mix.1 = (bf16[4,2,96,384]{3,2,1,0:T(8,128)(2,1)S(1)}, bf16[64,24,128]{2,1,0:T(8,128)(2,1)S(1)}) custom-call(bf16[2,96,384]{2,1,0:T(8,128)(2,1)S(1)} %take_left.1.left_ref, bf16[2,96,384]{2,1,0:T(8,128)(2,1)S(1)} %take_right.1.r0, bf16[2,96,384]{2,1,0:T(8,128)(2,1)S(1)} %collective-permute-done.r1, bf16[2,96,384]{2,1,0:T(8,128)(2,1)S(1)} %collective-permute-done.1.r2, ...), custom_call_target="tpu_custom_call" | custom-call | tf_op jit(solution)/shard_map/mix/pallas_call | solution.py:236
  47.5 21.1 %all_to_all.21.in_ref = bf16[64,24,128]{2,1,0:T(8,128)(2,1)S(1)} all-to-all(bf16[64,24,128]{2,1,0:T(8,128)(2,1)S(1)} %get-tuple-element.14), channel_id=1, replica_groups=mesh['z_lo'=2,'x'=4,'core'=2,'z_hi'=4,'y'=4] {'x','z_hi','y'}, dimensions={0} | all-to-all | bytes 786432 | tf_op jit(solution)/shard_map/all_to_all | solution.py:248
  68.6 1.7 %middle.1 = (bf16[64,24,128]{2,1,0:T(8,128)(2,1)S(1)}, bf16[576,128]{1,0:T(8,128)(2,1)S(1)}) custom-call(bf16[64,24,128]{2,1,0:T(8,128)(2,1)S(1)} %all_to_all.21.in_ref, bf16[576,128]{1,0:T(8,128)(2,1)S(1)} %bitcast.4, f32[24,24]{1,0:T(8,128)S(1)} %copy-done.13, f32[24,24]{1,0:T(8,128)S(1)} %copy-done.15, bf16[576,128]{1,0:T(8,128)(2,1)S(1)} %bitcast.6, ...), custom_call_target="tpu_custom_call" | custom-call | tf_op jit(solution)/shard_map/middle/pallas_call | solution.py:236
  70.3 22.5 %all_to_all.22.in_ref = bf16[64,24,128]{2,1,0:T(8,128)(2,1)S(1)} all-to-all(bf16[64,24,128]{2,1,0:T(8,128)(2,1)S(1)} %get-tuple-element.15), channel_id=1, replica_groups=mesh['z_lo'=2,'x'=4,'core'=2,'z_hi'=4,'y'=4] {'x','z_hi','y'}, dimensions={0} | all-to-all | bytes 786432 | tf_op jit(solution)/shard_map/all_to_all | solution.py:248
  92.7 0.9 right_grad.1
  93.8 2.4 %collective-permute-start.4 = (bf16[2,96,384]{2,1,0:T(8,128)(2,1)S(1)}, bf16[2,96,384]{2,1,0:T(8,128)(2,1)S(1)}, u32[]{:S(2)}, u32[]{:S(2)}) collective-permute-start(bf16[2,96,384]{2,1,0:T(8,128)(2,1)S(1)} %get-tuple-element.20), channel_id=1, source_target_pairs={{0,128},{128,0},{1,129},{129,1},{2,130},{130,2},{3,131},{131,3},{4... | collective-permute-start | bytes 442376 | tf_op jit(solution)/shard_map/ppermute | solution.py:252
  96.5 4.4 %collective-permute-done.4.r2 = bf16[2,96,384]{2,1,0:T(8,128)(2,1)S(1)} collective-permute-done((bf16[2,96,384]{2,1,0:T(8,128)(2,1)S(1)}, bf16[2,96,384]{2,1,0:T(8,128)(2,1)S(1)}, u32[]{:S(2)}, u32[]{:S(2)}) %collective-permute-start.4) | collective-permute-done | bytes 147488 | tf_op jit(solution)/shard_map/ppermute | solution.py:252
  100.8 2.6 %collective-permute-done.5.r3 = bf16[2,96,384]{2,1,0:T(8,128)(2,1)S(1)} collective-permute-done((bf16[2,96,384]{2,1,0:T(8,128)(2,1)S(1)}, bf16[2,96,384]{2,1,0:T(8,128)(2,1)S(1)}, u32[]{:S(2)}, u32[]{:S(2)}) %collective-permute-start.5) | collective-permute-done | bytes 147488 | tf_op jit(solution)/shard_map/ppermute | solution.py:295
  103.4 0.5 return.1
  104.0 23.3 %all_to_all.23.in_ref = bf16[64,24,128]{2,1,0:T(8,128)(2,1)S(1)} all-to-all(bf16[64,24,128]{2,1,0:T(8,128)(2,1)S(1)} %return.1), channel_id=1, replica_groups=mesh['z_lo'=2,'x'=4,'core'=2,'z_hi'=4,'y'=4] {'x','z_hi','y'}, dimensions={0} | all-to-all | bytes 786432 | tf_op jit(solution)/shard_map/all_to_all | solution.py:248
  127.3 2.5 %last.1 = f32[576,128]{1,0:T(8,128)} custom-call(bf16[64,24,128]{2,1,0:T(8,128)(2,1)S(1)} %all_to_all.23.in_ref, bf16[576,128]{1,0:T(8,128)(2,1)S(1)} %bitcast.5, f32[24,24]{1,0:T(8,128)S(1)} %copy-done.13, f32[24,24]{1,0:T(8,128)S(1)} %copy-done.15, s32[24,24]{1,0:T(8,128)S(1)} %copy-done.17, bf16[576,128]{1,0:T(8,128)(2,1)S(1)} %get-tuple-element.22.grad_gate_ref, ...), custom_call_target="tpu_custom_call" | custom-call | tf_op jit(solution)/shard_map/last/pallas_call | solution.py:236
  (39 shorter events, 1.0 us)
Async XLA Ops:
  0.0 0.9 copy-start
  0.9 0.8 copy-start.3
  1.7 0.8 copy-start.5
  2.4 0.8 copy-start.7
  3.2 0.8 copy-start.9
  3.9 0.7 copy-start.12
  4.7 0.7 copy-start.14
  38.9 5.2 %collective-permute-start.1 = (bf16[2,96,384]{2,1,0:T(8,128)(2,1)S(1)}, bf16[2,96,384]{2,1,0:T(8,128)(2,1)S(1)}, u32[]{:S(2)}, u32[]{:S(2)}) collective-permute-start(bf16[2,96,384]{2,1,0:T(8,128)(2,1)S(1)} %take_right.1.r0), channel_id=1, source_target_pairs={{0,128},{128,0},{1,129},{129,1},{2,130},{130,2},{3,131},{131,3},{4... | collective-permute-start | bytes 442376 | tf_op jit(solution)/shard_map/ppermute | solution.py:252
  40.0 4.4 %collective-permute-start = (bf16[2,96,384]{2,1,0:T(8,128)(2,1)S(1)}, bf16[2,96,384]{2,1,0:T(8,128)(2,1)S(1)}, u32[]{:S(2)}, u32[]{:S(2)}) collective-permute-start(bf16[2,96,384]{2,1,0:T(8,128)(2,1)S(1)} %take_right.1.r0), channel_id=1, source_target_pairs={{0,16},{16,0},{1,17},{17,1},{2,18},{18,2},{3,19},{19,3},{4,20},{20... | collective-permute-start | bytes 442376 | tf_op jit(solution)/shard_map/ppermute | solution.py:252
  44.2 1.4 %collective-permute-start.2 = (bf16[2,96,384]{2,1,0:T(8,128)(2,1)S(1)}, bf16[2,96,384]{2,1,0:T(8,128)(2,1)S(1)}, u32[]{:S(2)}, u32[]{:S(2)}) collective-permute-start(bf16[2,96,384]{2,1,0:T(8,128)(2,1)S(1)} %collective-permute-done.1.r2), channel_id=1, source_target_pairs={{0,16},{16,0},{1,17},{17,1},{2,18},{18,2},{3,19},{19,3},{4,20},{20... | collective-permute-start | bytes 442376 | tf_op jit(solution)/shard_map/ppermute | solution.py:252
  47.4 21.1 %copy-start.1 = (bf16[24,24,128]{2,1,0:T(8,128)(2,1)S(1)}, bf16[24,24,128]{2,1,0:T(8,128)(2,1)}, u32[]{:S(2)}) copy-start(bf16[24,24,128]{2,1,0:T(8,128)(2,1)} %param.11) | copy-start | bytes 442372
  47.4 21.1 %copy-start.2 = (bf16[24,24,128]{2,1,0:T(8,128)(2,1)S(1)}, bf16[24,24,128]{2,1,0:T(8,128)(2,1)}, u32[]{:S(2)}) copy-start(bf16[24,24,128]{2,1,0:T(8,128)(2,1)} %param.15) | copy-start | bytes 442372
  47.4 21.1 %copy-start.11 = (bf16[128,128]{1,0:T(8,128)(2,1)S(1)}, bf16[128,128]{1,0:T(8,128)(2,1)}, u32[]{:S(2)}) copy-start(bf16[128,128]{1,0:T(8,128)(2,1)} %og.1) | copy-start | bytes 98308
  47.4 21.1 %copy-start.13 = (f32[24,24]{1,0:T(8,128)S(1)}, f32[24,24]{1,0:T(8,128)}, u32[]{:S(2)}) copy-start(f32[24,24]{1,0:T(8,128)} %mean_ref.5) | copy-start | bytes 6916
  47.5 21.1 %copy-start.15 = (f32[24,24]{1,0:T(8,128)S(1)}, f32[24,24]{1,0:T(8,128)}, u32[]{:S(2)}) copy-start(f32[24,24]{1,0:T(8,128)} %scale_ref.5) | copy-start | bytes 6916
  47.5 21.1 %copy-start.18 = (bf16[128,128]{1,0:T(8,128)(2,1)S(1)}, bf16[128,128]{1,0:T(8,128)(2,1)}, u32[]{:S(2)}) copy-start(bf16[128,128]{1,0:T(8,128)(2,1)} %weight_ref.1) | copy-start | bytes 98308
  93.7 2.8 %collective-permute-start.3 = (bf16[2,96,384]{2,1,0:T(8,128)(2,1)S(1)}, bf16[2,96,384]{2,1,0:T(8,128)(2,1)S(1)}, u32[]{:S(2)}, u32[]{:S(2)}) collective-permute-start(bf16[2,96,384]{2,1,0:T(8,128)(2,1)S(1)} %get-tuple-element.19), channel_id=1, source_target_pairs={{0,16},{16,0},{1,17},{17,1},{2,18},{18,2},{3,19},{19,3},{4,20},{20... | collective-permute-start | bytes 442376 | tf_op jit(solution)/shard_map/ppermute | solution.py:252
  93.8 7.1 %collective-permute-start.4 = (bf16[2,96,384]{2,1,0:T(8,128)(2,1)S(1)}, bf16[2,96,384]{2,1,0:T(8,128)(2,1)S(1)}, u32[]{:S(2)}, u32[]{:S(2)}) collective-permute-start(bf16[2,96,384]{2,1,0:T(8,128)(2,1)S(1)} %get-tuple-element.20), channel_id=1, source_target_pairs={{0,128},{128,0},{1,129},{129,1},{2,130},{130,2},{3,131},{131,3},{4... | collective-permute-start | bytes 442376 | tf_op jit(solution)/shard_map/ppermute | solution.py:252
  96.1 7.3 %collective-permute-start.5 = (bf16[2,96,384]{2,1,0:T(8,128)(2,1)S(1)}, bf16[2,96,384]{2,1,0:T(8,128)(2,1)S(1)}, u32[]{:S(2)}, u32[]{:S(2)}) collective-permute-start(bf16[2,96,384]{2,1,0:T(8,128)(2,1)S(1)} %get-tuple-element.21), channel_id=1, source_target_pairs={{0,144},{144,0},{16,128},{128,16},{1,145},{145,1},{17,129},{129,17... | collective-permute-start | bytes 442376 | tf_op jit(solution)/shard_map/ppermute | solution.py:295
  103.9 23.4 %copy-start.4 = (bf16[128,128]{1,0:T(8,128)(2,1)S(1)}, bf16[128,128]{1,0:T(8,128)(2,1)}, u32[]{:S(2)}) copy-start(bf16[128,128]{1,0:T(8,128)(2,1)} %lg.3) | copy-start | bytes 98308
  104.0 23.4 %copy-start.6 = (bf16[128,128]{1,0:T(8,128)(2,1)S(1)}, bf16[128,128]{1,0:T(8,128)(2,1)}, u32[]{:S(2)}) copy-start(bf16[128,128]{1,0:T(8,128)(2,1)} %lv.3) | copy-start | bytes 98308
  104.0 23.3 %copy-start.8 = (bf16[128,128]{1,0:T(8,128)(2,1)S(1)}, bf16[128,128]{1,0:T(8,128)(2,1)}, u32[]{:S(2)}) copy-start(bf16[128,128]{1,0:T(8,128)(2,1)} %rg.3) | copy-start | bytes 98308
  104.0 23.3 %copy-start.10 = (bf16[128,128]{1,0:T(8,128)(2,1)S(1)}, bf16[128,128]{1,0:T(8,128)(2,1)}, u32[]{:S(2)}) copy-start(bf16[128,128]{1,0:T(8,128)(2,1)} %rv.3) | copy-start | bytes 98308
  104.0 23.3 %copy-start.17 = (s32[24,24]{1,0:T(8,128)S(1)}, s32[24,24]{1,0:T(8,128)}, u32[]{:S(2)}) copy-start(s32[24,24]{1,0:T(8,128)} %mask_ref.3) | copy-start | bytes 6916
  (1 other events, 0.7 us)

commit v2 on v1

v2 whole, which is shorter than its diff:
```python
import jax
import jax.numpy as jnp
from jax import lax
from jax.experimental import pallas as pl
from jax.experimental.pallas import tpu as pltpu
from jax.sharding import Mesh, PartitionSpec as P

epsilon = 1e-05
SIDE = 24
BLOCKS = 16
PAIRS = SIDE * SIDE
WIDTH = 128
GROUPS = 8
HALF = GROUPS * SIDE
TOKENS = SIDE * BLOCKS
SPREAD = ("z_lo", "x", "z_hi", "y")
TILES = TOKENS // WIDTH
ALONE, PAIRED = 6, 5
f32 = jnp.float32
bf16 = jnp.bfloat16
VMEM = pl.BlockSpec(memory_space=pltpu.VMEM)
HBM = pl.BlockSpec(memory_space=pltpu.HBM)


def dot(a, b, over=((1,), (0,))):
    return lax.dot_general(a, b, (over, ((), ())), preferred_element_type=f32)


def columns(ref):
    turned = jnp.transpose(ref[...].astype(f32))
    return jnp.concatenate([turned[:, i : i + 1] for i in range(SIDE)], axis=0)


def lanes(rows):
    return lax.broadcasted_iota(jnp.int32, (rows, WIDTH), 1)


def roll(value, by):
    by = by % WIDTH
    return value if by == 0 else pltpu.roll(value, by, 1)


def place(c):
    return (c % 2) * GROUPS + c // 2


def layer_back(grad, normed, scale):
    centre = jnp.mean(grad, axis=-1, keepdims=True)
    along = jnp.mean(grad * normed, axis=-1, keepdims=True)
    return scale * (grad - centre - normed * along)


def to_messages(parts, scratch):
    total = scratch.shape[0] // WIDTH
    lines = total // len(parts)
    for p, part in enumerate(parts):
        for r in range(lines):
            stack = [part[i * SIDE : (i + 1) * SIDE] for i in range(r, SIDE, lines)]
            stack.append(jnp.zeros((WIDTH - len(stack) * SIDE, WIDTH), f32))
            turned = jnp.transpose(jnp.concatenate(stack, axis=0))
            scratch[pl.ds(lines * p + r, WIDTH, stride=total), :] = turned
    return scratch[...].astype(bf16)


def from_messages(in_ref, scratch, count):
    total = in_ref.shape[0] // WIDTH
    lines = total // count
    scratch[...] = in_ref[...].astype(f32)
    parts = []
    for p in range(count):
        rows = [None] * SIDE
        for r in range(lines):
            turned = jnp.transpose(scratch[pl.ds(lines * p + r, WIDTH, stride=total), :])
            for n, i in enumerate(range(r, SIDE, lines)):
                rows[i] = turned[n * SIDE : (n + 1) * SIDE]
        parts.append(jnp.concatenate(rows, axis=0))
    return parts


def assemble(scratch, panels, lines, first, spot):
    total = scratch.shape[0] // WIDTH
    lane = lanes(GROUPS)
    order = {spot(c): c for c in range(BLOCKS)}
    for r in range(lines):
        found = [scratch[pl.ds(c * total + first + r, GROUPS, stride=BLOCKS * total), :] for c in range(BLOCKS)]
        for n, i in enumerate(range(r, SIDE, lines)):
            for t in range(TILES):
                tile = None
                for at in range(BLOCKS):
                    begin, end = at * SIDE - t * WIDTH, (at + 1) * SIDE - t * WIDTH
                    if end <= 0 or begin >= WIDTH:
                        continue
                    piece = roll(found[order[at]], begin - n * SIDE)
                    tile = piece if tile is None else jnp.where(lane >= begin, piece, tile)
                panels[t, pl.ds(i, GROUPS, stride=SIDE), :] = tile


def whole(panels):
    return jnp.concatenate([panels[t] for t in range(TILES)], axis=1)


def fill(panels, value):
    for t in range(TILES):
        panels[t] = value[:, t * WIDTH : (t + 1) * WIDTH]


def disassemble(panels, scratch, lines, first, spot):
    total = scratch.shape[0] // WIDTH
    lane = lanes(GROUPS)
    for c in range(BLOCKS):
        begin = spot(c) * SIDE
        t, after = begin // WIDTH, (begin + SIDE - 1) // WIDTH
        for r in range(lines):
            line = None
            for n, i in enumerate(range(r, SIDE, lines)):
                rows = pl.ds(i, GROUPS, stride=SIDE)
                shift = n * SIDE - begin
                piece = roll(panels[t, rows, :], shift)
                if after != t:
                    border = n * SIDE + after * WIDTH - begin
                    piece = jnp.where(lane < border, piece, roll(panels[after, rows, :], shift))
                line = piece if line is None else jnp.where(lane >= n * SIDE, piece, line)
            scratch[pl.ds(c * total + first + r, GROUPS, stride=BLOCKS * total), :] = line


def normalise(pair_ref, mean_ref, scale_ref):
    scale = columns(scale_ref)
    normed = (pair_ref[...].astype(f32) - columns(mean_ref)) * scale
    return normed, scale


def edges_kernel(*refs):
    given, out_ref, scratch, held, sems = refs[:8], refs[8], refs[9], refs[10:18], refs[18]
    copies = [pltpu.make_async_copy(a, b, sems.at[n]) for n, (a, b) in enumerate(zip(given, held))]
    for copy in copies:
        copy.start()
    for copy in copies:
        copy.wait()
    pair_ref, mean_ref, scale_ref, mask_ref, lg, lv, rg, rv = held
    normed, _ = normalise(pair_ref, mean_ref, scale_ref)
    low = normed.astype(bf16)
    keep = columns(mask_ref)
    left = jax.nn.sigmoid(dot(low, lg[...])) * dot(low, lv[...]) * keep
    right = jax.nn.sigmoid(dot(low, rg[...])) * dot(low, rv[...]) * keep
    out_ref[...] = to_messages([left, right], scratch)


def assemble_kernel(edge, in_ref, out_ref, scratch, panels):
    scratch[...] = in_ref[...].astype(f32)
    assemble(scratch, panels, PAIRED, edge * PAIRED, lambda c: c)
    out_ref[...] = whole(panels).astype(bf16)


def mixed_kernel(left_ref, own_ref, other_ref, right_ref, out_ref, scratch, panels):
    core = lax.axis_index("core")
    right_ref[core] = own_ref[...]
    right_ref[1 - core] = other_ref[...]
    fill(panels, dot(left_ref[...], right_ref[...].reshape(TOKENS, TOKENS), ((1,), (1,))))
    disassemble(panels, scratch, ALONE, 0, place)
    out_ref[...] = scratch[...].astype(bf16)


def middle_kernel(
    in_ref, pair_ref, mean_ref, scale_ref, cot_ref, gate_ref, weight_ref, out_ref, grad_gate_ref, scratch
):
    (mixed,) = from_messages(in_ref, scratch, 1)
    normed, _ = normalise(pair_ref, mean_ref, scale_ref)
    out_sig = jax.nn.sigmoid(dot(normed.astype(bf16), gate_ref[...]))
    upstream = cot_ref[...].astype(f32)
    grad_y = (upstream * out_sig).astype(bf16)
    grad_mixnorm = dot(grad_y, weight_ref[...], ((1,), (1,)))
    centred = mixed - jnp.mean(mixed, axis=-1, keepdims=True)
    mix_scale = lax.rsqrt(jnp.mean(centred * centred, axis=-1, keepdims=True) + epsilon)
    mix_normed = centred * mix_scale
    out_lin = dot(mix_normed.astype(bf16), weight_ref[...])
    grad_gate_ref[...] = (upstream * out_lin * out_sig * (1.0 - out_sig)).astype(bf16)
    grad_mix = layer_back(grad_mixnorm, mix_normed, mix_scale)
    out_ref[...] = to_messages([grad_mix], scratch)


def right_grad_kernel(in_ref, left_ref, grad_ref, own_ref, sent_ref, scratch, panels, sums):
    scratch[...] = in_ref[...].astype(f32)
    assemble(scratch, panels, ALONE, 0, place)
    grad = whole(panels)
    grad_ref[...] = grad.astype(bf16)
    sums[...] = dot(jnp.transpose(grad).astype(bf16), left_ref[...]).reshape(2, HALF, TOKENS)
    core = lax.axis_index("core")
    own_ref[...] = sums[core]
    sent_ref[...] = sums[1 - core].astype(bf16)


def left_grad_kernel(grad_ref, right_ref, out_ref):
    out_ref[...] = dot(grad_ref[...], right_ref[...].reshape(TOKENS, TOKENS))


def return_kernel(left_ref, own_ref, other_ref, out_ref, scratch, panels):
    fill(panels, left_ref[...])
    disassemble(panels, scratch, PAIRED, 0, lambda c: c)
    fill(panels, own_ref[...] + other_ref[...].astype(f32))
    disassemble(panels, scratch, PAIRED, PAIRED, lambda c: c)
    out_ref[...] = scratch[...].astype(bf16)


def last_kernel(
    in_ref, pair_ref, mean_ref, scale_ref, mask_ref, grad_gate_ref, lg, lv, rg, rv, og, out_ref, scratch
):
    grad_left, grad_right = from_messages(in_ref, scratch, 2)
    normed, scale = normalise(pair_ref, mean_ref, scale_ref)
    low = normed.astype(bf16)
    keep = columns(mask_ref)
    over = ((1,), (1,))
    grad_normed = dot(grad_gate_ref[...], og[...], over)
    for grad, gate, value in ((grad_left, lg, lv), (grad_right, rg, rv)):
        sig = jax.nn.sigmoid(dot(low, gate[...]))
        lin = dot(low, value[...])
        kept = grad * keep
        grad_normed += dot((kept * lin * sig * (1.0 - sig)).astype(bf16), gate[...], over)
        grad_normed += dot((kept * sig).astype(bf16), value[...], over)
    out_ref[...] = layer_back(grad_normed, normed, scale)


def call(kernel, outs, *args, scratch=(), name=None, space=VMEM, limit=48):
    return pl.pallas_call(
        kernel,
        out_shape=[jax.ShapeDtypeStruct(shape, dtype) for shape, dtype in outs],
        in_specs=[space for _ in args],
        out_specs=[VMEM for _ in outs],
        scratch_shapes=list(scratch),
        compiler_params=pltpu.CompilerParams(vmem_limit_bytes=limit * 1024 * 1024),
        name=name,
    )(*args)


def spread(messages):
    paired = messages.reshape(WIDTH, -1, 2, WIDTH)
    return lax.all_to_all(paired, SPREAD, 0, 0, tiled=True).reshape(messages.shape)


def swap(value):
    return lax.ppermute(value, "core", [(0, 1), (1, 0)])


def per_device(
    pair_input,
    norm_mean,
    norm_scale,
    pair_mask,
    cotangent,
    left_gate,
    left_value,
    right_gate,
    right_value,
    output_gate,
    output_weight,
):
    pair = pair_input.reshape(PAIRS, WIDTH)
    cot = cotangent.reshape(PAIRS, WIDTH)
    one, two = (WIDTH * ALONE, WIDTH), (WIDTH * 2 * PAIRED, WIDTH)
    line_one, line_two = pltpu.VMEM(one, f32), pltpu.VMEM(two, f32)
    panels = pltpu.VMEM((TILES, HALF, WIDTH), f32)
    one, two = (one, bf16), (two, bf16)
    panel, wide = ((HALF, TOKENS), bf16), ((HALF, TOKENS), f32)
    given = [pair, norm_mean, norm_scale, pair_mask, left_gate, left_value, right_gate, right_value]
    held = [pltpu.VMEM(a.shape, a.dtype) for a in given]
    (sent,) = call(
        edges_kernel, [two], *given, scratch=[line_two] + held + [pltpu.SemaphoreType.DMA((len(given),))],
        name="edges", space=HBM, limit=60,
    )
    came = spread(sent)
    (right_own,) = call(lambda *r: assemble_kernel(1, *r), [panel], came, scratch=[line_two, panels], name="take_right")
    right_other = swap(right_own)
    (left,) = call(lambda *r: assemble_kernel(0, *r), [panel], came, scratch=[line_two, panels], name="take_left")
    right, sent = call(
        mixed_kernel, [((2, HALF, TOKENS), bf16), one], left, right_own, right_other, scratch=[line_one, panels],
        name="mix",
    )
    came = spread(sent)
    sent, grad_gate = call(
        middle_kernel, [one, ((PAIRS, WIDTH), bf16)], came, pair, norm_mean, norm_scale, cot, output_gate,
        output_weight, scratch=[line_one], name="middle",
    )
    came = spread(sent)
    grad, own, sent = call(
        right_grad_kernel, [panel, wide, panel], came, left,
        scratch=[line_one, panels, pltpu.VMEM((2, HALF, TOKENS), f32)],
        name="right_grad",
    )
    other = swap(sent)
    (grad_left,) = call(left_grad_kernel, [wide], grad, right, name="left_grad")
    (sent,) = call(return_kernel, [two], grad_left, own, other, scratch=[line_two, panels], name="return")
    came = spread(sent)
    (out,) = call(
        last_kernel, [((PAIRS, WIDTH), f32)], came, pair, norm_mean, norm_scale, pair_mask, grad_gate, left_gate,
        left_value, right_gate, right_value, output_gate, scratch=[line_two], name="last",
    )
    return out.reshape(SIDE, SIDE, WIDTH)


def solution(mesh):
    fine = Mesh(mesh.devices.reshape(2, 4, 2, 4, 4), ("z_lo", "x", "core", "z_hi", "y"))
    row, col = ("z_lo", "x", "core"), ("z_hi", "y")
    placed = (P(row, col, None), P(row, col), P(row, col), P(row, col), P(row, col, None)) + (P(),) * 6
    return jax.shard_map(per_device, mesh=fine, in_specs=placed, out_specs=P(row, col, None), check_vma=False)
```

time: 131 us -> 103 us (0.79)
  waiting for transfers between devices: 12.2 us -> 1.95 us
  blocking collectives: 98.2 us -> 89.3 us
  local copies, waits for them, and re-layouts: 6.13 us -> 0.07 us
  starting transfers between devices: 3.6 us -> 0.37 us
    ppermute x6 -> x2, waiting for transfers between devices: 12.2 us -> 1.95 us  [swap(): return lax.ppermute(value, 'core', [(0, 1), (1, 0)])]
    all_to_all x4, blocking collectives: 98.2 us -> 89.3 us  [spread(): lax.all_to_all(paired, SPREAD, 0, 0, tiled=True).reshape(messages.shape)]
    unnamed x38 -> x22, local copies, waits for them, and re-layouts: 6.13 us -> 0.07 us
    ppermute x6 -> x2, starting transfers between devices: 3.6 us -> 0.37 us  [swap(): return lax.ppermute(value, 'core', [(0, 1), (1, 0)])]
  transfers between devices with their start and end apart: 6 -> 2, of which waited for: 4 -> 2; matrix products, arithmetic and copies ran while one was open for 0% -> 0% of each run, Pallas kernels for 0% -> 1%
where the time goes in v2:
time: 103 us; the launch traced here: 102 us
  blocking collectives  89.3 us (87%)
  Pallas kernels  10.1 us (10%)
  waiting for transfers between devices  1.95 us (2%)
    all_to_all x4, blocking collectives, spread(): lax.all_to_all(paired, SPREAD, 0, 0, tiled=True).reshape(messages.shape)  89.3 us
    pallas_call x9, Pallas kernels, call(): pl.pallas_call(kernel, out_shape=[jax.ShapeDtypeStruct(shape, dtype) for...  10.1 us
  transfers between devices with their start and end apart: 2, of which 2 were waited for; matrix products, arithmetic and copies ran while one was open for 0% of the time, Pallas kernels for 1%

profile of v2, /device:TPU:32, one launch (start us, length us, event | category | flops | bytes accessed | tf_op | source)
XLA Modules:
  0.0 101.9 jit_solution(10865169497842522377)
XLA Ops:
  0.0 2.6 %edges.1 = bf16[1280,128]{1,0:T(8,128)(2,1)} custom-call(bf16[576,128]{1,0:T(8,128)(2,1)} %bitcast.13, f32[24,24]{1,0:T(8,128)} %mean_ref.3, f32[24,24]{1,0:T(8,128)} %scale_ref.3, s32[24,24]{1,0:T(8,128)} %mask_ref.1, bf16[128,128]{1,0:T(8,128)(2,1)} %lg.1, bf16[128,128]{1,0:T(8,128)(2,1)} %lv.1, bf16[128,128]{1,0:T(8,128)(2,1)} %rg.1, bf16[128,128]{1,0:T(8,128)(2,1)} %rv.1), custom_call_target="tpu_custom_call" | custom-call | tf_op jit(solution)/shard_map/edges/pallas_call | solution.py:223
  2.6 29.1 %all_to_all.20 = bf16[128,5,2,128]{3,2,1,0:T(2,128)(2,1)S(1)} all-to-all(bf16[128,5,2,128]{3,2,1,0:T(2,128)(2,1)} %bitcast.23), channel_id=1, replica_groups=mesh['z_lo'=2,'x'=4,'core'=2,'z_hi'=4,'y'=4] {'z_lo','x','z_hi','y'}, dimensions={0} | all-to-all | bytes 655360 | tf_op jit(solution)/shard_map/all_to_all | solution.py:236
  31.7 0.5 take_right.1.own_ref
  32.2 0.1 collective-permute-start
  32.3 0.5 take_left.1.left_ref
  32.9 0.8 collective-permute-done.other_ref
  33.7 0.9 mix.1
  34.6 0.0 copy-start
  34.6 0.0 copy-start.1
  34.6 0.0 copy-start.6
  34.7 0.0 copy-start.10
  34.7 20.5 %all_to_all.21 = bf16[128,3,2,128]{3,2,1,0:T(2,128)(2,1)S(1)} all-to-all(bf16[128,3,2,128]{3,2,1,0:T(2,128)(2,1)S(1)} %bitcast.20), channel_id=1, replica_groups=mesh['z_lo'=2,'x'=4,'core'=2,'z_hi'=4,'y'=4] {'z_lo','x','z_hi','y'}, dimensions={0} | all-to-all | bytes 393216 | tf_op jit(solution)/shard_map/all_to_all | solution.py:236
  55.3 1.1 %middle.1 = (bf16[768,128]{1,0:T(8,128)(2,1)S(1)}, bf16[576,128]{1,0:T(8,128)(2,1)S(1)}) custom-call(bf16[768,128]{1,0:T(8,128)(2,1)S(1)} %bitcast.19, bf16[576,128]{1,0:T(8,128)(2,1)S(1)} %bitcast.14, f32[24,24]{1,0:T(8,128)S(1)} %copy-done.7, f32[24,24]{1,0:T(8,128)S(1)} %copy-done.8, bf16[576,128]{1,0:T(8,128)(2,1)S(1)} %bitcast.22, ...), custom_call_target="tpu_custom_call" | custom-call | tf_op jit(solution)/shard_map/middle/pallas_call | solution.py:223
  56.3 18.5 %all_to_all.22 = bf16[128,3,2,128]{3,2,1,0:T(2,128)(2,1)S(1)} all-to-all(bf16[128,3,2,128]{3,2,1,0:T(2,128)(2,1)S(1)} %bitcast.21), channel_id=1, replica_groups=mesh['z_lo'=2,'x'=4,'core'=2,'z_hi'=4,'y'=4] {'z_lo','x','z_hi','y'}, dimensions={0} | all-to-all | bytes 393216 | tf_op jit(solution)/shard_map/all_to_all | solution.py:236
  74.9 0.9 right_grad.1
  75.8 0.3 collective-permute-start.1
  76.1 0.2 left_grad.1.left_ref
  76.3 1.1 %collective-permute-done.1.other_ref = bf16[192,384]{1,0:T(8,128)(2,1)S(1)} collective-permute-done((bf16[192,384]{1,0:T(8,128)(2,1)S(1)}, bf16[192,384]{1,0:T(8,128)(2,1)S(1)}, u32[]{:S(2)}, u32[]{:S(2)}) %collective-permute-start.1) | collective-permute-done | bytes 147488 | tf_op jit(solution)/shard_map/ppermute | solution.py:240
  77.5 1.0 return.1
  78.5 0.0 copy-start.2
  78.5 0.0 copy-start.3
  78.5 0.0 copy-start.9
  78.5 21.1 %all_to_all.23 = bf16[128,5,2,128]{3,2,1,0:T(2,128)(2,1)S(1)} all-to-all(bf16[128,5,2,128]{3,2,1,0:T(2,128)(2,1)S(1)} %bitcast.16), channel_id=1, replica_groups=mesh['z_lo'=2,'x'=4,'core'=2,'z_hi'=4,'y'=4] {'z_lo','x','z_hi','y'}, dimensions={0} | all-to-all | bytes 655360 | tf_op jit(solution)/shard_map/all_to_all | solution.py:236
  99.6 2.3 %last.1 = f32[576,128]{1,0:T(8,128)} custom-call(bf16[1280,128]{1,0:T(8,128)(2,1)S(1)} %bitcast.17, bf16[576,128]{1,0:T(8,128)(2,1)S(1)} %bitcast.15, f32[24,24]{1,0:T(8,128)S(1)} %copy-done.7, f32[24,24]{1,0:T(8,128)S(1)} %copy-done.8, s32[24,24]{1,0:T(8,128)S(1)} %copy-done.9, bf16[576,128]{1,0:T(8,128)(2,1)S(1)} %get-tuple-element.18.grad_gate_ref, ...), custom_call_target="tpu_custom_call" | custom-call | tf_op jit(solution)/shard_map/last/pallas_call | solution.py:223
  (15 shorter events, 0.0 us)
Async XLA Ops:
  32.2 1.5 %collective-permute-start = (bf16[192,384]{1,0:T(8,128)(2,1)S(1)}, bf16[192,384]{1,0:T(8,128)(2,1)S(1)}, u32[]{:S(2)}, u32[]{:S(2)}) collective-permute-start(bf16[192,384]{1,0:T(8,128)(2,1)S(1)} %take_right.1.own_ref), channel_id=1, source_target_pairs={{0,16},{16,0},{1,17},{17,1},{2,18},{18,2},{3,19},{19,3},{4,20},{20... | collective-permute-start | bytes 442376 | tf_op jit(solution)/shard_map/ppermute | solution.py:240
  34.6 20.6 %copy-start = (bf16[24,24,128]{2,1,0:T(8,128)(2,1)S(1)}, bf16[24,24,128]{2,1,0:T(8,128)(2,1)}, u32[]{:S(2)}) copy-start(bf16[24,24,128]{2,1,0:T(8,128)(2,1)} %param.11) | copy-start | bytes 442372
  34.6 20.6 %copy-start.1 = (bf16[24,24,128]{2,1,0:T(8,128)(2,1)S(1)}, bf16[24,24,128]{2,1,0:T(8,128)(2,1)}, u32[]{:S(2)}) copy-start(bf16[24,24,128]{2,1,0:T(8,128)(2,1)} %param.15) | copy-start | bytes 442372
  34.6 20.6 %copy-start.6 = (bf16[128,128]{1,0:T(8,128)(2,1)S(1)}, bf16[128,128]{1,0:T(8,128)(2,1)}, u32[]{:S(2)}) copy-start(bf16[128,128]{1,0:T(8,128)(2,1)} %og.1) | copy-start | bytes 98308
  34.6 20.6 %copy-start.7 = (f32[24,24]{1,0:T(8,128)S(1)}, f32[24,24]{1,0:T(8,128)}, u32[]{:S(2)}) copy-start(f32[24,24]{1,0:T(8,128)} %mean_ref.3) | copy-start | bytes 6916
  34.6 20.6 %copy-start.8 = (f32[24,24]{1,0:T(8,128)S(1)}, f32[24,24]{1,0:T(8,128)}, u32[]{:S(2)}) copy-start(f32[24,24]{1,0:T(8,128)} %scale_ref.3) | copy-start | bytes 6916
  34.7 20.6 %copy-start.10 = (bf16[128,128]{1,0:T(8,128)(2,1)S(1)}, bf16[128,128]{1,0:T(8,128)(2,1)}, u32[]{:S(2)}) copy-start(bf16[128,128]{1,0:T(8,128)(2,1)} %weight_ref.1) | copy-start | bytes 98308
  75.8 1.6 %collective-permute-start.1 = (bf16[192,384]{1,0:T(8,128)(2,1)S(1)}, bf16[192,384]{1,0:T(8,128)(2,1)S(1)}, u32[]{:S(2)}, u32[]{:S(2)}) collective-permute-start(bf16[192,384]{1,0:T(8,128)(2,1)S(1)} %get-tuple-element.17), channel_id=1, source_target_pairs={{0,16},{16,0},{1,17},{17,1},{2,18},{18,2},{3,19},{19,3},{4,20},{20... | collective-permute-start | bytes 442376 | tf_op jit(solution)/shard_map/ppermute | solution.py:240
  78.5 21.2 %copy-start.2 = (bf16[128,128]{1,0:T(8,128)(2,1)S(1)}, bf16[128,128]{1,0:T(8,128)(2,1)}, u32[]{:S(2)}) copy-start(bf16[128,128]{1,0:T(8,128)(2,1)} %lg.1) | copy-start | bytes 98308
  78.5 21.1 %copy-start.3 = (bf16[128,128]{1,0:T(8,128)(2,1)S(1)}, bf16[128,128]{1,0:T(8,128)(2,1)}, u32[]{:S(2)}) copy-start(bf16[128,128]{1,0:T(8,128)(2,1)} %lv.1) | copy-start | bytes 98308
  78.5 21.1 %copy-start.4 = (bf16[128,128]{1,0:T(8,128)(2,1)S(1)}, bf16[128,128]{1,0:T(8,128)(2,1)}, u32[]{:S(2)}) copy-start(bf16[128,128]{1,0:T(8,128)(2,1)} %rg.1) | copy-start | bytes 98308
  78.5 21.1 %copy-start.5 = (bf16[128,128]{1,0:T(8,128)(2,1)S(1)}, bf16[128,128]{1,0:T(8,128)(2,1)}, u32[]{:S(2)}) copy-start(bf16[128,128]{1,0:T(8,128)(2,1)} %rv.1) | copy-start | bytes 98308
  78.5 21.1 %copy-start.9 = (s32[24,24]{1,0:T(8,128)S(1)}, s32[24,24]{1,0:T(8,128)}, u32[]{:S(2)}) copy-start(s32[24,24]{1,0:T(8,128)} %mask_ref.1) | copy-start | bytes 6916

commit v3 on v2

v3 whole, which is shorter than its diff:
```python
import jax
import jax.numpy as jnp
from jax import lax
from jax.experimental import pallas as pl
from jax.experimental.pallas import tpu as pltpu
from jax.sharding import Mesh, PartitionSpec as P

epsilon = 1e-05
SIDE = 24
BLOCKS = 16
PAIRS = SIDE * SIDE
WIDTH = 128
GROUPS = 8
HALF = GROUPS * SIDE
TOKENS = SIDE * BLOCKS
SPREAD = ("z_hi", "y", "z_lo", "x")
TILES = TOKENS // WIDTH
ALONE, PAIRED = 6, 5
f32 = jnp.float32
bf16 = jnp.bfloat16
VMEM = pl.BlockSpec(memory_space=pltpu.VMEM)
HBM = pl.BlockSpec(memory_space=pltpu.HBM)


def dot(a, b, over=((1,), (0,))):
    return lax.dot_general(a, b, (over, ((), ())), preferred_element_type=f32)


def spread_pairs(ref):
    turned = jnp.transpose(ref[...].astype(f32))
    return jnp.concatenate([jnp.broadcast_to(turned[:, i : i + 1], (SIDE, WIDTH)) for i in range(SIDE)], axis=0)


def lanes(rows):
    return lax.broadcasted_iota(jnp.int32, (rows, WIDTH), 1)


def roll(value, by):
    by = by % WIDTH
    return value if by == 0 else pltpu.roll(value, by, 1)


def place(c):
    return (c % 2) * GROUPS + c // 2


def layer_back(grad, normed, scale):
    centre = jnp.mean(grad, axis=-1, keepdims=True)
    along = jnp.mean(grad * normed, axis=-1, keepdims=True)
    return scale * (grad - centre - normed * along)


def to_messages(parts, scratch):
    total = scratch.shape[0] // WIDTH
    lines = total // len(parts)
    for p, part in enumerate(parts):
        for r in range(lines):
            stack = [part[i * SIDE : (i + 1) * SIDE] for i in range(r, SIDE, lines)]
            stack.append(jnp.zeros((WIDTH - len(stack) * SIDE, WIDTH), f32))
            turned = jnp.transpose(jnp.concatenate(stack, axis=0))
            scratch[pl.ds(lines * p + r, WIDTH, stride=total), :] = turned
    return scratch[...].astype(bf16)


def from_messages(in_ref, scratch, count):
    total = in_ref.shape[0] // WIDTH
    lines = total // count
    scratch[...] = in_ref[...].astype(f32)
    parts = []
    for p in range(count):
        rows = [None] * SIDE
        for r in range(lines):
            turned = jnp.transpose(scratch[pl.ds(lines * p + r, WIDTH, stride=total), :])
            for n, i in enumerate(range(r, SIDE, lines)):
                rows[i] = turned[n * SIDE : (n + 1) * SIDE]
        parts.append(jnp.concatenate(rows, axis=0))
    return parts


def assemble(scratch, lines, first, spot, store):
    total = scratch.shape[0] // WIDTH
    lane = lanes(GROUPS)
    order = {spot(c): c for c in range(BLOCKS)}
    for r in range(lines):
        found = [scratch[pl.ds(c * GROUPS * total + first + r, GROUPS, stride=total), :] for c in range(BLOCKS)]
        for n, i in enumerate(range(r, SIDE, lines)):
            for t in range(TILES):
                tile = None
                for at in range(BLOCKS):
                    begin, end = at * SIDE - t * WIDTH, (at + 1) * SIDE - t * WIDTH
                    if end <= 0 or begin >= WIDTH:
                        continue
                    piece = roll(found[order[at]], begin - n * SIDE)
                    tile = piece if tile is None else jnp.where(lane >= begin, piece, tile)
                store(i, t, tile)


def disassemble(load, scratch, lines, first, blocks):
    total = scratch.shape[0] // (GROUPS * blocks)
    lane = lanes(GROUPS)
    for c in range(blocks):
        begin = c * SIDE
        t, after = begin // WIDTH, (begin + SIDE - 1) // WIDTH
        for r in range(lines):
            line = None
            for n, i in enumerate(range(r, SIDE, lines)):
                shift = n * SIDE - begin
                piece = roll(load(i, t), shift)
                if after != t:
                    border = n * SIDE + after * WIDTH - begin
                    piece = jnp.where(lane < border, piece, roll(load(i, after), shift))
                line = piece if line is None else jnp.where(lane >= n * SIDE, piece, line)
            scratch[pl.ds(c * GROUPS * total + first + r, GROUPS, stride=total), :] = line


def columns_of(t):
    return slice(t * WIDTH, (t + 1) * WIDTH)


def normalise(pair_ref, mean_ref, scale_ref):
    scale = spread_pairs(scale_ref)
    normed = (pair_ref[...].astype(f32) - spread_pairs(mean_ref)) * scale
    return normed, scale


def edges_kernel(*refs):
    given, out_ref, scratch, held, sems = refs[:8], refs[8], refs[9], refs[10:18], refs[18]
    copies = [pltpu.make_async_copy(a, b, sems.at[n]) for n, (a, b) in enumerate(zip(given, held))]
    for copy in copies:
        copy.start()
    for copy in copies:
        copy.wait()
    pair_ref, mean_ref, scale_ref, mask_ref, lg, lv, rg, rv = held
    normed, _ = normalise(pair_ref, mean_ref, scale_ref)
    low = normed.astype(bf16)
    keep = spread_pairs(mask_ref)
    parts = []
    for gate, value in ((lg, lv), (rg, rv)):
        both = dot(low, jnp.concatenate([gate[...], value[...]], axis=1))
        parts.append(jax.nn.sigmoid(both[:, :WIDTH]) * both[:, WIDTH:] * keep)
    out_ref[...] = to_messages(parts, scratch)


def take_right_kernel(in_ref, out_ref, scratch, panels):
    scratch[...] = in_ref[...].astype(f32)

    def store(i, t, tile):
        panels[t, pl.ds(i * (GROUPS + 1), GROUPS), :] = tile

    assemble(scratch, PAIRED, PAIRED, lambda c: c, store)
    for group in range(GROUPS):
        rows = [panels[t, pl.ds(group, SIDE, stride=GROUPS + 1), :] for t in range(TILES)]
        out_ref[group * SIDE : (group + 1) * SIDE, :] = jnp.concatenate(rows, axis=1).astype(bf16)


def assemble_left(in_ref, scratch, panel, lines, spot):
    scratch[...] = in_ref[...].astype(f32)

    def store(i, t, tile):
        panel[i * GROUPS : (i + 1) * GROUPS, columns_of(t)] = tile

    assemble(scratch, lines, 0, spot, store)


def rows_of(panel):
    return lambda i, t: panel[i * GROUPS : (i + 1) * GROUPS, columns_of(t)]


def take_left_kernel(in_ref, out_ref, scratch, panel):
    assemble_left(in_ref, scratch, panel, PAIRED, lambda c: c)
    out_ref[...] = panel[...].astype(bf16)


def half_mixed(left_ref, right_ref, scratch, panel):
    panel[:, :HALF] = dot(left_ref[...], right_ref[...], ((1,), (1,)))
    disassemble(rows_of(panel), scratch, ALONE, 0, BLOCKS // 2)


def mix_own_kernel(left_ref, right_ref, out_ref, panel):
    half_mixed(left_ref, right_ref, out_ref, panel)


def mix_kernel(left_ref, right_ref, own_ref, out_ref, scratch, panel):
    half_mixed(left_ref, right_ref, scratch, panel)
    first = lax.axis_index("core") == 0
    size = GROUPS * ALONE
    for n in range(BLOCKS // 2):
        here = slice(n * size, (n + 1) * size)
        own, other = own_ref[here, :], scratch[here, :]
        out_ref[2 * n * size : (2 * n + 1) * size, :] = jnp.where(first, own, other).astype(bf16)
        out_ref[(2 * n + 1) * size : (2 * n + 2) * size, :] = jnp.where(first, other, own).astype(bf16)


def ready_kernel(pair_ref, mean_ref, scale_ref, cot_ref, gate_ref, weight_ref, grad_ref, factor_ref):
    normed, _ = normalise(pair_ref, mean_ref, scale_ref)
    out_sig = jax.nn.sigmoid(dot(normed.astype(bf16), gate_ref[...]))
    grad_y = cot_ref[...].astype(f32) * out_sig
    grad_ref[...] = dot(grad_y.astype(bf16), weight_ref[...], ((1,), (1,)))
    factor_ref[...] = grad_y * (1.0 - out_sig)


def middle_kernel(in_ref, grad_ref, factor_ref, weight_ref, out_ref, grad_gate_ref, scratch):
    (mixed,) = from_messages(in_ref, scratch, 1)
    centred = mixed - jnp.mean(mixed, axis=-1, keepdims=True)
    mix_scale = lax.rsqrt(jnp.mean(centred * centred, axis=-1, keepdims=True) + epsilon)
    mix_normed = centred * mix_scale
    out_lin = dot(mix_normed.astype(bf16), weight_ref[...])
    grad_gate_ref[...] = (factor_ref[...] * out_lin).astype(bf16)
    grad_mix = layer_back(grad_ref[...], mix_normed, mix_scale)
    out_ref[...] = to_messages([grad_mix], scratch)


def right_grad_kernel(in_ref, left_ref, grad_ref, own_ref, sent_ref, scratch, panel, sums):
    assemble_left(in_ref, scratch, panel, ALONE, place)
    grad = panel[...]
    grad_ref[...] = grad.astype(bf16)
    sums[...] = dot(jnp.transpose(grad).astype(bf16), left_ref[...]).reshape(2, HALF, TOKENS)
    core = lax.axis_index("core")
    own_ref[...] = sums[core]
    sent_ref[...] = sums[1 - core].astype(bf16)


def left_grad_kernel(grad_ref, own_ref, other_ref, out_ref, right, panel):
    core = lax.axis_index("core")
    right[core] = own_ref[...]
    right[1 - core] = other_ref[...]
    panel[...] = dot(grad_ref[...], right[...].reshape(TOKENS, TOKENS))
    disassemble(rows_of(panel), out_ref, PAIRED, 0, BLOCKS)


def return_kernel(lines_ref, own_ref, other_ref, kept_ref, out_ref, panels):
    for group in range(GROUPS):
        here = slice(group * SIDE, (group + 1) * SIDE)
        total = own_ref[here, :] + other_ref[here, :].astype(f32)
        for t in range(TILES):
            panels[t, pl.ds(group * (SIDE + 1), SIDE), :] = total[:, columns_of(t)]
    load = lambda i, t: panels[t, pl.ds(i, GROUPS, stride=SIDE + 1), :]
    disassemble(load, kept_ref, PAIRED, PAIRED, BLOCKS)
    out_ref[...] = kept_ref[...].astype(bf16)


def prepare_kernel(
    pair_ref, mean_ref, scale_ref, mask_ref, grad_gate_ref, lg, lv, rg, rv, og, normed_ref, scaled_ref, base_ref, factors_ref
):
    normed, scale = normalise(pair_ref, mean_ref, scale_ref)
    normed_ref[...] = normed
    scaled_ref[...] = scale
    base_ref[...] = dot(grad_gate_ref[...], og[...], ((1,), (1,)))
    low = normed.astype(bf16)
    keep = spread_pairs(mask_ref)
    for n, (gate, value) in enumerate(((lg, lv), (rg, rv))):
        both = dot(low, jnp.concatenate([gate[...], value[...]], axis=1))
        sig, lin = jax.nn.sigmoid(both[:, :WIDTH]), both[:, WIDTH:]
        factors_ref[2 * n + 1] = keep * sig
        factors_ref[2 * n] = keep * lin * sig * (1.0 - sig)


def last_kernel(in_ref, normed_ref, scale_ref, base_ref, factors_ref, lg, lv, rg, rv, out_ref, scratch):
    grads = from_messages(in_ref, scratch, 2)
    grad_normed = base_ref[...]
    for n, (gate, value) in enumerate(((lg, lv), (rg, rv))):
        pre_grads = jnp.concatenate([grads[n] * factors_ref[2 * n], grads[n] * factors_ref[2 * n + 1]], axis=1)
        weights = jnp.concatenate([gate[...], value[...]], axis=1)
        grad_normed += dot(pre_grads.astype(bf16), weights, ((1,), (1,)))
    out_ref[...] = layer_back(grad_normed, normed_ref[...], scale_ref[...])


def call(kernel, outs, *args, scratch=(), name=None, space=VMEM, aliases={}):
    return pl.pallas_call(
        kernel,
        out_shape=[jax.ShapeDtypeStruct(shape, dtype) for shape, dtype in outs],
        in_specs=[space for _ in args],
        out_specs=[VMEM for _ in outs],
        scratch_shapes=list(scratch),
        input_output_aliases=aliases,
        compiler_params=pltpu.CompilerParams(vmem_limit_bytes=48 * 1024 * 1024),
        name=name,
    )(*args)


def spread(messages):
    paired = messages.reshape(WIDTH, -1, 2, WIDTH)
    return lax.all_to_all(paired, SPREAD, 0, 0, tiled=True).reshape(messages.shape)


def swap(value):
    return lax.ppermute(value, "core", [(0, 1), (1, 0)])


def per_device(
    pair_input,
    norm_mean,
    norm_scale,
    pair_mask,
    cotangent,
    left_gate,
    left_value,
    right_gate,
    right_value,
    output_gate,
    output_weight,
):
    pair = pair_input.reshape(PAIRS, WIDTH)
    cot = cotangent.reshape(PAIRS, WIDTH)
    one, two = (WIDTH * ALONE, WIDTH), (WIDTH * 2 * PAIRED, WIDTH)
    line_one, line_two = pltpu.VMEM(one, f32), pltpu.VMEM(two, f32)
    panel_left = pltpu.VMEM((HALF, TOKENS), f32)
    panels_in = pltpu.VMEM((TILES, SIDE * (GROUPS + 1), WIDTH), f32)
    panels_out = pltpu.VMEM((TILES, GROUPS * (SIDE + 1), WIDTH), f32)
    one, two = (one, bf16), (two, bf16)
    panel, wide = ((HALF, TOKENS), bf16), ((HALF, TOKENS), f32)
    given = [
        pltpu.with_memory_space_constraint(a, pltpu.HBM)
        for a in (pair, norm_mean, norm_scale, pair_mask, left_gate, left_value, right_gate, right_value)
    ]
    held = [pltpu.VMEM(a.shape, a.dtype) for a in given]
    (sent,) = call(
        edges_kernel, [two], *given, scratch=[line_two] + held + [pltpu.SemaphoreType.DMA((len(given),))],
        name="edges", space=HBM,
    )
    came = spread(sent)
    (right_own,) = call(take_right_kernel, [panel], came, scratch=[line_two, panels_in], name="take_right")
    right_other = swap(right_own)
    (left,) = call(take_left_kernel, [panel], came, scratch=[line_two, panel_left], name="take_left")
    line_half, panel_half = pltpu.VMEM((WIDTH * ALONE // 2, WIDTH), f32), pltpu.VMEM((HALF, 2 * WIDTH), f32)
    (mixed_own,) = call(
        mix_own_kernel, [((WIDTH * ALONE // 2, WIDTH), f32)], left, right_own, scratch=[panel_half], name="mix_own",
    )
    grad_mixnorm, factor = call(
        ready_kernel, [((PAIRS, WIDTH), f32)] * 2, pair, norm_mean, norm_scale, cot, output_gate, output_weight,
        name="ready",
    )
    mixed_own, grad_mixnorm, factor = lax.optimization_barrier((mixed_own, grad_mixnorm, factor))
    (sent,) = call(mix_kernel, [one], left, right_other, mixed_own, scratch=[line_half, panel_half], name="mix")
    came = spread(sent)
    sent, grad_gate = call(
        middle_kernel, [one, ((PAIRS, WIDTH), bf16)], came, grad_mixnorm, factor, output_weight, scratch=[line_one],
        name="middle",
    )
    came = spread(sent)
    grad, own, sent = call(
        right_grad_kernel, [panel, wide, panel], came, left,
        scratch=[line_one, panel_left, pltpu.VMEM((2, HALF, TOKENS), f32)],
        name="right_grad",
    )
    other = swap(sent)
    lined = ((WIDTH * 2 * PAIRED, WIDTH), f32)
    (lines,) = call(
        left_grad_kernel, [lined], grad, right_own, right_other,
        scratch=[pltpu.VMEM((2, HALF, TOKENS), bf16), panel_left], name="left_grad",
    )
    many = ((PAIRS, WIDTH), f32)
    prepared = call(
        prepare_kernel, [many, many, many, ((4, PAIRS, WIDTH), f32)], pair, norm_mean, norm_scale, pair_mask, grad_gate,
        left_gate, left_value, right_gate, right_value, output_gate, name="prepare",
    )
    lines, prepared = lax.optimization_barrier((lines, prepared))
    _, sent = call(return_kernel, [lined, two], lines, own, other, scratch=[panels_out], name="return", aliases={0: 0})
    came = spread(sent)
    (out,) = call(
        last_kernel, [many], came, *prepared, left_gate, left_value, right_gate, right_value, scratch=[line_two],
        name="last",
    )
    return out.reshape(SIDE, SIDE, WIDTH)


def solution(mesh):
    fine = Mesh(mesh.devices.reshape(2, 4, 2, 4, 4), ("z_lo", "x", "core", "z_hi", "y"))
    row, col = ("z_lo", "x", "core"), ("z_hi", "y")
    placed = (P(row, col, None), P(row, col), P(row, col), P(row, col), P(row, col, None)) + (P(),) * 6
    return jax.shard_map(per_device, mesh=fine, in_specs=placed, out_specs=P(row, col, None), check_vma=False)
```

time: 103 us -> 101 us (0.981)
  blocking collectives: 89.3 us -> 91.4 us
  waiting for transfers between devices: 1.95 us -> 0.01 us
  Pallas kernels: 10.1 us -> 8.54 us
    all_to_all x4, blocking collectives: 89.3 us -> 91.4 us  [spread(): lax.all_to_all(paired, SPREAD, 0, 0, tiled=True).reshape(messages.shape)]
    ppermute x2, waiting for transfers between devices: 1.95 us -> 0.01 us  [swap(): return lax.ppermute(value, 'core', [(0, 1), (1, 0)])]
    pallas_call x9 -> x12, Pallas kernels: 10.1 us -> 8.54 us  [call(): pl.pallas_call(kernel, out_shape=[jax.ShapeDtypeStruct(shape, dtype) for...]
  transfers between devices with their start and end apart: 2 -> 2, of which waited for: 2 -> 0; matrix products, arithmetic and copies ran while one was open for 0% -> 0% of each run, Pallas kernels for 1% -> 3%
where the time goes in v3:
time: 101 us; the launch traced here: 100 us
  blocking collectives  91.4 us (90%)
  Pallas kernels  8.54 us (8%)
    all_to_all x4, blocking collectives, spread(): lax.all_to_all(paired, SPREAD, 0, 0, tiled=True).reshape(messages.shape)  91.4 us
    pallas_call x12, Pallas kernels, call(): pl.pallas_call(kernel, out_shape=[jax.ShapeDtypeStruct(shape, dtype) for...  8.54 us
  transfers between devices with their start and end apart: 2, of which 0 were waited for; matrix products, arithmetic and copies ran while one was open for 0% of the time, Pallas kernels for 3%

profile of v3, /device:TPU:32, one launch (start us, length us, event | category | flops | bytes accessed | tf_op | source)
XLA Modules:
  0.0 100.4 jit_solution(1650191576378737333)
XLA Ops:
  0.0 1.9 %edges.1 = bf16[1280,128]{1,0:T(8,128)(2,1)S(1)} custom-call(bf16[576,128]{1,0:T(8,128)(2,1)} %bitcast.13, f32[24,24]{1,0:T(8,128)} %mean_ref.3, f32[24,24]{1,0:T(8,128)} %scale_ref.3, s32[24,24]{1,0:T(8,128)} %mask_ref.1, bf16[128,128]{1,0:T(8,128)(2,1)} %lg.3, bf16[128,128]{1,0:T(8,128)(2,1)} %lv.3, bf16[128,128]{1,0:T(8,128)(2,1)} %rg.3, bf16[128,128]{1,0:T(8,128)(2,1)} %rv.3), custom_call_target="tpu_custom_call" | custom-call | tf_op jit(solution)/shard_map/edges/pallas_call | solution.py:269
  1.9 30.6 %all_to_all.20 = bf16[128,5,2,128]{3,2,1,0:T(2,128)(2,1)S(1)} all-to-all(bf16[128,5,2,128]{3,2,1,0:T(2,128)(2,1)S(1)} %bitcast.16), channel_id=1, replica_groups=mesh['z_lo'=2,'x'=4,'core'=2,'z_hi'=4,'y'=4] {'z_hi','y','z_lo','x'}, dimensions={0} | all-to-all | bytes 655360 | tf_op jit(solution)/shard_map/all_to_all | solution.py:283
  32.5 0.3 take_right.1.right_ref.own_ref
  32.8 0.1 collective-permute-start
  33.0 0.6 ready.1
  33.6 0.3 take_left.1.left_ref
  33.9 0.5 mix_own.1.own_ref
  34.3 0.0 copy-start.1
  34.4 0.0 copy-start.2
  34.4 0.0 copy-start.3
  34.4 0.0 copy-start.4
  34.4 0.0 copy-start.10
  34.4 0.0 collective-permute-done.right_ref.other_ref
  34.4 0.5 mix.1
  34.9 19.8 %all_to_all.21 = bf16[128,3,2,128]{3,2,1,0:T(2,128)(2,1)S(1)} all-to-all(bf16[128,3,2,128]{3,2,1,0:T(2,128)(2,1)S(1)} %bitcast.20), channel_id=1, replica_groups=mesh['z_lo'=2,'x'=4,'core'=2,'z_hi'=4,'y'=4] {'z_hi','y','z_lo','x'}, dimensions={0} | all-to-all | bytes 393216 | tf_op jit(solution)/shard_map/all_to_all | solution.py:283
  54.7 0.7 middle.1
  55.4 18.4 %all_to_all.22 = bf16[128,3,2,128]{3,2,1,0:T(2,128)(2,1)S(1)} all-to-all(bf16[128,3,2,128]{3,2,1,0:T(2,128)(2,1)S(1)} %bitcast.22), channel_id=1, replica_groups=mesh['z_lo'=2,'x'=4,'core'=2,'z_hi'=4,'y'=4] {'z_hi','y','z_lo','x'}, dimensions={0} | all-to-all | bytes 393216 | tf_op jit(solution)/shard_map/all_to_all | solution.py:283
  73.8 0.7 right_grad.1
  74.5 0.1 collective-permute-start.1
  74.7 0.6 prepare.1
  75.3 0.7 left_grad.1.lines_ref
  76.0 0.6 return.1
  76.6 22.5 %all_to_all.23 = bf16[128,5,2,128]{3,2,1,0:T(2,128)(2,1)S(1)} all-to-all(bf16[128,5,2,128]{3,2,1,0:T(2,128)(2,1)S(1)} %bitcast.21), channel_id=1, replica_groups=mesh['z_lo'=2,'x'=4,'core'=2,'z_hi'=4,'y'=4] {'z_hi','y','z_lo','x'}, dimensions={0} | all-to-all | bytes 655360 | tf_op jit(solution)/shard_map/all_to_all | solution.py:283
  99.2 1.3 %last.1 = f32[576,128]{1,0:T(8,128)} custom-call(bf16[1280,128]{1,0:T(8,128)(2,1)S(1)} %bitcast.17, f32[576,128]{1,0:T(8,128)S(1)} %get-tuple-element.41.normed_ref, f32[576,128]{1,0:T(8,128)S(1)} %get-tuple-element.42.scale_ref, f32[576,128]{1,0:T(8,128)S(1)} %get-tuple-element.43.base_ref, f32[4,576,128]{2,1,0:T(8,128)S(1)} %get-tuple-element.44.factors_ref, ...), custom_call_target="tpu_custom_call" | custom-call | tf_op jit(solution)/shard_map/last/pallas_call | solution.py:269
  (18 shorter events, 0.0 us)
Async XLA Ops:
  0.0 32.9 %copy-start.9 = (f32[24,24]{1,0:T(8,128)S(1)}, f32[24,24]{1,0:T(8,128)}, u32[]{:S(2)}) copy-start(f32[24,24]{1,0:T(8,128)} %scale_ref.3) | copy-start | bytes 6916
  0.0 32.9 %copy-start.8 = (f32[24,24]{1,0:T(8,128)S(1)}, f32[24,24]{1,0:T(8,128)}, u32[]{:S(2)}) copy-start(f32[24,24]{1,0:T(8,128)} %mean_ref.3) | copy-start | bytes 6916
  0.0 32.9 %copy-start = (bf16[24,24,128]{2,1,0:T(8,128)(2,1)S(1)}, bf16[24,24,128]{2,1,0:T(8,128)(2,1)}, u32[]{:S(2)}) copy-start(bf16[24,24,128]{2,1,0:T(8,128)(2,1)} %param.11) | copy-start | bytes 442372
  0.0 32.9 %copy-start.6 = (bf16[128,128]{1,0:T(8,128)(2,1)S(1)}, bf16[128,128]{1,0:T(8,128)(2,1)}, u32[]{:S(2)}) copy-start(bf16[128,128]{1,0:T(8,128)(2,1)} %weight_ref.3) | copy-start | bytes 98308
  0.0 32.9 %copy-start.7 = (bf16[128,128]{1,0:T(8,128)(2,1)S(1)}, bf16[128,128]{1,0:T(8,128)(2,1)}, u32[]{:S(2)}) copy-start(bf16[128,128]{1,0:T(8,128)(2,1)} %og.1) | copy-start | bytes 98308
  0.0 32.9 %copy-start.5 = (bf16[24,24,128]{2,1,0:T(8,128)(2,1)S(1)}, bf16[24,24,128]{2,1,0:T(8,128)(2,1)}, u32[]{:S(2)}) copy-start(bf16[24,24,128]{2,1,0:T(8,128)(2,1)} %param.15) | copy-start | bytes 442372
  32.8 1.6 %collective-permute-start = (bf16[192,384]{1,0:T(8,128)(2,1)S(1)}, bf16[192,384]{1,0:T(8,128)(2,1)S(1)}, u32[]{:S(2)}, u32[]{:S(2)}) collective-permute-start(bf16[192,384]{1,0:T(8,128)(2,1)S(1)} %take_right.1.right_ref.own_ref), channel_id=1, source_target_pairs={{0,16},{16,0},{1,17},{17,1},{2,18},{18,2},{3,19},{19,3},{4,20},{20... | collective-permute-start | bytes 442376 | tf_op jit(solution)/shard_map/ppermute | solution.py:287
  34.3 40.3 %copy-start.1 = (bf16[128,128]{1,0:T(8,128)(2,1)S(1)}, bf16[128,128]{1,0:T(8,128)(2,1)}, u32[]{:S(2)}) copy-start(bf16[128,128]{1,0:T(8,128)(2,1)} %lg.3) | copy-start | bytes 98308
  34.4 40.3 %copy-start.2 = (bf16[128,128]{1,0:T(8,128)(2,1)S(1)}, bf16[128,128]{1,0:T(8,128)(2,1)}, u32[]{:S(2)}) copy-start(bf16[128,128]{1,0:T(8,128)(2,1)} %lv.3) | copy-start | bytes 98308
  34.4 40.3 %copy-start.3 = (bf16[128,128]{1,0:T(8,128)(2,1)S(1)}, bf16[128,128]{1,0:T(8,128)(2,1)}, u32[]{:S(2)}) copy-start(bf16[128,128]{1,0:T(8,128)(2,1)} %rg.3) | copy-start | bytes 98308
  34.4 40.3 %copy-start.4 = (bf16[128,128]{1,0:T(8,128)(2,1)S(1)}, bf16[128,128]{1,0:T(8,128)(2,1)}, u32[]{:S(2)}) copy-start(bf16[128,128]{1,0:T(8,128)(2,1)} %rv.3) | copy-start | bytes 98308
  34.4 40.3 %copy-start.10 = (s32[24,24]{1,0:T(8,128)S(1)}, s32[24,24]{1,0:T(8,128)}, u32[]{:S(2)}) copy-start(s32[24,24]{1,0:T(8,128)} %mask_ref.1) | copy-start | bytes 6916
  74.5 1.5 %collective-permute-start.1 = (bf16[192,384]{1,0:T(8,128)(2,1)S(1)}, bf16[192,384]{1,0:T(8,128)(2,1)S(1)}, u32[]{:S(2)}, u32[]{:S(2)}) collective-permute-start(bf16[192,384]{1,0:T(8,128)(2,1)S(1)} %get-tuple-element.39), channel_id=1, source_target_pairs={{0,16},{16,0},{1,17},{17,1},{2,18},{18,2},{3,19},{19,3},{4,20},{20... | collective-permute-start | bytes 442376 | tf_op jit(solution)/shard_map/ppermute | solution.py:287

commit v4 on v3

--- a/solution.py
+++ b/solution.py
@@ -26,8 +26,8 @@
     return lax.dot_general(a, b, (over, ((), ())), preferred_element_type=f32)
 
 
-def spread_pairs(ref):
-    turned = jnp.transpose(ref[...].astype(f32))
+def spread_pairs(value):
+    turned = jnp.transpose(value)
     return jnp.concatenate([jnp.broadcast_to(turned[:, i : i + 1], (SIDE, WIDTH)) for i in range(SIDE)], axis=0)
 
 
@@ -48,6 +48,11 @@
     centre = jnp.mean(grad, axis=-1, keepdims=True)
     along = jnp.mean(grad * normed, axis=-1, keepdims=True)
     return scale * (grad - centre - normed * along)
+
+
+def rows_in(line, lines):
+    many = -(-SIDE // lines)
+    return range(line * many, min((line + 1) * many, SIDE))
 
 
 def to_messages(parts, scratch):
@@ -55,7 +60,7 @@
     lines = total // len(parts)
     for p, part in enumerate(parts):
         for r in range(lines):
-            stack = [part[i * SIDE : (i + 1) * SIDE] for i in range(r, SIDE, lines)]
+            stack = [part[i * SIDE : (i + 1) * SIDE] for i in rows_in(r, lines)]
             stack.append(jnp.zeros((WIDTH - len(stack) * SIDE, WIDTH), f32))
             turned = jnp.transpose(jnp.concatenate(stack, axis=0))
             scratch[pl.ds(lines * p + r, WIDTH, stride=total), :] = turned
@@ -71,7 +76,7 @@
         rows = [None] * SIDE
         for r in range(lines):
             turned = jnp.transpose(scratch[pl.ds(lines * p + r, WIDTH, stride=total), :])
-            for n, i in enumerate(range(r, SIDE, lines)):
+            for n, i in enumerate(rows_in(r, lines)):
                 rows[i] = turned[n * SIDE : (n + 1) * SIDE]
         parts.append(jnp.concatenate(rows, axis=0))
     return parts
@@ -83,7 +88,7 @@
     order = {spot(c): c for c in range(BLOCKS)}
     for r in range(lines):
         found = [scratch[pl.ds(c * GROUPS * total + first + r, GROUPS, stride=total), :] for c in range(BLOCKS)]
-        for n, i in enumerate(range(r, SIDE, lines)):
+        for n, i in enumerate(rows_in(r, lines)):
             for t in range(TILES):
                 tile = None
                 for at in range(BLOCKS):
@@ -103,7 +108,7 @@
         t, after = begin // WIDTH, (begin + SIDE - 1) // WIDTH
         for r in range(lines):
             line = None
-            for n, i in enumerate(range(r, SIDE, lines)):
+            for n, i in enumerate(rows_in(r, lines)):
                 shift = n * SIDE - begin
                 piece = roll(load(i, t), shift)
                 if after != t:
@@ -118,8 +123,8 @@
 
 
 def normalise(pair_ref, mean_ref, scale_ref):
-    scale = spread_pairs(scale_ref)
-    normed = (pair_ref[...].astype(f32) - spread_pairs(mean_ref)) * scale
+    scale = spread_pairs(scale_ref[...])
+    normed = (pair_ref[...].astype(f32) - spread_pairs(mean_ref[...])) * scale
     return normed, scale
 
 
@@ -131,13 +136,12 @@
     for copy in copies:
         copy.wait()
     pair_ref, mean_ref, scale_ref, mask_ref, lg, lv, rg, rv = held
-    normed, _ = normalise(pair_ref, mean_ref, scale_ref)
-    low = normed.astype(bf16)
-    keep = spread_pairs(mask_ref)
+    kept_scale = spread_pairs(scale_ref[...] * mask_ref[...].astype(f32))
+    low = ((pair_ref[...].astype(f32) - spread_pairs(mean_ref[...])) * kept_scale).astype(bf16)
     parts = []
     for gate, value in ((lg, lv), (rg, rv)):
         both = dot(low, jnp.concatenate([gate[...], value[...]], axis=1))
-        parts.append(jax.nn.sigmoid(both[:, :WIDTH]) * both[:, WIDTH:] * keep)
+        parts.append(jax.nn.sigmoid(both[:, :WIDTH]) * both[:, WIDTH:])
     out_ref[...] = to_messages(parts, scratch)
 
 
@@ -210,14 +214,14 @@
     out_ref[...] = to_messages([grad_mix], scratch)
 
 
-def right_grad_kernel(in_ref, left_ref, grad_ref, own_ref, sent_ref, scratch, panel, sums):
+def right_grad_kernel(in_ref, left_ref, grad_ref, own_ref, sent_ref, scratch, panel):
     assemble_left(in_ref, scratch, panel, ALONE, place)
     grad = panel[...]
     grad_ref[...] = grad.astype(bf16)
-    sums[...] = dot(jnp.transpose(grad).astype(bf16), left_ref[...]).reshape(2, HALF, TOKENS)
-    core = lax.axis_index("core")
-    own_ref[...] = sums[core]
-    sent_ref[...] = sums[1 - core].astype(bf16)
+    first = lax.axis_index("core") == 0
+    sums = dot(jnp.transpose(grad).astype(bf16), left_ref[...])
+    own_ref[...] = jnp.where(first, sums[:HALF], sums[HALF:])
+    sent_ref[...] = jnp.where(first, sums[HALF:], sums[:HALF]).astype(bf16)
 
 
 def left_grad_kernel(grad_ref, own_ref, other_ref, out_ref, right, panel):
@@ -247,7 +251,7 @@
     scaled_ref[...] = scale
     base_ref[...] = dot(grad_gate_ref[...], og[...], ((1,), (1,)))
     low = normed.astype(bf16)
-    keep = spread_pairs(mask_ref)
+    keep = spread_pairs(mask_ref[...].astype(f32))
     for n, (gate, value) in enumerate(((lg, lv), (rg, rv))):
         both = dot(low, jnp.concatenate([gate[...], value[...]], axis=1))
         sig, lin = jax.nn.sigmoid(both[:, :WIDTH]), both[:, WIDTH:]
@@ -255,22 +259,34 @@
         factors_ref[2 * n] = keep * lin * sig * (1.0 - sig)
 
 
-def last_kernel(in_ref, normed_ref, scale_ref, base_ref, factors_ref, lg, lv, rg, rv, out_ref, scratch):
-    grads = from_messages(in_ref, scratch, 2)
-    grad_normed = base_ref[...]
-    for n, (gate, value) in enumerate(((lg, lv), (rg, rv))):
-        pre_grads = jnp.concatenate([grads[n] * factors_ref[2 * n], grads[n] * factors_ref[2 * n + 1]], axis=1)
-        weights = jnp.concatenate([gate[...], value[...]], axis=1)
-        grad_normed += dot(pre_grads.astype(bf16), weights, ((1,), (1,)))
-    out_ref[...] = layer_back(grad_normed, normed_ref[...], scale_ref[...])
-
-
-def call(kernel, outs, *args, scratch=(), name=None, space=VMEM, aliases={}):
+def last_kernel(
+    in_ref, normed_ref, scale_ref, base_ref, factors_ref, lg, lv, rg, rv, out_ref, scratch, held, sems
+):
+    scratch[...] = in_ref[...].astype(f32)
+    weights = [jnp.concatenate([gate[...], value[...]], axis=1) for gate, value in ((lg, lv), (rg, rv))]
+    copies = []
+    for r in range(PAIRED):
+        rows = rows_in(r, PAIRED)
+        here = slice(rows[0] * SIDE, (rows[-1] + 1) * SIDE)
+        grad_normed = base_ref[here, :]
+        for n in range(2):
+            turned = jnp.transpose(scratch[pl.ds(PAIRED * n + r, WIDTH, stride=2 * PAIRED), :])
+            grad = turned[: len(rows) * SIDE]
+            pre_grads = jnp.concatenate([grad * factors_ref[2 * n, here], grad * factors_ref[2 * n + 1, here]], axis=1)
+            grad_normed += dot(pre_grads.astype(bf16), weights[n], ((1,), (1,)))
+        held[here, :] = layer_back(grad_normed, normed_ref[here, :], scale_ref[here, :])
+        copies.append(pltpu.make_async_copy(held.at[here], out_ref.at[here], sems.at[r]))
+        copies[-1].start()
+    for copy in copies:
+        copy.wait()
+
+
+def call(kernel, outs, *args, scratch=(), name=None, space=VMEM, aliases={}, out_space=VMEM):
     return pl.pallas_call(
         kernel,
         out_shape=[jax.ShapeDtypeStruct(shape, dtype) for shape, dtype in outs],
         in_specs=[space for _ in args],
-        out_specs=[VMEM for _ in outs],
+        out_specs=[out_space for _ in outs],
         scratch_shapes=list(scratch),
         input_output_aliases=aliases,
         compiler_params=pltpu.CompilerParams(vmem_limit_bytes=48 * 1024 * 1024),
@@ -340,7 +356,7 @@
     came = spread(sent)
     grad, own, sent = call(
         right_grad_kernel, [panel, wide, panel], came, left,
-        scratch=[line_one, panel_left, pltpu.VMEM((2, HALF, TOKENS), f32)],
+        scratch=[line_one, panel_left],
         name="right_grad",
     )
     other = swap(sent)
@@ -358,8 +374,9 @@
     _, sent = call(return_kernel, [lined, two], lines, own, other, scratch=[panels_out], name="return", aliases={0: 0})
     came = spread(sent)
     (out,) = call(
-        last_kernel, [many], came, *prepared, left_gate, left_value, right_gate, right_value, scratch=[line_two],
-        name="last",
+        last_kernel, [many], came, *prepared, left_gate, left_value, right_gate, right_value,
+        scratch=[line_two, pltpu.VMEM((PAIRS, WIDTH), f32), pltpu.SemaphoreType.DMA((PAIRED,))], name="last",
+        out_space=HBM,
     )
     return out.reshape(SIDE, SIDE, WIDTH)
 

time: 101 us -> 100 us (0.990)
  no operation moved by 1% of the time
where the time goes in v4:
time: 100 us
  blocking collectives  91.4 us (91%)
  Pallas kernels  8.2 us (8%)
    all_to_all x4, blocking collectives, spread(): lax.all_to_all(paired, SPREAD, 0, 0, tiled=True).reshape(messages.shape)  91.4 us
    pallas_call x12, Pallas kernels, call(): pl.pallas_call(kernel, out_shape=[jax.ShapeDtypeStruct(shape, dtype) for...  8.2 us
  transfers between devices with their start and end apart: 2, of which 0 were waited for; matrix products, arithmetic and copies ran while one was open for 0% of the time, Pallas kernels for 3%

profile of v4, /device:TPU:32, one launch (start us, length us, event | category | flops | bytes accessed | tf_op | source)
XLA Modules:
  0.0 100.1 jit_solution(118117854393992580)
XLA Ops:
  0.0 1.8 %edges.1 = bf16[1280,128]{1,0:T(8,128)(2,1)S(1)} custom-call(bf16[576,128]{1,0:T(8,128)(2,1)} %bitcast.13, f32[24,24]{1,0:T(8,128)} %mean_ref.3, f32[24,24]{1,0:T(8,128)} %scale_ref.3, s32[24,24]{1,0:T(8,128)} %mask_ref.1, bf16[128,128]{1,0:T(8,128)(2,1)} %lg.3, bf16[128,128]{1,0:T(8,128)(2,1)} %lv.3, bf16[128,128]{1,0:T(8,128)(2,1)} %rg.3, bf16[128,128]{1,0:T(8,128)(2,1)} %rv.3), custom_call_target="tpu_custom_call" | custom-call | tf_op jit(solution)/shard_map/edges/pallas_call | solution.py:285
  1.8 30.6 %all_to_all.20 = bf16[128,5,2,128]{3,2,1,0:T(2,128)(2,1)S(1)} all-to-all(bf16[128,5,2,128]{3,2,1,0:T(2,128)(2,1)S(1)} %bitcast.16), channel_id=1, replica_groups=mesh['z_lo'=2,'x'=4,'core'=2,'z_hi'=4,'y'=4] {'z_hi','y','z_lo','x'}, dimensions={0} | all-to-all | bytes 655360 | tf_op jit(solution)/shard_map/all_to_all | solution.py:299
  32.4 0.3 take_right.1.right_ref.own_ref
  32.7 0.1 collective-permute-start
  32.9 0.6 ready.1
  33.5 0.3 take_left.1.left_ref
  33.8 0.5 mix_own.1.own_ref
  34.2 0.0 copy-start.1
  34.2 0.0 copy-start.2
  34.2 0.0 copy-start.3
  34.3 0.0 copy-start.4
  34.3 0.0 copy-start.10
  34.3 0.0 collective-permute-done.right_ref.other_ref
  34.3 0.5 mix.1
  34.8 19.8 %all_to_all.21 = bf16[128,3,2,128]{3,2,1,0:T(2,128)(2,1)S(1)} all-to-all(bf16[128,3,2,128]{3,2,1,0:T(2,128)(2,1)S(1)} %bitcast.20), channel_id=1, replica_groups=mesh['z_lo'=2,'x'=4,'core'=2,'z_hi'=4,'y'=4] {'z_hi','y','z_lo','x'}, dimensions={0} | all-to-all | bytes 393216 | tf_op jit(solution)/shard_map/all_to_all | solution.py:299
  54.6 0.6 middle.1
  55.3 18.4 %all_to_all.22 = bf16[128,3,2,128]{3,2,1,0:T(2,128)(2,1)S(1)} all-to-all(bf16[128,3,2,128]{3,2,1,0:T(2,128)(2,1)S(1)} %bitcast.22), channel_id=1, replica_groups=mesh['z_lo'=2,'x'=4,'core'=2,'z_hi'=4,'y'=4] {'z_hi','y','z_lo','x'}, dimensions={0} | all-to-all | bytes 393216 | tf_op jit(solution)/shard_map/all_to_all | solution.py:299
  73.7 0.6 right_grad.1
  74.3 0.1 collective-permute-start.1
  74.4 0.6 prepare.1
  75.1 0.7 left_grad.1.lines_ref
  75.8 0.6 return.1
  76.3 22.5 %all_to_all.23 = bf16[128,5,2,128]{3,2,1,0:T(2,128)(2,1)S(1)} all-to-all(bf16[128,5,2,128]{3,2,1,0:T(2,128)(2,1)S(1)} %bitcast.21), channel_id=1, replica_groups=mesh['z_lo'=2,'x'=4,'core'=2,'z_hi'=4,'y'=4] {'z_hi','y','z_lo','x'}, dimensions={0} | all-to-all | bytes 655360 | tf_op jit(solution)/shard_map/all_to_all | solution.py:299
  98.9 1.2 %last.1 = f32[576,128]{1,0:T(8,128)} custom-call(bf16[1280,128]{1,0:T(8,128)(2,1)S(1)} %bitcast.17, f32[576,128]{1,0:T(8,128)S(1)} %get-tuple-element.41.normed_ref, f32[576,128]{1,0:T(8,128)S(1)} %get-tuple-element.42.scale_ref, f32[576,128]{1,0:T(8,128)S(1)} %get-tuple-element.43.base_ref, f32[4,576,128]{2,1,0:T(8,128)S(1)} %get-tuple-element.44.factors_ref, ...), custom_call_target="tpu_custom_call" | custom-call | tf_op jit(solution)/shard_map/last/pallas_call | solution.py:285
  (18 shorter events, 0.0 us)
Async XLA Ops:
  0.0 32.8 %copy-start.9 = (f32[24,24]{1,0:T(8,128)S(1)}, f32[24,24]{1,0:T(8,128)}, u32[]{:S(2)}) copy-start(f32[24,24]{1,0:T(8,128)} %scale_ref.3) | copy-start | bytes 6916
  0.0 32.8 %copy-start.8 = (f32[24,24]{1,0:T(8,128)S(1)}, f32[24,24]{1,0:T(8,128)}, u32[]{:S(2)}) copy-start(f32[24,24]{1,0:T(8,128)} %mean_ref.3) | copy-start | bytes 6916
  0.0 32.8 %copy-start = (bf16[24,24,128]{2,1,0:T(8,128)(2,1)S(1)}, bf16[24,24,128]{2,1,0:T(8,128)(2,1)}, u32[]{:S(2)}) copy-start(bf16[24,24,128]{2,1,0:T(8,128)(2,1)} %param.11) | copy-start | bytes 442372
  0.0 32.8 %copy-start.6 = (bf16[128,128]{1,0:T(8,128)(2,1)S(1)}, bf16[128,128]{1,0:T(8,128)(2,1)}, u32[]{:S(2)}) copy-start(bf16[128,128]{1,0:T(8,128)(2,1)} %weight_ref.3) | copy-start | bytes 98308
  0.0 32.8 %copy-start.7 = (bf16[128,128]{1,0:T(8,128)(2,1)S(1)}, bf16[128,128]{1,0:T(8,128)(2,1)}, u32[]{:S(2)}) copy-start(bf16[128,128]{1,0:T(8,128)(2,1)} %og.1) | copy-start | bytes 98308
  0.0 32.8 %copy-start.5 = (bf16[24,24,128]{2,1,0:T(8,128)(2,1)S(1)}, bf16[24,24,128]{2,1,0:T(8,128)(2,1)}, u32[]{:S(2)}) copy-start(bf16[24,24,128]{2,1,0:T(8,128)(2,1)} %param.15) | copy-start | bytes 442372
  32.7 1.6 %collective-permute-start = (bf16[192,384]{1,0:T(8,128)(2,1)S(1)}, bf16[192,384]{1,0:T(8,128)(2,1)S(1)}, u32[]{:S(2)}, u32[]{:S(2)}) collective-permute-start(bf16[192,384]{1,0:T(8,128)(2,1)S(1)} %take_right.1.right_ref.own_ref), channel_id=1, source_target_pairs={{0,16},{16,0},{1,17},{17,1},{2,18},{18,2},{3,19},{19,3},{4,20},{20... | collective-permute-start | bytes 442376 | tf_op jit(solution)/shard_map/ppermute | solution.py:303
  34.2 40.1 %copy-start.1 = (bf16[128,128]{1,0:T(8,128)(2,1)S(1)}, bf16[128,128]{1,0:T(8,128)(2,1)}, u32[]{:S(2)}) copy-start(bf16[128,128]{1,0:T(8,128)(2,1)} %lg.3) | copy-start | bytes 98308
  34.2 40.1 %copy-start.2 = (bf16[128,128]{1,0:T(8,128)(2,1)S(1)}, bf16[128,128]{1,0:T(8,128)(2,1)}, u32[]{:S(2)}) copy-start(bf16[128,128]{1,0:T(8,128)(2,1)} %lv.3) | copy-start | bytes 98308
  34.2 40.1 %copy-start.3 = (bf16[128,128]{1,0:T(8,128)(2,1)S(1)}, bf16[128,128]{1,0:T(8,128)(2,1)}, u32[]{:S(2)}) copy-start(bf16[128,128]{1,0:T(8,128)(2,1)} %rg.3) | copy-start | bytes 98308
  34.3 40.1 %copy-start.4 = (bf16[128,128]{1,0:T(8,128)(2,1)S(1)}, bf16[128,128]{1,0:T(8,128)(2,1)}, u32[]{:S(2)}) copy-start(bf16[128,128]{1,0:T(8,128)(2,1)} %rv.3) | copy-start | bytes 98308
  34.3 40.1 %copy-start.10 = (s32[24,24]{1,0:T(8,128)S(1)}, s32[24,24]{1,0:T(8,128)}, u32[]{:S(2)}) copy-start(s32[24,24]{1,0:T(8,128)} %mask_ref.1) | copy-start | bytes 6916
  74.3 1.5 %collective-permute-start.1 = (bf16[192,384]{1,0:T(8,128)(2,1)S(1)}, bf16[192,384]{1,0:T(8,128)(2,1)S(1)}, u32[]{:S(2)}, u32[]{:S(2)}) collective-permute-start(bf16[192,384]{1,0:T(8,128)(2,1)S(1)} %get-tuple-element.39), channel_id=1, source_target_pairs={{0,16},{16,0},{1,17},{17,1},{2,18},{18,2},{3,19},{19,3},{4,20},{20... | collective-permute-start | bytes 442376 | tf_op jit(solution)/shard_map/ppermute | solution.py:303

commit v5 on v4

--- a/solution.py
+++ b/solution.py
@@ -1,3 +1,5 @@
+import functools
+
 import jax
 import jax.numpy as jnp
 from jax import lax
@@ -145,7 +147,8 @@
     out_ref[...] = to_messages(parts, scratch)
 
 
-def take_right_kernel(in_ref, out_ref, scratch, panels):
+def take_right_kernel(in_ref, *refs):
+    given, (out_ref, *made), (scratch, panels) = refs[:6], refs[6:9], refs[9:]
     scratch[...] = in_ref[...].astype(f32)
 
     def store(i, t, tile):
@@ -155,6 +158,7 @@
     for group in range(GROUPS):
         rows = [panels[t, pl.ds(group, SIDE, stride=GROUPS + 1), :] for t in range(TILES)]
         out_ref[group * SIDE : (group + 1) * SIDE, :] = jnp.concatenate(rows, axis=1).astype(bf16)
+    on_core(1, ready, given, made)
 
 
 def assemble_left(in_ref, scratch, panel, lines, spot):
@@ -195,12 +199,23 @@
         out_ref[(2 * n + 1) * size : (2 * n + 2) * size, :] = jnp.where(first, other, own).astype(bf16)
 
 
-def ready_kernel(pair_ref, mean_ref, scale_ref, cot_ref, gate_ref, weight_ref, grad_ref, factor_ref):
+def ready(given, grad_ref, factor_ref):
+    pair_ref, mean_ref, scale_ref, cot_ref, gate_ref, weight_ref = given
     normed, _ = normalise(pair_ref, mean_ref, scale_ref)
     out_sig = jax.nn.sigmoid(dot(normed.astype(bf16), gate_ref[...]))
     grad_y = cot_ref[...].astype(f32) * out_sig
     grad_ref[...] = dot(grad_y.astype(bf16), weight_ref[...], ((1,), (1,)))
     factor_ref[...] = grad_y * (1.0 - out_sig)
+
+
+def on_core(core, work, given, made):
+    @pl.when(lax.axis_index("core") == core)
+    def _():
+        work(given, *made)
+
+
+def later_kernel(work, count, *refs):
+    on_core(0, work, refs[count:-count], refs[-count:])
 
 
 def middle_kernel(in_ref, grad_ref, factor_ref, weight_ref, out_ref, grad_gate_ref, scratch):
@@ -214,7 +229,8 @@
     out_ref[...] = to_messages([grad_mix], scratch)
 
 
-def right_grad_kernel(in_ref, left_ref, grad_ref, own_ref, sent_ref, scratch, panel):
+def right_grad_kernel(in_ref, left_ref, *refs):
+    given, (grad_ref, own_ref, sent_ref), made, (scratch, panel) = refs[:10], refs[10:13], refs[13:17], refs[17:]
     assemble_left(in_ref, scratch, panel, ALONE, place)
     grad = panel[...]
     grad_ref[...] = grad.astype(bf16)
@@ -222,6 +238,7 @@
     sums = dot(jnp.transpose(grad).astype(bf16), left_ref[...])
     own_ref[...] = jnp.where(first, sums[:HALF], sums[HALF:])
     sent_ref[...] = jnp.where(first, sums[HALF:], sums[:HALF]).astype(bf16)
+    on_core(1, prepare, given, made)
 
 
 def left_grad_kernel(grad_ref, own_ref, other_ref, out_ref, right, panel):
@@ -243,9 +260,8 @@
     out_ref[...] = kept_ref[...].astype(bf16)
 
 
-def prepare_kernel(
-    pair_ref, mean_ref, scale_ref, mask_ref, grad_gate_ref, lg, lv, rg, rv, og, normed_ref, scaled_ref, base_ref, factors_ref
-):
+def prepare(given, normed_ref, scaled_ref, base_ref, factors_ref):
+    pair_ref, mean_ref, scale_ref, mask_ref, grad_gate_ref, lg, lv, rg, rv, og = given
     normed, scale = normalise(pair_ref, mean_ref, scale_ref)
     normed_ref[...] = normed
     scaled_ref[...] = scale
@@ -335,7 +351,11 @@
         name="edges", space=HBM,
     )
     came = spread(sent)
-    (right_own,) = call(take_right_kernel, [panel], came, scratch=[line_two, panels_in], name="take_right")
+    many = ((PAIRS, WIDTH), f32)
+    given = [pair, norm_mean, norm_scale, cot, output_gate, output_weight]
+    right_own, *made = call(
+        take_right_kernel, [panel, many, many], came, *given, scratch=[line_two, panels_in], name="take_right"
+    )
     right_other = swap(right_own)
     (left,) = call(take_left_kernel, [panel], came, scratch=[line_two, panel_left], name="take_left")
     line_half, panel_half = pltpu.VMEM((WIDTH * ALONE // 2, WIDTH), f32), pltpu.VMEM((HALF, 2 * WIDTH), f32)
@@ -343,8 +363,7 @@
         mix_own_kernel, [((WIDTH * ALONE // 2, WIDTH), f32)], left, right_own, scratch=[panel_half], name="mix_own",
     )
     grad_mixnorm, factor = call(
-        ready_kernel, [((PAIRS, WIDTH), f32)] * 2, pair, norm_mean, norm_scale, cot, output_gate, output_weight,
-        name="ready",
+        functools.partial(later_kernel, ready, 2), [many, many], *made, *given, name="ready", aliases={0: 0, 1: 1}
     )
     mixed_own, grad_mixnorm, factor = lax.optimization_barrier((mixed_own, grad_mixnorm, factor))
     (sent,) = call(mix_kernel, [one], left, right_other, mixed_own, scratch=[line_half, panel_half], name="mix")
@@ -354,10 +373,13 @@
         name="middle",
     )
     came = spread(sent)
-    grad, own, sent = call(
-        right_grad_kernel, [panel, wide, panel], came, left,
-        scratch=[line_one, panel_left],
-        name="right_grad",
+    given = [
+        pair, norm_mean, norm_scale, pair_mask, grad_gate, left_gate, left_value, right_gate, right_value, output_gate
+    ]
+    factors = ((4, PAIRS, WIDTH), f32)
+    grad, own, sent, *made = call(
+        right_grad_kernel, [panel, wide, panel, many, many, many, factors], came, left, *given,
+        scratch=[line_one, panel_left], name="right_grad",
     )
     other = swap(sent)
     lined = ((WIDTH * 2 * PAIRED, WIDTH), f32)
@@ -365,10 +387,9 @@
         left_grad_kernel, [lined], grad, right_own, right_other,
         scratch=[pltpu.VMEM((2, HALF, TOKENS), bf16), panel_left], name="left_grad",
     )
-    many = ((PAIRS, WIDTH), f32)
     prepared = call(
-        prepare_kernel, [many, many, many, ((4, PAIRS, WIDTH), f32)], pair, norm_mean, norm_scale, pair_mask, grad_gate,
-        left_gate, left_value, right_gate, right_value, output_gate, name="prepare",
+        functools.partial(later_kernel, prepare, 4), [many, many, many, factors], *made, *given, name="prepare",
+        aliases={n: n for n in range(4)},
     )
     lines, prepared = lax.optimization_barrier((lines, prepared))
     _, sent = call(return_kernel, [lined, two], lines, own, other, scratch=[panels_out], name="return", aliases={0: 0})

time: 100 us -> 99.6 us (level)
  blocking collectives: 91.4 us -> 90.3 us
    all_to_all x4, blocking collectives: 91.4 us -> 90.3 us  [spread(): lax.all_to_all(paired, SPREAD, 0, 0, tiled=True).reshape(messages.shape)]
where the time goes in v5:
time: 99.6 us; the launch traced here: 99.4 us
  blocking collectives  90.3 us (91%)
  Pallas kernels  8.42 us (8%)
    all_to_all x4, blocking collectives, spread(): lax.all_to_all(paired, SPREAD, 0, 0, tiled=True).reshape(messages.shape)  90.3 us
    pallas_call x12, Pallas kernels, call(): pl.pallas_call(kernel, out_shape=[jax.ShapeDtypeStruct(shape, dtype) for...  8.42 us
  transfers between devices with their start and end apart: 2, of which 0 were waited for; matrix products, arithmetic and copies ran while one was open for 0% of the time, Pallas kernels for 3%

profile of v5, /device:TPU:32, one launch (start us, length us, event | category | flops | bytes accessed | tf_op | source)
XLA Modules:
  0.0 99.4 jit_solution(13165796462236925742)
XLA Ops:
  0.0 1.8 %edges.1 = bf16[1280,128]{1,0:T(8,128)(2,1)S(1)} custom-call(bf16[576,128]{1,0:T(8,128)(2,1)} %bitcast.11, f32[24,24]{1,0:T(8,128)} %refs_5_.7, f32[24,24]{1,0:T(8,128)} %refs_6_.7, s32[24,24]{1,0:T(8,128)} %refs_7_.7, bf16[128,128]{1,0:T(8,128)(2,1)} %lg.1, bf16[128,128]{1,0:T(8,128)(2,1)} %lv.1, bf16[128,128]{1,0:T(8,128)(2,1)} %rg.1, bf16[128,128]{1,0:T(8,128)(2,1)} %rv.1), custom_call_target="tpu_custom_call" | custom-call | tf_op jit(solution)/shard_map/edges/pallas_call | solution.py:301
  1.8 30.6 %all_to_all.20 = bf16[128,5,2,128]{3,2,1,0:T(2,128)(2,1)S(1)} all-to-all(bf16[128,5,2,128]{3,2,1,0:T(2,128)(2,1)S(1)} %bitcast.18), channel_id=1, replica_groups=mesh['z_lo'=2,'x'=4,'core'=2,'z_hi'=4,'y'=4] {'z_hi','y','z_lo','x'}, dimensions={0} | all-to-all | bytes 655360 | tf_op jit(solution)/shard_map/all_to_all | solution.py:315
  32.4 0.0 copy-done.8
  32.4 0.3 take_right.1
  32.7 0.1 collective-permute-start
  32.8 0.3 take_left.1.left_ref
  33.1 0.5 mix_own.1.own_ref
  33.6 0.6 ready.1
  34.2 0.0 copy-start.4
  34.2 0.0 copy-start.5
  34.2 0.0 copy-start.10
  34.3 0.0 collective-permute-done.right_ref.other_ref
  34.3 0.5 mix.1
  34.7 19.5 %all_to_all.21 = bf16[128,3,2,128]{3,2,1,0:T(2,128)(2,1)S(1)} all-to-all(bf16[128,3,2,128]{3,2,1,0:T(2,128)(2,1)S(1)} %bitcast.22), channel_id=1, replica_groups=mesh['z_lo'=2,'x'=4,'core'=2,'z_hi'=4,'y'=4] {'z_hi','y','z_lo','x'}, dimensions={0} | all-to-all | bytes 393216 | tf_op jit(solution)/shard_map/all_to_all | solution.py:315
  54.2 0.7 middle.1
  54.9 18.1 %all_to_all.22 = bf16[128,3,2,128]{3,2,1,0:T(2,128)(2,1)S(1)} all-to-all(bf16[128,3,2,128]{3,2,1,0:T(2,128)(2,1)S(1)} %bitcast.26), channel_id=1, replica_groups=mesh['z_lo'=2,'x'=4,'core'=2,'z_hi'=4,'y'=4] {'z_hi','y','z_lo','x'}, dimensions={0} | all-to-all | bytes 393216 | tf_op jit(solution)/shard_map/all_to_all | solution.py:315
  73.1 0.6 right_grad.1
  73.6 0.1 collective-permute-start.1
  73.7 0.8 prepare.1
  74.6 0.7 left_grad.1.lines_ref
  75.3 0.0 collective-permute-done.1.other_ref
  75.3 0.6 return.1
  75.8 22.2 %all_to_all.23 = bf16[128,5,2,128]{3,2,1,0:T(2,128)(2,1)S(1)} all-to-all(bf16[128,5,2,128]{3,2,1,0:T(2,128)(2,1)S(1)} %bitcast.25), channel_id=1, replica_groups=mesh['z_lo'=2,'x'=4,'core'=2,'z_hi'=4,'y'=4] {'z_hi','y','z_lo','x'}, dimensions={0} | all-to-all | bytes 655360 | tf_op jit(solution)/shard_map/all_to_all | solution.py:315
  98.0 1.2 %last.1 = f32[576,128]{1,0:T(8,128)} custom-call(bf16[1280,128]{1,0:T(8,128)(2,1)S(1)} %bitcast.19, f32[576,128]{1,0:T(8,128)S(1)} %get-tuple-element.55.normed_ref, f32[576,128]{1,0:T(8,128)S(1)} %get-tuple-element.56.scale_ref, f32[576,128]{1,0:T(8,128)S(1)} %get-tuple-element.57.base_ref, f32[4,576,128]{2,1,0:T(8,128)S(1)} %get-tuple-element.58.factors_ref, ...), custom_call_target="tpu_custom_call" | custom-call | tf_op jit(solution)/shard_map/last/pallas_call | solution.py:301
  (18 shorter events, 0.0 us)
Async XLA Ops:
  0.0 32.4 %copy-start = (bf16[24,24,128]{2,1,0:T(8,128)(2,1)S(1)}, bf16[24,24,128]{2,1,0:T(8,128)(2,1)}, u32[]{:S(2)}) copy-start(bf16[24,24,128]{2,1,0:T(8,128)(2,1)} %param.11) | copy-start | bytes 442372
  0.0 32.4 %copy-start.7 = (f32[24,24]{1,0:T(8,128)S(1)}, f32[24,24]{1,0:T(8,128)}, u32[]{:S(2)}) copy-start(f32[24,24]{1,0:T(8,128)} %refs_5_.7) | copy-start | bytes 6916
  0.0 32.4 %copy-start.8 = (f32[24,24]{1,0:T(8,128)S(1)}, f32[24,24]{1,0:T(8,128)}, u32[]{:S(2)}) copy-start(f32[24,24]{1,0:T(8,128)} %refs_6_.7) | copy-start | bytes 6916
  0.0 32.4 %copy-start.1 = (bf16[24,24,128]{2,1,0:T(8,128)(2,1)S(1)}, bf16[24,24,128]{2,1,0:T(8,128)(2,1)}, u32[]{:S(2)}) copy-start(bf16[24,24,128]{2,1,0:T(8,128)(2,1)} %param.15) | copy-start | bytes 442372
  0.0 32.4 %copy-start.6 = (bf16[128,128]{1,0:T(8,128)(2,1)S(1)}, bf16[128,128]{1,0:T(8,128)(2,1)}, u32[]{:S(2)}) copy-start(bf16[128,128]{1,0:T(8,128)(2,1)} %refs_13_.1) | copy-start | bytes 98308
  0.0 32.4 %copy-start.9 = (bf16[128,128]{1,0:T(8,128)(2,1)S(1)}, bf16[128,128]{1,0:T(8,128)(2,1)}, u32[]{:S(2)}) copy-start(bf16[128,128]{1,0:T(8,128)(2,1)} %weight_ref.1) | copy-start | bytes 98308
  32.7 1.5 %collective-permute-start = (bf16[192,384]{1,0:T(8,128)(2,1)S(1)}, bf16[192,384]{1,0:T(8,128)(2,1)S(1)}, u32[]{:S(2)}, u32[]{:S(2)}) collective-permute-start(bf16[192,384]{1,0:T(8,128)(2,1)S(1)} %get-tuple-element.32.right_ref.own_ref), channel_id=1, source_target_pairs={{0,16},{16,0},{1,17},{17,1},{2,18},{18,2},{3,19},{19,3},{4,20},{20... | collective-permute-start | bytes 442376 | tf_op jit(solution)/shard_map/ppermute | solution.py:319
  34.2 38.8 %copy-start.2 = (bf16[128,128]{1,0:T(8,128)(2,1)S(1)}, bf16[128,128]{1,0:T(8,128)(2,1)}, u32[]{:S(2)}) copy-start(bf16[128,128]{1,0:T(8,128)(2,1)} %lg.1) | copy-start | bytes 98308
  34.2 38.8 %copy-start.3 = (bf16[128,128]{1,0:T(8,128)(2,1)S(1)}, bf16[128,128]{1,0:T(8,128)(2,1)}, u32[]{:S(2)}) copy-start(bf16[128,128]{1,0:T(8,128)(2,1)} %lv.1) | copy-start | bytes 98308
  34.2 38.8 %copy-start.4 = (bf16[128,128]{1,0:T(8,128)(2,1)S(1)}, bf16[128,128]{1,0:T(8,128)(2,1)}, u32[]{:S(2)}) copy-start(bf16[128,128]{1,0:T(8,128)(2,1)} %rg.1) | copy-start | bytes 98308
  34.2 38.8 %copy-start.5 = (bf16[128,128]{1,0:T(8,128)(2,1)S(1)}, bf16[128,128]{1,0:T(8,128)(2,1)}, u32[]{:S(2)}) copy-start(bf16[128,128]{1,0:T(8,128)(2,1)} %rv.1) | copy-start | bytes 98308
  34.2 38.8 %copy-start.10 = (s32[24,24]{1,0:T(8,128)S(1)}, s32[24,24]{1,0:T(8,128)}, u32[]{:S(2)}) copy-start(s32[24,24]{1,0:T(8,128)} %refs_7_.7) | copy-start | bytes 6916
  73.6 1.6 %collective-permute-start.1 = (bf16[192,384]{1,0:T(8,128)(2,1)S(1)}, bf16[192,384]{1,0:T(8,128)(2,1)S(1)}, u32[]{:S(2)}, u32[]{:S(2)}) collective-permute-start(bf16[192,384]{1,0:T(8,128)(2,1)S(1)} %get-tuple-element.53), channel_id=1, source_target_pairs={{0,16},{16,0},{1,17},{17,1},{2,18},{18,2},{3,19},{19,3},{4,20},{20... | collective-permute-start | bytes 442376 | tf_op jit(solution)/shard_map/ppermute | solution.py:319

commit v6 on v5

--- a/solution.py
+++ b/solution.py
@@ -1,5 +1,3 @@
-import functools
-
 import jax
 import jax.numpy as jnp
 from jax import lax
@@ -84,22 +82,25 @@
     return parts
 
 
-def assemble(scratch, lines, first, spot, store):
+def assemble(scratch, lines, first, spot, store, spots=range(BLOCKS)):
     total = scratch.shape[0] // WIDTH
     lane = lanes(GROUPS)
     order = {spot(c): c for c in range(BLOCKS)}
     for r in range(lines):
-        found = [scratch[pl.ds(c * GROUPS * total + first + r, GROUPS, stride=total), :] for c in range(BLOCKS)]
+        found = {
+            at: scratch[pl.ds(order[at] * GROUPS * total + first + r, GROUPS, stride=total), :] for at in spots
+        }
         for n, i in enumerate(rows_in(r, lines)):
             for t in range(TILES):
                 tile = None
-                for at in range(BLOCKS):
+                for at in spots:
                     begin, end = at * SIDE - t * WIDTH, (at + 1) * SIDE - t * WIDTH
                     if end <= 0 or begin >= WIDTH:
                         continue
-                    piece = roll(found[order[at]], begin - n * SIDE)
+                    piece = roll(found[at], begin - n * SIDE)
                     tile = piece if tile is None else jnp.where(lane >= begin, piece, tile)
-                store(i, t, tile)
+                if tile is not None:
+                    store(i, t, tile)
 
 
 def disassemble(load, scratch, lines, first, blocks):
@@ -161,13 +162,13 @@
     on_core(1, ready, given, made)
 
 
-def assemble_left(in_ref, scratch, panel, lines, spot):
+def assemble_left(in_ref, scratch, panel, lines, spot, spots=range(BLOCKS)):
     scratch[...] = in_ref[...].astype(f32)
 
     def store(i, t, tile):
         panel[i * GROUPS : (i + 1) * GROUPS, columns_of(t)] = tile
 
-    assemble(scratch, lines, 0, spot, store)
+    assemble(scratch, lines, 0, spot, store, spots)
 
 
 def rows_of(panel):
@@ -184,19 +185,25 @@
     disassemble(rows_of(panel), scratch, ALONE, 0, BLOCKS // 2)
 
 
-def mix_own_kernel(left_ref, right_ref, out_ref, panel):
-    half_mixed(left_ref, right_ref, out_ref, panel)
-
-
-def mix_kernel(left_ref, right_ref, own_ref, out_ref, scratch, panel):
+def put_half(scratch, out_ref, own):
+    size = GROUPS * ALONE
+    for core in range(2):
+
+        @pl.when(lax.axis_index("core") == (core if own else 1 - core))
+        def _(core=core):
+            for n in range(BLOCKS // 2):
+                there = (2 * n + core) * size
+                out_ref[there : there + size, :] = scratch[n * size : (n + 1) * size, :].astype(bf16)
+
+
+def mix_own_kernel(left_ref, right_ref, out_ref, scratch, panel):
     half_mixed(left_ref, right_ref, scratch, panel)
-    first = lax.axis_index("core") == 0
-    size = GROUPS * ALONE
-    for n in range(BLOCKS // 2):
-        here = slice(n * size, (n + 1) * size)
-        own, other = own_ref[here, :], scratch[here, :]
-        out_ref[2 * n * size : (2 * n + 1) * size, :] = jnp.where(first, own, other).astype(bf16)
-        out_ref[(2 * n + 1) * size : (2 * n + 2) * size, :] = jnp.where(first, other, own).astype(bf16)
+    put_half(scratch, out_ref, True)
+
+
+def mix_kernel(_, left_ref, right_ref, out_ref, scratch, panel):
+    half_mixed(left_ref, right_ref, scratch, panel)
+    put_half(scratch, out_ref, False)
 
 
 def ready(given, grad_ref, factor_ref):
@@ -214,31 +221,54 @@
         work(given, *made)
 
 
-def later_kernel(work, count, *refs):
-    on_core(0, work, refs[count:-count], refs[-count:])
-
-
-def middle_kernel(in_ref, grad_ref, factor_ref, weight_ref, out_ref, grad_gate_ref, scratch):
+def ready_later_kernel(*refs):
+    on_core(0, ready, refs[2:-2], refs[-2:])
+
+
+def middle_kernel(in_ref, grad_ref, out_ref, normed_ref, scratch):
     (mixed,) = from_messages(in_ref, scratch, 1)
     centred = mixed - jnp.mean(mixed, axis=-1, keepdims=True)
     mix_scale = lax.rsqrt(jnp.mean(centred * centred, axis=-1, keepdims=True) + epsilon)
     mix_normed = centred * mix_scale
-    out_lin = dot(mix_normed.astype(bf16), weight_ref[...])
-    grad_gate_ref[...] = (factor_ref[...] * out_lin).astype(bf16)
+    normed_ref[...] = mix_normed.astype(bf16)
     grad_mix = layer_back(grad_ref[...], mix_normed, mix_scale)
     out_ref[...] = to_messages([grad_mix], scratch)
 
 
-def right_grad_kernel(in_ref, left_ref, *refs):
-    given, (grad_ref, own_ref, sent_ref), made, (scratch, panel) = refs[:10], refs[10:13], refs[13:17], refs[17:]
+def right_grad_all(in_ref, left_ref, grad_ref, own_ref, scratch, panel):
     assemble_left(in_ref, scratch, panel, ALONE, place)
     grad = panel[...]
     grad_ref[...] = grad.astype(bf16)
     first = lax.axis_index("core") == 0
     sums = dot(jnp.transpose(grad).astype(bf16), left_ref[...])
     own_ref[...] = jnp.where(first, sums[:HALF], sums[HALF:])
-    sent_ref[...] = jnp.where(first, sums[HALF:], sums[:HALF]).astype(bf16)
-    on_core(1, prepare, given, made)
+    return jnp.where(first, sums[HALF:], sums[:HALF])
+
+
+def right_grad_kernel(in_ref, left_ref, *refs):
+    given, (grad_ref, own_ref, sent_ref), made, (scratch, panel) = refs[:12], refs[12:15], refs[15:19], refs[19:]
+    core = lax.axis_index("core")
+
+    @pl.when(core == 0)
+    def _():
+        assemble_left(in_ref, scratch, panel, ALONE, place, range(BLOCKS // 2, BLOCKS))
+        turned = jnp.transpose(panel[:, WIDTH:])[HALF - WIDTH :]
+        sent_ref[...] = dot(turned.astype(bf16), left_ref[...]).astype(bf16)
+
+    @pl.when(core == 1)
+    def _():
+        sent_ref[...] = right_grad_all(in_ref, left_ref, grad_ref, own_ref, scratch, panel).astype(bf16)
+        prepare(given, *made)
+
+
+def right_grad_later_kernel(*refs):
+    in_ref, left_ref, *given = refs[6:20]
+    (grad_ref, own_ref), made, (scratch, panel) = refs[20:22], refs[22:26], refs[26:]
+
+    @pl.when(lax.axis_index("core") == 0)
+    def _():
+        right_grad_all(in_ref, left_ref, grad_ref, own_ref, scratch, panel)
+        prepare(given, *made)
 
 
 def left_grad_kernel(grad_ref, own_ref, other_ref, out_ref, right, panel):
@@ -261,11 +291,12 @@
 
 
 def prepare(given, normed_ref, scaled_ref, base_ref, factors_ref):
-    pair_ref, mean_ref, scale_ref, mask_ref, grad_gate_ref, lg, lv, rg, rv, og = given
+    pair_ref, mean_ref, scale_ref, mask_ref, mix_normed_ref, factor_ref, weight_ref, lg, lv, rg, rv, og = given
     normed, scale = normalise(pair_ref, mean_ref, scale_ref)
     normed_ref[...] = normed
     scaled_ref[...] = scale
-    base_ref[...] = dot(grad_gate_ref[...], og[...], ((1,), (1,)))
+    grad_gate = factor_ref[...] * dot(mix_normed_ref[...], weight_ref[...])
+    base_ref[...] = dot(grad_gate.astype(bf16), og[...], ((1,), (1,)))
     low = normed.astype(bf16)
     keep = spread_pairs(mask_ref[...].astype(f32))
     for n, (gate, value) in enumerate(((lg, lv), (rg, rv))):
@@ -360,21 +391,23 @@
     (left,) = call(take_left_kernel, [panel], came, scratch=[line_two, panel_left], name="take_left")
     line_half, panel_half = pltpu.VMEM((WIDTH * ALONE // 2, WIDTH), f32), pltpu.VMEM((HALF, 2 * WIDTH), f32)
     (mixed_own,) = call(
-        mix_own_kernel, [((WIDTH * ALONE // 2, WIDTH), f32)], left, right_own, scratch=[panel_half], name="mix_own",
+        mix_own_kernel, [one], left, right_own, scratch=[line_half, panel_half], name="mix_own",
     )
     grad_mixnorm, factor = call(
-        functools.partial(later_kernel, ready, 2), [many, many], *made, *given, name="ready", aliases={0: 0, 1: 1}
+        ready_later_kernel, [many, many], *made, *given, name="ready", aliases={0: 0, 1: 1}
     )
     mixed_own, grad_mixnorm, factor = lax.optimization_barrier((mixed_own, grad_mixnorm, factor))
-    (sent,) = call(mix_kernel, [one], left, right_other, mixed_own, scratch=[line_half, panel_half], name="mix")
+    (sent,) = call(
+        mix_kernel, [one], mixed_own, left, right_other, scratch=[line_half, panel_half], name="mix", aliases={0: 0}
+    )
     came = spread(sent)
-    sent, grad_gate = call(
-        middle_kernel, [one, ((PAIRS, WIDTH), bf16)], came, grad_mixnorm, factor, output_weight, scratch=[line_one],
-        name="middle",
+    sent, mix_normed = call(
+        middle_kernel, [one, ((PAIRS, WIDTH), bf16)], came, grad_mixnorm, scratch=[line_one], name="middle"
     )
     came = spread(sent)
     given = [
-        pair, norm_mean, norm_scale, pair_mask, grad_gate, left_gate, left_value, right_gate, right_value, output_gate
+        pair, norm_mean, norm_scale, pair_mask, mix_normed, factor, output_weight, left_gate, left_value, right_gate,
+        right_value, output_gate,
     ]
     factors = ((4, PAIRS, WIDTH), f32)
     grad, own, sent, *made = call(
@@ -383,13 +416,13 @@
     )
     other = swap(sent)
     lined = ((WIDTH * 2 * PAIRED, WIDTH), f32)
+    grad, own, *prepared = call(
+        right_grad_later_kernel, [panel, wide, many, many, many, factors], grad, own, *made, came, left, *given,
+        scratch=[line_one, panel_left], name="right_grad_later", aliases={n: n for n in range(6)},
+    )
     (lines,) = call(
         left_grad_kernel, [lined], grad, right_own, right_other,
         scratch=[pltpu.VMEM((2, HALF, TOKENS), bf16), panel_left], name="left_grad",
-    )
-    prepared = call(
-        functools.partial(later_kernel, prepare, 4), [many, many, many, factors], *made, *given, name="prepare",
-        aliases={n: n for n in range(4)},
     )
     lines, prepared = lax.optimization_barrier((lines, prepared))
     _, sent = call(return_kernel, [lined, two], lines, own, other, scratch=[panels_out], name="return", aliases={0: 0})

time: 99.6 us -> 99.5 us (level)
  no operation moved by 1% of the time
where the time goes in v6:
time: 99.5 us; the launch traced here: 99.3 us
  blocking collectives  90 us (90%)
  Pallas kernels  8.67 us (9%)
    all_to_all x4, blocking collectives, spread(): lax.all_to_all(paired, SPREAD, 0, 0, tiled=True).reshape(messages.shape)  90 us
    pallas_call x12, Pallas kernels, call(): pl.pallas_call(kernel, out_shape=[jax.ShapeDtypeStruct(shape, dtype) for...  8.67 us
  transfers between devices with their start and end apart: 2, of which 0 were waited for; matrix products, arithmetic and copies ran while one was open for 0% of the time, Pallas kernels for 3%

profile of v6, /device:TPU:32, one launch (start us, length us, event | category | flops | bytes accessed | tf_op | source)
XLA Modules:
  0.0 99.3 jit_solution(5457225293350684087)
XLA Ops:
  0.0 1.8 %edges.1 = bf16[1280,128]{1,0:T(8,128)(2,1)S(1)} custom-call(bf16[576,128]{1,0:T(8,128)(2,1)} %bitcast.11, f32[24,24]{1,0:T(8,128)} %refs_9_.3, f32[24,24]{1,0:T(8,128)} %refs_10_.3, s32[24,24]{1,0:T(8,128)} %refs_11_.3, bf16[128,128]{1,0:T(8,128)(2,1)} %lg.1, bf16[128,128]{1,0:T(8,128)(2,1)} %lv.1, bf16[128,128]{1,0:T(8,128)(2,1)} %rg.1, bf16[128,128]{1,0:T(8,128)(2,1)} %rv.1), custom_call_target="tpu_custom_call" | custom-call | tf_op jit(solution)/shard_map/edges/pallas_call | solution.py:332
  1.8 30.6 %all_to_all.20 = bf16[128,5,2,128]{3,2,1,0:T(2,128)(2,1)S(1)} all-to-all(bf16[128,5,2,128]{3,2,1,0:T(2,128)(2,1)S(1)} %bitcast.21), channel_id=1, replica_groups=mesh['z_lo'=2,'x'=4,'core'=2,'z_hi'=4,'y'=4] {'z_hi','y','z_lo','x'}, dimensions={0} | all-to-all | bytes 655360 | tf_op jit(solution)/shard_map/all_to_all | solution.py:346
  32.4 0.3 take_right.1
  32.7 0.1 collective-permute-start
  32.8 0.3 take_left.1.left_ref.refs_7_
  33.1 0.5 mix_own.1._
  33.6 0.6 ready.1
  34.2 0.0 copy-start.4
  34.2 0.0 copy-start.5
  34.3 0.0 copy-start.10
  34.3 0.0 collective-permute-done.right_ref.other_ref
  34.3 0.5 mix.1
  34.8 19.5 %all_to_all.21 = bf16[128,3,2,128]{3,2,1,0:T(2,128)(2,1)S(1)} all-to-all(bf16[128,3,2,128]{3,2,1,0:T(2,128)(2,1)S(1)} %bitcast.20), channel_id=1, replica_groups=mesh['z_lo'=2,'x'=4,'core'=2,'z_hi'=4,'y'=4] {'z_hi','y','z_lo','x'}, dimensions={0} | all-to-all | bytes 393216 | tf_op jit(solution)/shard_map/all_to_all | solution.py:346
  54.2 0.6 middle.1
  54.9 18.1 %all_to_all.22 = bf16[128,3,2,128]{3,2,1,0:T(2,128)(2,1)S(1)} all-to-all(bf16[128,3,2,128]{3,2,1,0:T(2,128)(2,1)S(1)} %bitcast.27), channel_id=1, replica_groups=mesh['z_lo'=2,'x'=4,'core'=2,'z_hi'=4,'y'=4] {'z_hi','y','z_lo','x'}, dimensions={0} | all-to-all | bytes 393216 | tf_op jit(solution)/shard_map/all_to_all | solution.py:346
  73.0 0.0 copy-done.4
  73.0 0.5 right_grad.1
  73.5 0.1 collective-permute-start.1
  73.6 1.2 %right_grad_later.1 = (bf16[192,384]{1,0:T(8,128)(2,1)S(1)}, f32[192,384]{1,0:T(8,128)S(1)}, f32[576,128]{1,0:T(8,128)S(1)}, f32[576,128]{1,0:T(8,128)S(1)}, f32...) custom-call(bf16[192,384]{1,0:T(8,128)(2,1)S(1)} %get-tuple-element., ...), custom_call_target="tpu_custom_call", output_to_operand_aliasing={{0}: (0, {}), {1}: (1, {}), {2}: (2, {}), {3}: (3, {}), {4}... | custom-call | tf_op jit(solution)/shard_map/right_grad_later/pallas_call | solution.py:332
  74.8 0.7 left_grad.1.lines_ref
  75.5 0.0 collective-permute-done.1.other_ref
  75.5 0.6 return.1
  76.1 21.8 %all_to_all.23 = bf16[128,5,2,128]{3,2,1,0:T(2,128)(2,1)S(1)} all-to-all(bf16[128,5,2,128]{3,2,1,0:T(2,128)(2,1)S(1)} %bitcast.26), channel_id=1, replica_groups=mesh['z_lo'=2,'x'=4,'core'=2,'z_hi'=4,'y'=4] {'z_hi','y','z_lo','x'}, dimensions={0} | all-to-all | bytes 655360 | tf_op jit(solution)/shard_map/all_to_all | solution.py:346
  97.9 1.2 %last.1 = f32[576,128]{1,0:T(8,128)} custom-call(bf16[1280,128]{1,0:T(8,128)(2,1)S(1)} %bitcast.22, f32[576,128]{1,0:T(8,128)S(1)} %get-tuple-element.59.normed_ref, f32[576,128]{1,0:T(8,128)S(1)} %get-tuple-element.60.scale_ref, f32[576,128]{1,0:T(8,128)S(1)} %get-tuple-element.61.base_ref, f32[4,576,128]{2,1,0:T(8,128)S(1)} %get-tuple-element.62.factors_ref, ...), custom_call_target="tpu_custom_call" | custom-call | tf_op jit(solution)/shard_map/last/pallas_call | solution.py:332
  (18 shorter events, 0.0 us)
Async XLA Ops:
  0.0 32.4 %copy-start.9 = (f32[24,24]{1,0:T(8,128)S(1)}, f32[24,24]{1,0:T(8,128)}, u32[]{:S(2)}) copy-start(f32[24,24]{1,0:T(8,128)} %refs_10_.3) | copy-start | bytes 6916
  0.0 32.4 %copy-start.8 = (f32[24,24]{1,0:T(8,128)S(1)}, f32[24,24]{1,0:T(8,128)}, u32[]{:S(2)}) copy-start(f32[24,24]{1,0:T(8,128)} %refs_9_.3) | copy-start | bytes 6916
  0.0 32.4 %copy-start = (bf16[24,24,128]{2,1,0:T(8,128)(2,1)S(1)}, bf16[24,24,128]{2,1,0:T(8,128)(2,1)}, u32[]{:S(2)}) copy-start(bf16[24,24,128]{2,1,0:T(8,128)(2,1)} %param.11) | copy-start | bytes 442372
  0.0 32.4 %copy-start.7 = (bf16[128,128]{1,0:T(8,128)(2,1)S(1)}, bf16[128,128]{1,0:T(8,128)(2,1)}, u32[]{:S(2)}) copy-start(bf16[128,128]{1,0:T(8,128)(2,1)} %refs_14_.1) | copy-start | bytes 98308
  0.0 32.4 %copy-start.6 = (bf16[128,128]{1,0:T(8,128)(2,1)S(1)}, bf16[128,128]{1,0:T(8,128)(2,1)}, u32[]{:S(2)}) copy-start(bf16[128,128]{1,0:T(8,128)(2,1)} %refs_19_.1) | copy-start | bytes 98308
  0.0 32.4 %copy-start.1 = (bf16[24,24,128]{2,1,0:T(8,128)(2,1)S(1)}, bf16[24,24,128]{2,1,0:T(8,128)(2,1)}, u32[]{:S(2)}) copy-start(bf16[24,24,128]{2,1,0:T(8,128)(2,1)} %param.15) | copy-start | bytes 442372
  32.7 1.5 %collective-permute-start = (bf16[192,384]{1,0:T(8,128)(2,1)S(1)}, bf16[192,384]{1,0:T(8,128)(2,1)S(1)}, u32[]{:S(2)}, u32[]{:S(2)}) collective-permute-start(bf16[192,384]{1,0:T(8,128)(2,1)S(1)} %get-tuple-element.34.right_ref.own_ref), channel_id=1, source_target_pairs={{0,16},{16,0},{1,17},{17,1},{2,18},{18,2},{3,19},{19,3},{4,20},{20... | collective-permute-start | bytes 442376 | tf_op jit(solution)/shard_map/ppermute | solution.py:350
  34.2 38.8 %copy-start.2 = (bf16[128,128]{1,0:T(8,128)(2,1)S(1)}, bf16[128,128]{1,0:T(8,128)(2,1)}, u32[]{:S(2)}) copy-start(bf16[128,128]{1,0:T(8,128)(2,1)} %lg.1) | copy-start | bytes 98308
  34.2 38.8 %copy-start.3 = (bf16[128,128]{1,0:T(8,128)(2,1)S(1)}, bf16[128,128]{1,0:T(8,128)(2,1)}, u32[]{:S(2)}) copy-start(bf16[128,128]{1,0:T(8,128)(2,1)} %lv.1) | copy-start | bytes 98308
  34.2 38.8 %copy-start.4 = (bf16[128,128]{1,0:T(8,128)(2,1)S(1)}, bf16[128,128]{1,0:T(8,128)(2,1)}, u32[]{:S(2)}) copy-start(bf16[128,128]{1,0:T(8,128)(2,1)} %rg.1) | copy-start | bytes 98308
  34.2 38.8 %copy-start.5 = (bf16[128,128]{1,0:T(8,128)(2,1)S(1)}, bf16[128,128]{1,0:T(8,128)(2,1)}, u32[]{:S(2)}) copy-start(bf16[128,128]{1,0:T(8,128)(2,1)} %rv.1) | copy-start | bytes 98308
  34.3 38.8 %copy-start.10 = (s32[24,24]{1,0:T(8,128)S(1)}, s32[24,24]{1,0:T(8,128)}, u32[]{:S(2)}) copy-start(s32[24,24]{1,0:T(8,128)} %refs_11_.3) | copy-start | bytes 6916
  73.5 2.0 %collective-permute-start.1 = (bf16[192,384]{1,0:T(8,128)(2,1)S(1)}, bf16[192,384]{1,0:T(8,128)(2,1)S(1)}, u32[]{:S(2)}, u32[]{:S(2)}) collective-permute-start(bf16[192,384]{1,0:T(8,128)(2,1)S(1)} %get-tuple-element.57), channel_id=1, source_target_pairs={{0,16},{16,0},{1,17},{17,1},{2,18},{18,2},{3,19},{19,3},{4,20},{20... | collective-permute-start | bytes 442376 | tf_op jit(solution)/shard_map/ppermute | solution.py:350

commit v7 on v6

--- a/solution.py
+++ b/solution.py
@@ -159,7 +159,7 @@
     for group in range(GROUPS):
         rows = [panels[t, pl.ds(group, SIDE, stride=GROUPS + 1), :] for t in range(TILES)]
         out_ref[group * SIDE : (group + 1) * SIDE, :] = jnp.concatenate(rows, axis=1).astype(bf16)
-    on_core(1, ready, given, made)
+    on_core(1, lambda: ready(given, *made))
 
 
 def assemble_left(in_ref, scratch, panel, lines, spot, spots=range(BLOCKS)):
@@ -185,25 +185,22 @@
     disassemble(rows_of(panel), scratch, ALONE, 0, BLOCKS // 2)
 
 
-def put_half(scratch, out_ref, own):
+def mix_own_kernel(left_ref, right_ref, out_ref, scratch, panel):
+    half_mixed(left_ref, right_ref, scratch, panel)
+    out_ref[...] = scratch[...].astype(bf16)
+
+
+def mix_kernel(own_ref, left_ref, right_ref, out_ref, scratch, panel):
+    half_mixed(left_ref, right_ref, scratch, panel)
     size = GROUPS * ALONE
     for core in range(2):
 
-        @pl.when(lax.axis_index("core") == (core if own else 1 - core))
+        @pl.when(lax.axis_index("core") == core)
         def _(core=core):
             for n in range(BLOCKS // 2):
-                there = (2 * n + core) * size
-                out_ref[there : there + size, :] = scratch[n * size : (n + 1) * size, :].astype(bf16)
-
-
-def mix_own_kernel(left_ref, right_ref, out_ref, scratch, panel):
-    half_mixed(left_ref, right_ref, scratch, panel)
-    put_half(scratch, out_ref, True)
-
-
-def mix_kernel(_, left_ref, right_ref, out_ref, scratch, panel):
-    half_mixed(left_ref, right_ref, scratch, panel)
-    put_half(scratch, out_ref, False)
+                here, mine, other = (slice(at * size, (at + 1) * size) for at in (n, 2 * n + core, 2 * n + 1 - core))
+                out_ref[mine, :] = own_ref[here, :]
+                out_ref[other, :] = scratch[here, :].astype(bf16)
 
 
 def ready(given, grad_ref, factor_ref):
@@ -215,14 +212,22 @@
     factor_ref[...] = grad_y * (1.0 - out_sig)
 
 
-def on_core(core, work, given, made):
-    @pl.when(lax.axis_index("core") == core)
-    def _():
-        work(given, *made)
+def on_core(core, work):
+    pl.when(lax.axis_index("core") == core)(work)
+
+
+def hand_on(early, made):
+    def work():
+        for a, b in zip(early, made):
+            b[...] = a[...]
+
+    on_core(1, work)
 
 
 def ready_later_kernel(*refs):
-    on_core(0, ready, refs[2:-2], refs[-2:])
+    early, given, made = refs[:2], refs[2:-2], refs[-2:]
+    hand_on(early, made)
+    on_core(0, lambda: ready(given, *made))
 
 
 def middle_kernel(in_ref, grad_ref, out_ref, normed_ref, scratch):
@@ -247,28 +252,29 @@
 
 def right_grad_kernel(in_ref, left_ref, *refs):
     given, (grad_ref, own_ref, sent_ref), made, (scratch, panel) = refs[:12], refs[12:15], refs[15:19], refs[19:]
-    core = lax.axis_index("core")
-
-    @pl.when(core == 0)
-    def _():
+
+    def only_sent():
         assemble_left(in_ref, scratch, panel, ALONE, place, range(BLOCKS // 2, BLOCKS))
         turned = jnp.transpose(panel[:, WIDTH:])[HALF - WIDTH :]
         sent_ref[...] = dot(turned.astype(bf16), left_ref[...]).astype(bf16)
 
-    @pl.when(core == 1)
-    def _():
+    def everything():
         sent_ref[...] = right_grad_all(in_ref, left_ref, grad_ref, own_ref, scratch, panel).astype(bf16)
         prepare(given, *made)
 
+    on_core(0, only_sent)
+    on_core(1, everything)
+
 
 def right_grad_later_kernel(*refs):
-    in_ref, left_ref, *given = refs[6:20]
-    (grad_ref, own_ref), made, (scratch, panel) = refs[20:22], refs[22:26], refs[26:]
-
-    @pl.when(lax.axis_index("core") == 0)
-    def _():
-        right_grad_all(in_ref, left_ref, grad_ref, own_ref, scratch, panel)
-        prepare(given, *made)
+    early, (in_ref, left_ref, *given), made, (scratch, panel) = refs[:6], refs[6:20], refs[20:26], refs[26:]
+    hand_on(early, made)
+
+    def everything():
+        right_grad_all(in_ref, left_ref, *made[:2], scratch, panel)
+        prepare(given, *made[2:])
+
+    on_core(0, everything)
 
 
 def left_grad_kernel(grad_ref, own_ref, other_ref, out_ref, right, panel):
@@ -279,15 +285,19 @@
     disassemble(rows_of(panel), out_ref, PAIRED, 0, BLOCKS)
 
 
-def return_kernel(lines_ref, own_ref, other_ref, kept_ref, out_ref, panels):
+def return_kernel(lines_ref, own_ref, other_ref, out_ref, scratch, panels):
     for group in range(GROUPS):
         here = slice(group * SIDE, (group + 1) * SIDE)
         total = own_ref[here, :] + other_ref[here, :].astype(f32)
         for t in range(TILES):
             panels[t, pl.ds(group * (SIDE + 1), SIDE), :] = total[:, columns_of(t)]
     load = lambda i, t: panels[t, pl.ds(i, GROUPS, stride=SIDE + 1), :]
-    disassemble(load, kept_ref, PAIRED, PAIRED, BLOCKS)
-    out_ref[...] = kept_ref[...].astype(bf16)
+    disassemble(load, scratch, PAIRED, PAIRED, BLOCKS)
+    size = GROUPS * 2 * PAIRED
+    is_left = lax.broadcasted_iota(jnp.int32, (size, WIDTH), 0) % (2 * PAIRED) < PAIRED
+    for c in range(BLOCKS):
+        here = slice(c * size, (c + 1) * size)
+        out_ref[here, :] = jnp.where(is_left, lines_ref[here, :], scratch[here, :]).astype(bf16)
 
 
 def prepare(given, normed_ref, scaled_ref, base_ref, factors_ref):
@@ -328,14 +338,13 @@
         copy.wait()
 
 
-def call(kernel, outs, *args, scratch=(), name=None, space=VMEM, aliases={}, out_space=VMEM):
+def call(kernel, outs, *args, scratch=(), name=None, space=VMEM, out_space=VMEM):
     return pl.pallas_call(
         kernel,
         out_shape=[jax.ShapeDtypeStruct(shape, dtype) for shape, dtype in outs],
         in_specs=[space for _ in args],
         out_specs=[out_space for _ in outs],
         scratch_shapes=list(scratch),
-        input_output_aliases=aliases,
         compiler_params=pltpu.CompilerParams(vmem_limit_bytes=48 * 1024 * 1024),
         name=name,
     )(*args)
@@ -391,14 +400,14 @@
     (left,) = call(take_left_kernel, [panel], came, scratch=[line_two, panel_left], name="take_left")
     line_half, panel_half = pltpu.VMEM((WIDTH * ALONE // 2, WIDTH), f32), pltpu.VMEM((HALF, 2 * WIDTH), f32)
     (mixed_own,) = call(
-        mix_own_kernel, [one], left, right_own, scratch=[line_half, panel_half], name="mix_own",
+        mix_own_kernel, [((WIDTH * ALONE // 2, WIDTH), bf16)], left, right_own, scratch=[line_half, panel_half], name="mix_own",
     )
     grad_mixnorm, factor = call(
-        ready_later_kernel, [many, many], *made, *given, name="ready", aliases={0: 0, 1: 1}
+        ready_later_kernel, [many, many], *made, *given, name="ready"
     )
     mixed_own, grad_mixnorm, factor = lax.optimization_barrier((mixed_own, grad_mixnorm, factor))
     (sent,) = call(
-        mix_kernel, [one], mixed_own, left, right_other, scratch=[line_half, panel_half], name="mix", aliases={0: 0}
+        mix_kernel, [one], mixed_own, left, right_other, scratch=[line_half, panel_half], name="mix"
     )
     came = spread(sent)
     sent, mix_normed = call(
@@ -418,14 +427,14 @@
     lined = ((WIDTH * 2 * PAIRED, WIDTH), f32)
     grad, own, *prepared = call(
         right_grad_later_kernel, [panel, wide, many, many, many, factors], grad, own, *made, came, left, *given,
-        scratch=[line_one, panel_left], name="right_grad_later", aliases={n: n for n in range(6)},
+        scratch=[line_one, panel_left], name="right_grad_later",
     )
     (lines,) = call(
         left_grad_kernel, [lined], grad, right_own, right_other,
         scratch=[pltpu.VMEM((2, HALF, TOKENS), bf16), panel_left], name="left_grad",
     )
     lines, prepared = lax.optimization_barrier((lines, prepared))
-    _, sent = call(return_kernel, [lined, two], lines, own, other, scratch=[panels_out], name="return", aliases={0: 0})
+    (sent,) = call(return_kernel, [two], lines, own, other, scratch=[line_two, panels_out], name="return")
     came = spread(sent)
     (out,) = call(
         last_kernel, [many], came, *prepared, left_gate, left_value, right_gate, right_value,

time: 99.5 us -> 99.6 us (level)
  no operation moved by 1% of the time
where the time goes in v7:
time: 99.6 us; the launch traced here: 99.3 us
  blocking collectives  90.1 us (90%)
  Pallas kernels  8.67 us (9%)
    all_to_all x4, blocking collectives, spread(): lax.all_to_all(paired, SPREAD, 0, 0, tiled=True).reshape(messages.shape)  90.1 us
    pallas_call x12, Pallas kernels, call(): pl.pallas_call(kernel, out_shape=[jax.ShapeDtypeStruct(shape, dtype) for...  8.67 us
  transfers between devices with their start and end apart: 2, of which 0 were waited for; matrix products, arithmetic and copies ran while one was open for 0% of the time, Pallas kernels for 3%

profile of v7, /device:TPU:32, one launch (start us, length us, event | category | flops | bytes accessed | tf_op | source)
XLA Modules:
  0.0 99.3 jit_solution(3020236947691287947)
XLA Ops:
  0.0 0.0 copy-start.7
  0.0 1.8 %edges.1 = bf16[1280,128]{1,0:T(8,128)(2,1)S(1)} custom-call(bf16[576,128]{1,0:T(8,128)(2,1)} %bitcast.11, f32[24,24]{1,0:T(8,128)} %refs_9_.3, f32[24,24]{1,0:T(8,128)} %refs_10_.3, s32[24,24]{1,0:T(8,128)} %refs_11_.3, bf16[128,128]{1,0:T(8,128)(2,1)} %lg.1, bf16[128,128]{1,0:T(8,128)(2,1)} %lv.1, bf16[128,128]{1,0:T(8,128)(2,1)} %rg.1, bf16[128,128]{1,0:T(8,128)(2,1)} %rv.1), custom_call_target="tpu_custom_call" | custom-call | tf_op jit(solution)/shard_map/edges/pallas_call | solution.py:342
  1.8 30.6 %all_to_all.20 = bf16[128,5,2,128]{3,2,1,0:T(2,128)(2,1)S(1)} all-to-all(bf16[128,5,2,128]{3,2,1,0:T(2,128)(2,1)S(1)} %bitcast.20), channel_id=1, replica_groups=mesh['z_lo'=2,'x'=4,'core'=2,'z_hi'=4,'y'=4] {'z_hi','y','z_lo','x'}, dimensions={0} | all-to-all | bytes 655360 | tf_op jit(solution)/shard_map/all_to_all | solution.py:355
  32.4 0.3 take_right.1
  32.7 0.1 collective-permute-start
  32.8 0.3 take_left.1.left_ref.refs_7_
  33.1 0.5 mix_own.1.own_ref
  33.6 0.6 ready.1
  34.2 0.0 copy-start.4
  34.2 0.0 copy-start.5
  34.3 0.0 copy-start.10
  34.3 0.0 collective-permute-done.right_ref.other_ref
  34.3 0.5 mix.1
  34.8 19.5 %all_to_all.21 = bf16[128,3,2,128]{3,2,1,0:T(2,128)(2,1)S(1)} all-to-all(bf16[128,3,2,128]{3,2,1,0:T(2,128)(2,1)S(1)} %bitcast.24), channel_id=1, replica_groups=mesh['z_lo'=2,'x'=4,'core'=2,'z_hi'=4,'y'=4] {'z_hi','y','z_lo','x'}, dimensions={0} | all-to-all | bytes 393216 | tf_op jit(solution)/shard_map/all_to_all | solution.py:355
  54.2 0.6 middle.1
  54.9 18.1 %all_to_all.22 = bf16[128,3,2,128]{3,2,1,0:T(2,128)(2,1)S(1)} all-to-all(bf16[128,3,2,128]{3,2,1,0:T(2,128)(2,1)S(1)} %bitcast.27), channel_id=1, replica_groups=mesh['z_lo'=2,'x'=4,'core'=2,'z_hi'=4,'y'=4] {'z_hi','y','z_lo','x'}, dimensions={0} | all-to-all | bytes 393216 | tf_op jit(solution)/shard_map/all_to_all | solution.py:355
  73.0 0.5 right_grad.1
  73.5 0.1 collective-permute-start.1
  73.6 1.2 %right_grad_later.1 = (bf16[192,384]{1,0:T(8,128)(2,1)S(1)}, f32[192,384]{1,0:T(8,128)S(1)}, f32[576,128]{1,0:T(8,128)S(1)}, f32[576,128]{1,0:T(8,128)S(1)}, f32...) custom-call(bf16[192,384]{1,0:T(8,128)(2,1)S(1)} %get-tuple-element.43.refs_0_, ...), custom_call_target="tpu_custom_call" | custom-call | tf_op jit(solution)/shard_map/right_grad_later/pallas_call | solution.py:342
  74.8 0.7 left_grad.1.lines_ref
  75.5 0.0 collective-permute-done.1.other_ref
  75.5 0.6 return.1
  76.1 21.9 %all_to_all.23 = bf16[128,5,2,128]{3,2,1,0:T(2,128)(2,1)S(1)} all-to-all(bf16[128,5,2,128]{3,2,1,0:T(2,128)(2,1)S(1)} %bitcast.21), channel_id=1, replica_groups=mesh['z_lo'=2,'x'=4,'core'=2,'z_hi'=4,'y'=4] {'z_hi','y','z_lo','x'}, dimensions={0} | all-to-all | bytes 655360 | tf_op jit(solution)/shard_map/all_to_all | solution.py:355
  98.0 1.2 %last.1 = f32[576,128]{1,0:T(8,128)} custom-call(bf16[1280,128]{1,0:T(8,128)(2,1)S(1)} %bitcast.22, f32[576,128]{1,0:T(8,128)S(1)} %get-tuple-element.57.normed_ref, f32[576,128]{1,0:T(8,128)S(1)} %get-tuple-element.58.scale_ref, f32[576,128]{1,0:T(8,128)S(1)} %get-tuple-element.59.base_ref, f32[4,576,128]{2,1,0:T(8,128)S(1)} %get-tuple-element.60.factors_ref, ...), custom_call_target="tpu_custom_call" | custom-call | tf_op jit(solution)/shard_map/last/pallas_call | solution.py:342
  (18 shorter events, 0.0 us)
Async XLA Ops:
  0.0 32.4 %copy-start.9 = (f32[24,24]{1,0:T(8,128)S(1)}, f32[24,24]{1,0:T(8,128)}, u32[]{:S(2)}) copy-start(f32[24,24]{1,0:T(8,128)} %refs_10_.3) | copy-start | bytes 6916
  0.0 32.4 %copy-start.8 = (f32[24,24]{1,0:T(8,128)S(1)}, f32[24,24]{1,0:T(8,128)}, u32[]{:S(2)}) copy-start(f32[24,24]{1,0:T(8,128)} %refs_9_.3) | copy-start | bytes 6916
  0.0 32.4 %copy-start = (bf16[24,24,128]{2,1,0:T(8,128)(2,1)S(1)}, bf16[24,24,128]{2,1,0:T(8,128)(2,1)}, u32[]{:S(2)}) copy-start(bf16[24,24,128]{2,1,0:T(8,128)(2,1)} %param.11) | copy-start | bytes 442372
  0.0 32.4 %copy-start.7 = (bf16[128,128]{1,0:T(8,128)(2,1)S(1)}, bf16[128,128]{1,0:T(8,128)(2,1)}, u32[]{:S(2)}) copy-start(bf16[128,128]{1,0:T(8,128)(2,1)} %refs_14_.1) | copy-start | bytes 98308
  0.0 32.4 %copy-start.6 = (bf16[128,128]{1,0:T(8,128)(2,1)S(1)}, bf16[128,128]{1,0:T(8,128)(2,1)}, u32[]{:S(2)}) copy-start(bf16[128,128]{1,0:T(8,128)(2,1)} %refs_19_.1) | copy-start | bytes 98308
  0.0 32.4 %copy-start.1 = (bf16[24,24,128]{2,1,0:T(8,128)(2,1)S(1)}, bf16[24,24,128]{2,1,0:T(8,128)(2,1)}, u32[]{:S(2)}) copy-start(bf16[24,24,128]{2,1,0:T(8,128)(2,1)} %param.15) | copy-start | bytes 442372
  32.7 1.5 %collective-permute-start = (bf16[192,384]{1,0:T(8,128)(2,1)S(1)}, bf16[192,384]{1,0:T(8,128)(2,1)S(1)}, u32[]{:S(2)}, u32[]{:S(2)}) collective-permute-start(bf16[192,384]{1,0:T(8,128)(2,1)S(1)} %get-tuple-element.33.right_ref.own_ref), channel_id=1, source_target_pairs={{0,16},{16,0},{1,17},{17,1},{2,18},{18,2},{3,19},{19,3},{4,20},{20... | collective-permute-start | bytes 442376 | tf_op jit(solution)/shard_map/ppermute | solution.py:359
  34.2 38.8 %copy-start.2 = (bf16[128,128]{1,0:T(8,128)(2,1)S(1)}, bf16[128,128]{1,0:T(8,128)(2,1)}, u32[]{:S(2)}) copy-start(bf16[128,128]{1,0:T(8,128)(2,1)} %lg.1) | copy-start | bytes 98308
  34.2 38.8 %copy-start.3 = (bf16[128,128]{1,0:T(8,128)(2,1)S(1)}, bf16[128,128]{1,0:T(8,128)(2,1)}, u32[]{:S(2)}) copy-start(bf16[128,128]{1,0:T(8,128)(2,1)} %lv.1) | copy-start | bytes 98308
  34.2 38.8 %copy-start.4 = (bf16[128,128]{1,0:T(8,128)(2,1)S(1)}, bf16[128,128]{1,0:T(8,128)(2,1)}, u32[]{:S(2)}) copy-start(bf16[128,128]{1,0:T(8,128)(2,1)} %rg.1) | copy-start | bytes 98308
  34.2 38.8 %copy-start.5 = (bf16[128,128]{1,0:T(8,128)(2,1)S(1)}, bf16[128,128]{1,0:T(8,128)(2,1)}, u32[]{:S(2)}) copy-start(bf16[128,128]{1,0:T(8,128)(2,1)} %rv.1) | copy-start | bytes 98308
  34.3 38.8 %copy-start.10 = (s32[24,24]{1,0:T(8,128)S(1)}, s32[24,24]{1,0:T(8,128)}, u32[]{:S(2)}) copy-start(s32[24,24]{1,0:T(8,128)} %refs_11_.3) | copy-start | bytes 6916
  73.5 2.0 %collective-permute-start.1 = (bf16[192,384]{1,0:T(8,128)(2,1)S(1)}, bf16[192,384]{1,0:T(8,128)(2,1)S(1)}, u32[]{:S(2)}, u32[]{:S(2)}) collective-permute-start(bf16[192,384]{1,0:T(8,128)(2,1)S(1)} %get-tuple-element.56), channel_id=1, source_target_pairs={{0,16},{16,0},{1,17},{17,1},{2,18},{18,2},{3,19},{19,3},{4,20},{20... | collective-permute-start | bytes 442376 | tf_op jit(solution)/shard_map/ppermute | solution.py:359

commit v8 on v7

--- a/solution.py
+++ b/solution.py
@@ -80,6 +80,13 @@
                 rows[i] = turned[n * SIDE : (n + 1) * SIDE]
         parts.append(jnp.concatenate(rows, axis=0))
     return parts
+
+
+def chain(segments, lane):
+    line = None
+    for begin, source in sorted(segments, key=lambda segment: segment[0]):
+        line = source if line is None else jnp.where(lane >= begin, source, line)
+    return line
 
 
 def assemble(scratch, lines, first, spot, store, spots=range(BLOCKS)):
@@ -105,19 +112,24 @@
 
 def disassemble(load, scratch, lines, first, blocks):
     total = scratch.shape[0] // (GROUPS * blocks)
+    tiles = -(-blocks * SIDE // WIDTH)
     lane = lanes(GROUPS)
-    for c in range(blocks):
-        begin = c * SIDE
-        t, after = begin // WIDTH, (begin + SIDE - 1) // WIDTH
-        for r in range(lines):
-            line = None
-            for n, i in enumerate(rows_in(r, lines)):
-                shift = n * SIDE - begin
-                piece = roll(load(i, t), shift)
-                if after != t:
-                    border = n * SIDE + after * WIDTH - begin
-                    piece = jnp.where(lane < border, piece, roll(load(i, after), shift))
-                line = piece if line is None else jnp.where(lane >= n * SIDE, piece, line)
+    for r in range(lines):
+        turned = []
+        for n, i in enumerate(rows_in(r, lines)):
+            shift = n * SIDE
+            moved = [roll(load(i, t), shift) for t in range(tiles)]
+            if shift:
+                moved = [jnp.where(lane < shift, moved[t - 1], moved[t]) for t in range(tiles)]
+            turned.append(moved)
+        for c in range(blocks):
+            segments = []
+            for n, moved in enumerate(turned):
+                t, start = divmod((c + n) * SIDE, WIDTH)
+                segments.append((start, moved[t % tiles]))
+                if start + SIDE > WIDTH:
+                    segments.append((0, moved[(t + 1) % tiles]))
+            line = roll(chain(segments, lane), -c * SIDE)
             scratch[pl.ds(c * GROUPS * total + first + r, GROUPS, stride=total), :] = line
 
 

time: 99.6 us -> 99.3 us (level)
  no operation moved by 1% of the time
where the time goes in v8:
time: 99.3 us; the launch traced here: 99 us
  blocking collectives  90.3 us (91%)
  Pallas kernels  8.08 us (8%)
    all_to_all x4, blocking collectives, spread(): lax.all_to_all(paired, SPREAD, 0, 0, tiled=True).reshape(messages.shape)  90.3 us
    pallas_call x12, Pallas kernels, call(): pl.pallas_call(kernel, out_shape=[jax.ShapeDtypeStruct(shape, dtype) for...  8.08 us
  transfers between devices with their start and end apart: 2, of which 0 were waited for; matrix products, arithmetic and copies ran while one was open for 0% of the time, Pallas kernels for 3%

profile of v8, /device:TPU:32, one launch (start us, length us, event | category | flops | bytes accessed | tf_op | source)
XLA Modules:
  0.0 99.0 jit_solution(5877491712183304291)
XLA Ops:
  0.0 0.0 copy-start.7
  0.0 1.8 %edges.1 = bf16[1280,128]{1,0:T(8,128)(2,1)S(1)} custom-call(bf16[576,128]{1,0:T(8,128)(2,1)} %bitcast.11, f32[24,24]{1,0:T(8,128)} %refs_9_.3, f32[24,24]{1,0:T(8,128)} %refs_10_.3, s32[24,24]{1,0:T(8,128)} %refs_11_.3, bf16[128,128]{1,0:T(8,128)(2,1)} %lg.1, bf16[128,128]{1,0:T(8,128)(2,1)} %lv.1, bf16[128,128]{1,0:T(8,128)(2,1)} %rg.1, bf16[128,128]{1,0:T(8,128)(2,1)} %rv.1), custom_call_target="tpu_custom_call" | custom-call | tf_op jit(solution)/shard_map/edges/pallas_call | solution.py:354
  1.8 30.6 %all_to_all.20 = bf16[128,5,2,128]{3,2,1,0:T(2,128)(2,1)S(1)} all-to-all(bf16[128,5,2,128]{3,2,1,0:T(2,128)(2,1)S(1)} %bitcast.20), channel_id=1, replica_groups=mesh['z_lo'=2,'x'=4,'core'=2,'z_hi'=4,'y'=4] {'z_hi','y','z_lo','x'}, dimensions={0} | all-to-all | bytes 655360 | tf_op jit(solution)/shard_map/all_to_all | solution.py:367
  32.4 0.3 take_right.1
  32.7 0.1 collective-permute-start
  32.8 0.3 take_left.1.left_ref.refs_7_
  33.1 0.4 mix_own.1.own_ref
  33.5 0.6 ready.1
  34.2 0.0 copy-start.4
  34.2 0.0 copy-start.5
  34.2 0.0 copy-start.10
  34.2 0.0 collective-permute-done.right_ref.other_ref
  34.2 0.4 mix.1
  34.6 19.5 %all_to_all.21 = bf16[128,3,2,128]{3,2,1,0:T(2,128)(2,1)S(1)} all-to-all(bf16[128,3,2,128]{3,2,1,0:T(2,128)(2,1)S(1)} %bitcast.24), channel_id=1, replica_groups=mesh['z_lo'=2,'x'=4,'core'=2,'z_hi'=4,'y'=4] {'z_hi','y','z_lo','x'}, dimensions={0} | all-to-all | bytes 393216 | tf_op jit(solution)/shard_map/all_to_all | solution.py:367
  54.1 0.6 middle.1
  54.8 18.1 %all_to_all.22 = bf16[128,3,2,128]{3,2,1,0:T(2,128)(2,1)S(1)} all-to-all(bf16[128,3,2,128]{3,2,1,0:T(2,128)(2,1)S(1)} %bitcast.27), channel_id=1, replica_groups=mesh['z_lo'=2,'x'=4,'core'=2,'z_hi'=4,'y'=4] {'z_hi','y','z_lo','x'}, dimensions={0} | all-to-all | bytes 393216 | tf_op jit(solution)/shard_map/all_to_all | solution.py:367
  73.0 0.5 right_grad.1
  73.4 0.1 collective-permute-start.1
  73.5 1.2 %right_grad_later.1 = (bf16[192,384]{1,0:T(8,128)(2,1)S(1)}, f32[192,384]{1,0:T(8,128)S(1)}, f32[576,128]{1,0:T(8,128)S(1)}, f32[576,128]{1,0:T(8,128)S(1)}, f32...) custom-call(bf16[192,384]{1,0:T(8,128)(2,1)S(1)} %get-tuple-element.43.refs_0_, ...), custom_call_target="tpu_custom_call" | custom-call | tf_op jit(solution)/shard_map/right_grad_later/pallas_call | solution.py:354
  74.7 0.5 left_grad.1.lines_ref
  75.2 0.0 collective-permute-done.1.other_ref
  75.2 0.3 return.1
  75.6 22.1 %all_to_all.23 = bf16[128,5,2,128]{3,2,1,0:T(2,128)(2,1)S(1)} all-to-all(bf16[128,5,2,128]{3,2,1,0:T(2,128)(2,1)S(1)} %bitcast.21), channel_id=1, replica_groups=mesh['z_lo'=2,'x'=4,'core'=2,'z_hi'=4,'y'=4] {'z_hi','y','z_lo','x'}, dimensions={0} | all-to-all | bytes 655360 | tf_op jit(solution)/shard_map/all_to_all | solution.py:367
  97.6 1.2 %last.1 = f32[576,128]{1,0:T(8,128)} custom-call(bf16[1280,128]{1,0:T(8,128)(2,1)S(1)} %bitcast.22, f32[576,128]{1,0:T(8,128)S(1)} %get-tuple-element.57.normed_ref, f32[576,128]{1,0:T(8,128)S(1)} %get-tuple-element.58.scale_ref, f32[576,128]{1,0:T(8,128)S(1)} %get-tuple-element.59.base_ref, f32[4,576,128]{2,1,0:T(8,128)S(1)} %get-tuple-element.60.factors_ref, ...), custom_call_target="tpu_custom_call" | custom-call | tf_op jit(solution)/shard_map/last/pallas_call | solution.py:354
  (18 shorter events, 0.0 us)
Async XLA Ops:
  0.0 32.4 %copy-start.9 = (f32[24,24]{1,0:T(8,128)S(1)}, f32[24,24]{1,0:T(8,128)}, u32[]{:S(2)}) copy-start(f32[24,24]{1,0:T(8,128)} %refs_10_.3) | copy-start | bytes 6916
  0.0 32.4 %copy-start.8 = (f32[24,24]{1,0:T(8,128)S(1)}, f32[24,24]{1,0:T(8,128)}, u32[]{:S(2)}) copy-start(f32[24,24]{1,0:T(8,128)} %refs_9_.3) | copy-start | bytes 6916
  0.0 32.4 %copy-start = (bf16[24,24,128]{2,1,0:T(8,128)(2,1)S(1)}, bf16[24,24,128]{2,1,0:T(8,128)(2,1)}, u32[]{:S(2)}) copy-start(bf16[24,24,128]{2,1,0:T(8,128)(2,1)} %param.11) | copy-start | bytes 442372
  0.0 32.4 %copy-start.7 = (bf16[128,128]{1,0:T(8,128)(2,1)S(1)}, bf16[128,128]{1,0:T(8,128)(2,1)}, u32[]{:S(2)}) copy-start(bf16[128,128]{1,0:T(8,128)(2,1)} %refs_14_.1) | copy-start | bytes 98308
  0.0 32.4 %copy-start.6 = (bf16[128,128]{1,0:T(8,128)(2,1)S(1)}, bf16[128,128]{1,0:T(8,128)(2,1)}, u32[]{:S(2)}) copy-start(bf16[128,128]{1,0:T(8,128)(2,1)} %refs_19_.1) | copy-start | bytes 98308
  0.0 32.4 %copy-start.1 = (bf16[24,24,128]{2,1,0:T(8,128)(2,1)S(1)}, bf16[24,24,128]{2,1,0:T(8,128)(2,1)}, u32[]{:S(2)}) copy-start(bf16[24,24,128]{2,1,0:T(8,128)(2,1)} %param.15) | copy-start | bytes 442372
  32.7 1.5 %collective-permute-start = (bf16[192,384]{1,0:T(8,128)(2,1)S(1)}, bf16[192,384]{1,0:T(8,128)(2,1)S(1)}, u32[]{:S(2)}, u32[]{:S(2)}) collective-permute-start(bf16[192,384]{1,0:T(8,128)(2,1)S(1)} %get-tuple-element.33.right_ref.own_ref), channel_id=1, source_target_pairs={{0,16},{16,0},{1,17},{17,1},{2,18},{18,2},{3,19},{19,3},{4,20},{20... | collective-permute-start | bytes 442376 | tf_op jit(solution)/shard_map/ppermute | solution.py:371
  34.2 38.8 %copy-start.2 = (bf16[128,128]{1,0:T(8,128)(2,1)S(1)}, bf16[128,128]{1,0:T(8,128)(2,1)}, u32[]{:S(2)}) copy-start(bf16[128,128]{1,0:T(8,128)(2,1)} %lg.1) | copy-start | bytes 98308
  34.2 38.8 %copy-start.3 = (bf16[128,128]{1,0:T(8,128)(2,1)S(1)}, bf16[128,128]{1,0:T(8,128)(2,1)}, u32[]{:S(2)}) copy-start(bf16[128,128]{1,0:T(8,128)(2,1)} %lv.1) | copy-start | bytes 98308
  34.2 38.8 %copy-start.4 = (bf16[128,128]{1,0:T(8,128)(2,1)S(1)}, bf16[128,128]{1,0:T(8,128)(2,1)}, u32[]{:S(2)}) copy-start(bf16[128,128]{1,0:T(8,128)(2,1)} %rg.1) | copy-start | bytes 98308
  34.2 38.8 %copy-start.5 = (bf16[128,128]{1,0:T(8,128)(2,1)S(1)}, bf16[128,128]{1,0:T(8,128)(2,1)}, u32[]{:S(2)}) copy-start(bf16[128,128]{1,0:T(8,128)(2,1)} %rv.1) | copy-start | bytes 98308
  34.2 38.8 %copy-start.10 = (s32[24,24]{1,0:T(8,128)S(1)}, s32[24,24]{1,0:T(8,128)}, u32[]{:S(2)}) copy-start(s32[24,24]{1,0:T(8,128)} %refs_11_.3) | copy-start | bytes 6916
  73.4 1.8 %collective-permute-start.1 = (bf16[192,384]{1,0:T(8,128)(2,1)S(1)}, bf16[192,384]{1,0:T(8,128)(2,1)S(1)}, u32[]{:S(2)}, u32[]{:S(2)}) collective-permute-start(bf16[192,384]{1,0:T(8,128)(2,1)S(1)} %get-tuple-element.56), channel_id=1, source_target_pairs={{0,16},{16,0},{1,17},{17,1},{2,18},{18,2},{3,19},{19,3},{4,20},{20... | collective-permute-start | bytes 442376 | tf_op jit(solution)/shard_map/ppermute | solution.py:371

commit v9 on v8

--- a/solution.py
+++ b/solution.py
@@ -220,7 +220,8 @@
     normed, _ = normalise(pair_ref, mean_ref, scale_ref)
     out_sig = jax.nn.sigmoid(dot(normed.astype(bf16), gate_ref[...]))
     grad_y = cot_ref[...].astype(f32) * out_sig
-    grad_ref[...] = dot(grad_y.astype(bf16), weight_ref[...], ((1,), (1,)))
+    grad = dot(grad_y.astype(bf16), weight_ref[...], ((1,), (1,)))
+    grad_ref[...] = grad - jnp.mean(grad, axis=-1, keepdims=True)
     factor_ref[...] = grad_y * (1.0 - out_sig)
 
 
@@ -244,11 +245,12 @@
 
 def middle_kernel(in_ref, grad_ref, out_ref, normed_ref, scratch):
     (mixed,) = from_messages(in_ref, scratch, 1)
-    centred = mixed - jnp.mean(mixed, axis=-1, keepdims=True)
+    centred = mixed - dot(mixed.astype(bf16), jnp.full((WIDTH, WIDTH), 1 / WIDTH, bf16))
     mix_scale = lax.rsqrt(jnp.mean(centred * centred, axis=-1, keepdims=True) + epsilon)
     mix_normed = centred * mix_scale
     normed_ref[...] = mix_normed.astype(bf16)
-    grad_mix = layer_back(grad_ref[...], mix_normed, mix_scale)
+    grad = grad_ref[...]
+    grad_mix = mix_scale * (grad - mix_normed * jnp.mean(grad * mix_normed, axis=-1, keepdims=True))
     out_ref[...] = to_messages([grad_mix], scratch)
 
 
@@ -257,7 +259,7 @@
     grad = panel[...]
     grad_ref[...] = grad.astype(bf16)
     first = lax.axis_index("core") == 0
-    sums = dot(jnp.transpose(grad).astype(bf16), left_ref[...])
+    sums = dot(grad.astype(bf16), left_ref[...], ((0,), (0,)))
     own_ref[...] = jnp.where(first, sums[:HALF], sums[HALF:])
     return jnp.where(first, sums[HALF:], sums[:HALF])
 
@@ -267,8 +269,8 @@
 
     def only_sent():
         assemble_left(in_ref, scratch, panel, ALONE, place, range(BLOCKS // 2, BLOCKS))
-        turned = jnp.transpose(panel[:, WIDTH:])[HALF - WIDTH :]
-        sent_ref[...] = dot(turned.astype(bf16), left_ref[...]).astype(bf16)
+        sums = dot(panel[:, WIDTH:].astype(bf16), left_ref[...], ((0,), (0,)))
+        sent_ref[...] = sums[HALF - WIDTH :].astype(bf16)
 
     def everything():
         sent_ref[...] = right_grad_all(in_ref, left_ref, grad_ref, own_ref, scratch, panel).astype(bf16)

time: 99.3 us -> 99.2 us (level)
  no operation moved by 1% of the time
where the time goes in v9:
time: 99.2 us; the launch traced here: 98.9 us
  blocking collectives  90.2 us (91%)
  Pallas kernels  8.03 us (8%)
    all_to_all x4, blocking collectives, spread(): lax.all_to_all(paired, SPREAD, 0, 0, tiled=True).reshape(messages.shape)  90.2 us
    pallas_call x12, Pallas kernels, call(): pl.pallas_call(kernel, out_shape=[jax.ShapeDtypeStruct(shape, dtype) for...  8.03 us
  transfers between devices with their start and end apart: 2, of which 0 were waited for; matrix products, arithmetic and copies ran while one was open for 0% of the time, Pallas kernels for 3%

profile of v9, /device:TPU:32, one launch (start us, length us, event | category | flops | bytes accessed | tf_op | source)
XLA Modules:
  0.0 98.9 jit_solution(17155936501045480774)
XLA Ops:
  0.0 1.8 %edges.1 = bf16[1280,128]{1,0:T(8,128)(2,1)S(1)} custom-call(bf16[576,128]{1,0:T(8,128)(2,1)} %bitcast.11, f32[24,24]{1,0:T(8,128)} %refs_9_.3, f32[24,24]{1,0:T(8,128)} %refs_10_.3, s32[24,24]{1,0:T(8,128)} %refs_11_.3, bf16[128,128]{1,0:T(8,128)(2,1)} %lg.1, bf16[128,128]{1,0:T(8,128)(2,1)} %lv.1, bf16[128,128]{1,0:T(8,128)(2,1)} %rg.1, bf16[128,128]{1,0:T(8,128)(2,1)} %rv.1), custom_call_target="tpu_custom_call" | custom-call | tf_op jit(solution)/shard_map/edges/pallas_call | solution.py:356
  1.8 30.6 %all_to_all.20 = bf16[128,5,2,128]{3,2,1,0:T(2,128)(2,1)S(1)} all-to-all(bf16[128,5,2,128]{3,2,1,0:T(2,128)(2,1)S(1)} %bitcast.20), channel_id=1, replica_groups=mesh['z_lo'=2,'x'=4,'core'=2,'z_hi'=4,'y'=4] {'z_hi','y','z_lo','x'}, dimensions={0} | all-to-all | bytes 655360 | tf_op jit(solution)/shard_map/all_to_all | solution.py:369
  32.4 0.3 take_right.1
  32.7 0.1 collective-permute-start
  32.8 0.3 take_left.1.left_ref.refs_7_
  33.1 0.4 mix_own.1.own_ref
  33.5 0.7 ready.1
  34.2 0.0 copy-start.2
  34.2 0.0 copy-start.3
  34.2 0.0 copy-start.4
  34.3 0.0 copy-start.5
  34.3 0.0 copy-start.10
  34.3 0.0 collective-permute-done.right_ref.other_ref
  34.3 0.4 mix.1
  34.7 19.4 %all_to_all.21 = bf16[128,3,2,128]{3,2,1,0:T(2,128)(2,1)S(1)} all-to-all(bf16[128,3,2,128]{3,2,1,0:T(2,128)(2,1)S(1)} %bitcast.24), channel_id=1, replica_groups=mesh['z_lo'=2,'x'=4,'core'=2,'z_hi'=4,'y'=4] {'z_hi','y','z_lo','x'}, dimensions={0} | all-to-all | bytes 393216 | tf_op jit(solution)/shard_map/all_to_all | solution.py:369
  54.1 0.6 middle.1
  54.8 18.1 %all_to_all.22 = bf16[128,3,2,128]{3,2,1,0:T(2,128)(2,1)S(1)} all-to-all(bf16[128,3,2,128]{3,2,1,0:T(2,128)(2,1)S(1)} %bitcast.27), channel_id=1, replica_groups=mesh['z_lo'=2,'x'=4,'core'=2,'z_hi'=4,'y'=4] {'z_hi','y','z_lo','x'}, dimensions={0} | all-to-all | bytes 393216 | tf_op jit(solution)/shard_map/all_to_all | solution.py:369
  72.9 0.4 right_grad.1
  73.3 0.1 collective-permute-start.1
  73.4 1.1 %right_grad_later.1 = (bf16[192,384]{1,0:T(8,128)(2,1)S(1)}, f32[192,384]{1,0:T(8,128)S(1)}, f32[576,128]{1,0:T(8,128)S(1)}, f32[576,128]{1,0:T(8,128)S(1)}, f32...) custom-call(bf16[192,384]{1,0:T(8,128)(2,1)S(1)} %get-tuple-element.43.refs_0_, ...), custom_call_target="tpu_custom_call" | custom-call | tf_op jit(solution)/shard_map/right_grad_later/pallas_call | solution.py:356
  74.6 0.5 left_grad.1.lines_ref
  75.1 0.3 return.1
  75.4 22.1 %all_to_all.23 = bf16[128,5,2,128]{3,2,1,0:T(2,128)(2,1)S(1)} all-to-all(bf16[128,5,2,128]{3,2,1,0:T(2,128)(2,1)S(1)} %bitcast.21), channel_id=1, replica_groups=mesh['z_lo'=2,'x'=4,'core'=2,'z_hi'=4,'y'=4] {'z_hi','y','z_lo','x'}, dimensions={0} | all-to-all | bytes 655360 | tf_op jit(solution)/shard_map/all_to_all | solution.py:369
  97.5 1.2 %last.1 = f32[576,128]{1,0:T(8,128)} custom-call(bf16[1280,128]{1,0:T(8,128)(2,1)S(1)} %bitcast.22, f32[576,128]{1,0:T(8,128)S(1)} %get-tuple-element.57.normed_ref, f32[576,128]{1,0:T(8,128)S(1)} %get-tuple-element.58.scale_ref, f32[576,128]{1,0:T(8,128)S(1)} %get-tuple-element.59.base_ref, f32[4,576,128]{2,1,0:T(8,128)S(1)} %get-tuple-element.60.factors_ref, ...), custom_call_target="tpu_custom_call" | custom-call | tf_op jit(solution)/shard_map/last/pallas_call | solution.py:356
  (18 shorter events, 0.0 us)
Async XLA Ops:
  0.0 32.4 %copy-start.9 = (f32[24,24]{1,0:T(8,128)S(1)}, f32[24,24]{1,0:T(8,128)}, u32[]{:S(2)}) copy-start(f32[24,24]{1,0:T(8,128)} %refs_10_.3) | copy-start | bytes 6916
  0.0 32.4 %copy-start.8 = (f32[24,24]{1,0:T(8,128)S(1)}, f32[24,24]{1,0:T(8,128)}, u32[]{:S(2)}) copy-start(f32[24,24]{1,0:T(8,128)} %refs_9_.3) | copy-start | bytes 6916
  0.0 32.4 %copy-start = (bf16[24,24,128]{2,1,0:T(8,128)(2,1)S(1)}, bf16[24,24,128]{2,1,0:T(8,128)(2,1)}, u32[]{:S(2)}) copy-start(bf16[24,24,128]{2,1,0:T(8,128)(2,1)} %param.11) | copy-start | bytes 442372
  0.0 32.4 %copy-start.7 = (bf16[128,128]{1,0:T(8,128)(2,1)S(1)}, bf16[128,128]{1,0:T(8,128)(2,1)}, u32[]{:S(2)}) copy-start(bf16[128,128]{1,0:T(8,128)(2,1)} %refs_14_.1) | copy-start | bytes 98308
  0.0 32.4 %copy-start.6 = (bf16[128,128]{1,0:T(8,128)(2,1)S(1)}, bf16[128,128]{1,0:T(8,128)(2,1)}, u32[]{:S(2)}) copy-start(bf16[128,128]{1,0:T(8,128)(2,1)} %refs_19_.1) | copy-start | bytes 98308
  0.0 32.4 %copy-start.1 = (bf16[24,24,128]{2,1,0:T(8,128)(2,1)S(1)}, bf16[24,24,128]{2,1,0:T(8,128)(2,1)}, u32[]{:S(2)}) copy-start(bf16[24,24,128]{2,1,0:T(8,128)(2,1)} %param.15) | copy-start | bytes 442372
  32.7 1.5 %collective-permute-start = (bf16[192,384]{1,0:T(8,128)(2,1)S(1)}, bf16[192,384]{1,0:T(8,128)(2,1)S(1)}, u32[]{:S(2)}, u32[]{:S(2)}) collective-permute-start(bf16[192,384]{1,0:T(8,128)(2,1)S(1)} %get-tuple-element.33.right_ref.own_ref), channel_id=1, source_target_pairs={{0,16},{16,0},{1,17},{17,1},{2,18},{18,2},{3,19},{19,3},{4,20},{20... | collective-permute-start | bytes 442376 | tf_op jit(solution)/shard_map/ppermute | solution.py:373
  34.2 38.7 %copy-start.2 = (bf16[128,128]{1,0:T(8,128)(2,1)S(1)}, bf16[128,128]{1,0:T(8,128)(2,1)}, u32[]{:S(2)}) copy-start(bf16[128,128]{1,0:T(8,128)(2,1)} %lg.1) | copy-start | bytes 98308
  34.2 38.7 %copy-start.3 = (bf16[128,128]{1,0:T(8,128)(2,1)S(1)}, bf16[128,128]{1,0:T(8,128)(2,1)}, u32[]{:S(2)}) copy-start(bf16[128,128]{1,0:T(8,128)(2,1)} %lv.1) | copy-start | bytes 98308
  34.2 38.6 %copy-start.4 = (bf16[128,128]{1,0:T(8,128)(2,1)S(1)}, bf16[128,128]{1,0:T(8,128)(2,1)}, u32[]{:S(2)}) copy-start(bf16[128,128]{1,0:T(8,128)(2,1)} %rg.1) | copy-start | bytes 98308
  34.3 38.6 %copy-start.5 = (bf16[128,128]{1,0:T(8,128)(2,1)S(1)}, bf16[128,128]{1,0:T(8,128)(2,1)}, u32[]{:S(2)}) copy-start(bf16[128,128]{1,0:T(8,128)(2,1)} %rv.1) | copy-start | bytes 98308
  34.3 38.6 %copy-start.10 = (s32[24,24]{1,0:T(8,128)S(1)}, s32[24,24]{1,0:T(8,128)}, u32[]{:S(2)}) copy-start(s32[24,24]{1,0:T(8,128)} %refs_11_.3) | copy-start | bytes 6916
  73.3 1.7 %collective-permute-start.1 = (bf16[192,384]{1,0:T(8,128)(2,1)S(1)}, bf16[192,384]{1,0:T(8,128)(2,1)S(1)}, u32[]{:S(2)}, u32[]{:S(2)}) collective-permute-start(bf16[192,384]{1,0:T(8,128)(2,1)S(1)} %get-tuple-element.56), channel_id=1, source_target_pairs={{0,16},{16,0},{1,17},{17,1},{2,18},{18,2},{3,19},{19,3},{4,20},{20... | collective-permute-start | bytes 442376 | tf_op jit(solution)/shard_map/ppermute | solution.py:373

commit v10 on v9

--- a/solution.py
+++ b/solution.py
@@ -193,7 +193,7 @@
 
 
 def half_mixed(left_ref, right_ref, scratch, panel):
-    panel[:, :HALF] = dot(left_ref[...], right_ref[...], ((1,), (1,)))
+    panel[:, :HALF] = dot(left_ref[...], jnp.transpose(right_ref[...]))
     disassemble(rows_of(panel), scratch, ALONE, 0, BLOCKS // 2)
 
 

time: 99.2 us -> 99.2 us (level)
  no operation moved by 1% of the time
where the time goes in v10:
time: 99.2 us; the launch traced here: 98.9 us
  blocking collectives  90.2 us (91%)
  Pallas kernels  8.03 us (8%)
    all_to_all x4, blocking collectives, spread(): lax.all_to_all(paired, SPREAD, 0, 0, tiled=True).reshape(messages.shape)  90.2 us
    pallas_call x12, Pallas kernels, call(): pl.pallas_call(kernel, out_shape=[jax.ShapeDtypeStruct(shape, dtype) for...  8.03 us
  transfers between devices with their start and end apart: 2, of which 0 were waited for; matrix products, arithmetic and copies ran while one was open for 0% of the time, Pallas kernels for 3%

profile of v10, /device:TPU:32, one launch (start us, length us, event | category | flops | bytes accessed | tf_op | source)
XLA Modules:
  0.0 98.9 jit_solution(17155936501045480774)
XLA Ops:
  0.0 1.8 %edges.1 = bf16[1280,128]{1,0:T(8,128)(2,1)S(1)} custom-call(bf16[576,128]{1,0:T(8,128)(2,1)} %bitcast.11, f32[24,24]{1,0:T(8,128)} %refs_9_.3, f32[24,24]{1,0:T(8,128)} %refs_10_.3, s32[24,24]{1,0:T(8,128)} %refs_11_.3, bf16[128,128]{1,0:T(8,128)(2,1)} %lg.1, bf16[128,128]{1,0:T(8,128)(2,1)} %lv.1, bf16[128,128]{1,0:T(8,128)(2,1)} %rg.1, bf16[128,128]{1,0:T(8,128)(2,1)} %rv.1), custom_call_target="tpu_custom_call" | custom-call | tf_op jit(solution)/shard_map/edges/pallas_call | solution.py:356
  1.8 30.6 %all_to_all.20 = bf16[128,5,2,128]{3,2,1,0:T(2,128)(2,1)S(1)} all-to-all(bf16[128,5,2,128]{3,2,1,0:T(2,128)(2,1)S(1)} %bitcast.20), channel_id=1, replica_groups=mesh['z_lo'=2,'x'=4,'core'=2,'z_hi'=4,'y'=4] {'z_hi','y','z_lo','x'}, dimensions={0} | all-to-all | bytes 655360 | tf_op jit(solution)/shard_map/all_to_all | solution.py:369
  32.4 0.3 take_right.1
  32.7 0.1 collective-permute-start
  32.8 0.3 take_left.1.left_ref.refs_7_
  33.1 0.4 mix_own.1.own_ref
  33.5 0.7 ready.1
  34.2 0.0 copy-start.2
  34.2 0.0 copy-start.3
  34.2 0.0 copy-start.4
  34.3 0.0 copy-start.5
  34.3 0.0 copy-start.10
  34.3 0.0 collective-permute-done.right_ref.other_ref
  34.3 0.4 mix.1
  34.7 19.4 %all_to_all.21 = bf16[128,3,2,128]{3,2,1,0:T(2,128)(2,1)S(1)} all-to-all(bf16[128,3,2,128]{3,2,1,0:T(2,128)(2,1)S(1)} %bitcast.24), channel_id=1, replica_groups=mesh['z_lo'=2,'x'=4,'core'=2,'z_hi'=4,'y'=4] {'z_hi','y','z_lo','x'}, dimensions={0} | all-to-all | bytes 393216 | tf_op jit(solution)/shard_map/all_to_all | solution.py:369
  54.1 0.6 middle.1
  54.8 18.1 %all_to_all.22 = bf16[128,3,2,128]{3,2,1,0:T(2,128)(2,1)S(1)} all-to-all(bf16[128,3,2,128]{3,2,1,0:T(2,128)(2,1)S(1)} %bitcast.27), channel_id=1, replica_groups=mesh['z_lo'=2,'x'=4,'core'=2,'z_hi'=4,'y'=4] {'z_hi','y','z_lo','x'}, dimensions={0} | all-to-all | bytes 393216 | tf_op jit(solution)/shard_map/all_to_all | solution.py:369
  72.9 0.4 right_grad.1
  73.3 0.1 collective-permute-start.1
  73.4 1.1 %right_grad_later.1 = (bf16[192,384]{1,0:T(8,128)(2,1)S(1)}, f32[192,384]{1,0:T(8,128)S(1)}, f32[576,128]{1,0:T(8,128)S(1)}, f32[576,128]{1,0:T(8,128)S(1)}, f32...) custom-call(bf16[192,384]{1,0:T(8,128)(2,1)S(1)} %get-tuple-element.43.refs_0_, ...), custom_call_target="tpu_custom_call" | custom-call | tf_op jit(solution)/shard_map/right_grad_later/pallas_call | solution.py:356
  74.6 0.5 left_grad.1.lines_ref
  75.1 0.3 return.1
  75.4 22.1 %all_to_all.23 = bf16[128,5,2,128]{3,2,1,0:T(2,128)(2,1)S(1)} all-to-all(bf16[128,5,2,128]{3,2,1,0:T(2,128)(2,1)S(1)} %bitcast.21), channel_id=1, replica_groups=mesh['z_lo'=2,'x'=4,'core'=2,'z_hi'=4,'y'=4] {'z_hi','y','z_lo','x'}, dimensions={0} | all-to-all | bytes 655360 | tf_op jit(solution)/shard_map/all_to_all | solution.py:369
  97.5 1.2 %last.1 = f32[576,128]{1,0:T(8,128)} custom-call(bf16[1280,128]{1,0:T(8,128)(2,1)S(1)} %bitcast.22, f32[576,128]{1,0:T(8,128)S(1)} %get-tuple-element.57.normed_ref, f32[576,128]{1,0:T(8,128)S(1)} %get-tuple-element.58.scale_ref, f32[576,128]{1,0:T(8,128)S(1)} %get-tuple-element.59.base_ref, f32[4,576,128]{2,1,0:T(8,128)S(1)} %get-tuple-element.60.factors_ref, ...), custom_call_target="tpu_custom_call" | custom-call | tf_op jit(solution)/shard_map/last/pallas_call | solution.py:356
  (18 shorter events, 0.0 us)
Async XLA Ops:
  0.0 32.4 %copy-start.9 = (f32[24,24]{1,0:T(8,128)S(1)}, f32[24,24]{1,0:T(8,128)}, u32[]{:S(2)}) copy-start(f32[24,24]{1,0:T(8,128)} %refs_10_.3) | copy-start | bytes 6916
  0.0 32.4 %copy-start.8 = (f32[24,24]{1,0:T(8,128)S(1)}, f32[24,24]{1,0:T(8,128)}, u32[]{:S(2)}) copy-start(f32[24,24]{1,0:T(8,128)} %refs_9_.3) | copy-start | bytes 6916
  0.0 32.4 %copy-start = (bf16[24,24,128]{2,1,0:T(8,128)(2,1)S(1)}, bf16[24,24,128]{2,1,0:T(8,128)(2,1)}, u32[]{:S(2)}) copy-start(bf16[24,24,128]{2,1,0:T(8,128)(2,1)} %param.11) | copy-start | bytes 442372
  0.0 32.4 %copy-start.7 = (bf16[128,128]{1,0:T(8,128)(2,1)S(1)}, bf16[128,128]{1,0:T(8,128)(2,1)}, u32[]{:S(2)}) copy-start(bf16[128,128]{1,0:T(8,128)(2,1)} %refs_14_.1) | copy-start | bytes 98308
  0.0 32.4 %copy-start.6 = (bf16[128,128]{1,0:T(8,128)(2,1)S(1)}, bf16[128,128]{1,0:T(8,128)(2,1)}, u32[]{:S(2)}) copy-start(bf16[128,128]{1,0:T(8,128)(2,1)} %refs_19_.1) | copy-start | bytes 98308
  0.0 32.4 %copy-start.1 = (bf16[24,24,128]{2,1,0:T(8,128)(2,1)S(1)}, bf16[24,24,128]{2,1,0:T(8,128)(2,1)}, u32[]{:S(2)}) copy-start(bf16[24,24,128]{2,1,0:T(8,128)(2,1)} %param.15) | copy-start | bytes 442372
  32.7 1.5 %collective-permute-start = (bf16[192,384]{1,0:T(8,128)(2,1)S(1)}, bf16[192,384]{1,0:T(8,128)(2,1)S(1)}, u32[]{:S(2)}, u32[]{:S(2)}) collective-permute-start(bf16[192,384]{1,0:T(8,128)(2,1)S(1)} %get-tuple-element.33.right_ref.own_ref), channel_id=1, source_target_pairs={{0,16},{16,0},{1,17},{17,1},{2,18},{18,2},{3,19},{19,3},{4,20},{20... | collective-permute-start | bytes 442376 | tf_op jit(solution)/shard_map/ppermute | solution.py:373
  34.2 38.7 %copy-start.2 = (bf16[128,128]{1,0:T(8,128)(2,1)S(1)}, bf16[128,128]{1,0:T(8,128)(2,1)}, u32[]{:S(2)}) copy-start(bf16[128,128]{1,0:T(8,128)(2,1)} %lg.1) | copy-start | bytes 98308
  34.2 38.7 %copy-start.3 = (bf16[128,128]{1,0:T(8,128)(2,1)S(1)}, bf16[128,128]{1,0:T(8,128)(2,1)}, u32[]{:S(2)}) copy-start(bf16[128,128]{1,0:T(8,128)(2,1)} %lv.1) | copy-start | bytes 98308
  34.2 38.6 %copy-start.4 = (bf16[128,128]{1,0:T(8,128)(2,1)S(1)}, bf16[128,128]{1,0:T(8,128)(2,1)}, u32[]{:S(2)}) copy-start(bf16[128,128]{1,0:T(8,128)(2,1)} %rg.1) | copy-start | bytes 98308
  34.3 38.6 %copy-start.5 = (bf16[128,128]{1,0:T(8,128)(2,1)S(1)}, bf16[128,128]{1,0:T(8,128)(2,1)}, u32[]{:S(2)}) copy-start(bf16[128,128]{1,0:T(8,128)(2,1)} %rv.1) | copy-start | bytes 98308
  34.3 38.6 %copy-start.10 = (s32[24,24]{1,0:T(8,128)S(1)}, s32[24,24]{1,0:T(8,128)}, u32[]{:S(2)}) copy-start(s32[24,24]{1,0:T(8,128)} %refs_11_.3) | copy-start | bytes 6916
  73.3 1.7 %collective-permute-start.1 = (bf16[192,384]{1,0:T(8,128)(2,1)S(1)}, bf16[192,384]{1,0:T(8,128)(2,1)S(1)}, u32[]{:S(2)}, u32[]{:S(2)}) collective-permute-start(bf16[192,384]{1,0:T(8,128)(2,1)S(1)} %get-tuple-element.56), channel_id=1, source_target_pairs={{0,16},{16,0},{1,17},{17,1},{2,18},{18,2},{3,19},{19,3},{4,20},{20... | collective-permute-start | bytes 442376 | tf_op jit(solution)/shard_map/ppermute | solution.py:373

commit v11 on v10

--- a/solution.py
+++ b/solution.py
@@ -154,9 +154,10 @@
     kept_scale = spread_pairs(scale_ref[...] * mask_ref[...].astype(f32))
     low = ((pair_ref[...].astype(f32) - spread_pairs(mean_ref[...])) * kept_scale).astype(bf16)
     parts = []
-    for gate, value in ((lg, lv), (rg, rv)):
-        both = dot(low, jnp.concatenate([gate[...], value[...]], axis=1))
-        parts.append(jax.nn.sigmoid(both[:, :WIDTH]) * both[:, WIDTH:])
+    every = dot(low, jnp.concatenate([lg[...], lv[...], rg[...], rv[...]], axis=1))
+    for n in (0, 2):
+        gate, value = (every[:, m * WIDTH : (m + 1) * WIDTH] for m in (n, n + 1))
+        parts.append(jax.nn.sigmoid(gate) * value)
     out_ref[...] = to_messages(parts, scratch)
 
 

time: 99.2 us -> 99.2 us (level)
  no operation moved by 1% of the time
where the time goes in v11:
time: 99.2 us; the launch traced here: 98.9 us
  blocking collectives  90.2 us (91%)
  Pallas kernels  8.03 us (8%)
    all_to_all x4, blocking collectives, spread(): lax.all_to_all(paired, SPREAD, 0, 0, tiled=True).reshape(messages.shape)  90.2 us
    pallas_call x12, Pallas kernels, call(): pl.pallas_call(kernel, out_shape=[jax.ShapeDtypeStruct(shape, dtype) for...  8.03 us
  transfers between devices with their start and end apart: 2, of which 0 were waited for; matrix products, arithmetic and copies ran while one was open for 0% of the time, Pallas kernels for 3%

profile of v11, /device:TPU:32, one launch (start us, length us, event | category | flops | bytes accessed | tf_op | source)
XLA Modules:
  0.0 98.9 jit_solution(17155936501045480774)
XLA Ops:
  0.0 1.8 %edges.1 = bf16[1280,128]{1,0:T(8,128)(2,1)S(1)} custom-call(bf16[576,128]{1,0:T(8,128)(2,1)} %bitcast.11, f32[24,24]{1,0:T(8,128)} %refs_9_.3, f32[24,24]{1,0:T(8,128)} %refs_10_.3, s32[24,24]{1,0:T(8,128)} %refs_11_.3, bf16[128,128]{1,0:T(8,128)(2,1)} %lg.1, bf16[128,128]{1,0:T(8,128)(2,1)} %lv.1, bf16[128,128]{1,0:T(8,128)(2,1)} %rg.1, bf16[128,128]{1,0:T(8,128)(2,1)} %rv.1), custom_call_target="tpu_custom_call" | custom-call | tf_op jit(solution)/shard_map/edges/pallas_call | solution.py:357
  1.8 30.6 %all_to_all.20 = bf16[128,5,2,128]{3,2,1,0:T(2,128)(2,1)S(1)} all-to-all(bf16[128,5,2,128]{3,2,1,0:T(2,128)(2,1)S(1)} %bitcast.20), channel_id=1, replica_groups=mesh['z_lo'=2,'x'=4,'core'=2,'z_hi'=4,'y'=4] {'z_hi','y','z_lo','x'}, dimensions={0} | all-to-all | bytes 655360 | tf_op jit(solution)/shard_map/all_to_all | solution.py:370
  32.4 0.3 take_right.1
  32.7 0.1 collective-permute-start
  32.8 0.3 take_left.1.left_ref.refs_7_
  33.1 0.4 mix_own.1.own_ref
  33.5 0.7 ready.1
  34.2 0.0 copy-start.2
  34.2 0.0 copy-start.3
  34.2 0.0 copy-start.4
  34.3 0.0 copy-start.5
  34.3 0.0 copy-start.10
  34.3 0.0 collective-permute-done.right_ref.other_ref
  34.3 0.4 mix.1
  34.7 19.4 %all_to_all.21 = bf16[128,3,2,128]{3,2,1,0:T(2,128)(2,1)S(1)} all-to-all(bf16[128,3,2,128]{3,2,1,0:T(2,128)(2,1)S(1)} %bitcast.24), channel_id=1, replica_groups=mesh['z_lo'=2,'x'=4,'core'=2,'z_hi'=4,'y'=4] {'z_hi','y','z_lo','x'}, dimensions={0} | all-to-all | bytes 393216 | tf_op jit(solution)/shard_map/all_to_all | solution.py:370
  54.1 0.6 middle.1
  54.8 18.1 %all_to_all.22 = bf16[128,3,2,128]{3,2,1,0:T(2,128)(2,1)S(1)} all-to-all(bf16[128,3,2,128]{3,2,1,0:T(2,128)(2,1)S(1)} %bitcast.27), channel_id=1, replica_groups=mesh['z_lo'=2,'x'=4,'core'=2,'z_hi'=4,'y'=4] {'z_hi','y','z_lo','x'}, dimensions={0} | all-to-all | bytes 393216 | tf_op jit(solution)/shard_map/all_to_all | solution.py:370
  72.9 0.4 right_grad.1
  73.3 0.1 collective-permute-start.1
  73.4 1.1 %right_grad_later.1 = (bf16[192,384]{1,0:T(8,128)(2,1)S(1)}, f32[192,384]{1,0:T(8,128)S(1)}, f32[576,128]{1,0:T(8,128)S(1)}, f32[576,128]{1,0:T(8,128)S(1)}, f32...) custom-call(bf16[192,384]{1,0:T(8,128)(2,1)S(1)} %get-tuple-element.43.refs_0_, ...), custom_call_target="tpu_custom_call" | custom-call | tf_op jit(solution)/shard_map/right_grad_later/pallas_call | solution.py:357
  74.6 0.5 left_grad.1.lines_ref
  75.1 0.3 return.1
  75.4 22.1 %all_to_all.23 = bf16[128,5,2,128]{3,2,1,0:T(2,128)(2,1)S(1)} all-to-all(bf16[128,5,2,128]{3,2,1,0:T(2,128)(2,1)S(1)} %bitcast.21), channel_id=1, replica_groups=mesh['z_lo'=2,'x'=4,'core'=2,'z_hi'=4,'y'=4] {'z_hi','y','z_lo','x'}, dimensions={0} | all-to-all | bytes 655360 | tf_op jit(solution)/shard_map/all_to_all | solution.py:370
  97.5 1.2 %last.1 = f32[576,128]{1,0:T(8,128)} custom-call(bf16[1280,128]{1,0:T(8,128)(2,1)S(1)} %bitcast.22, f32[576,128]{1,0:T(8,128)S(1)} %get-tuple-element.57.normed_ref, f32[576,128]{1,0:T(8,128)S(1)} %get-tuple-element.58.scale_ref, f32[576,128]{1,0:T(8,128)S(1)} %get-tuple-element.59.base_ref, f32[4,576,128]{2,1,0:T(8,128)S(1)} %get-tuple-element.60.factors_ref, ...), custom_call_target="tpu_custom_call" | custom-call | tf_op jit(solution)/shard_map/last/pallas_call | solution.py:357
  (18 shorter events, 0.0 us)
Async XLA Ops:
  0.0 32.4 %copy-start.9 = (f32[24,24]{1,0:T(8,128)S(1)}, f32[24,24]{1,0:T(8,128)}, u32[]{:S(2)}) copy-start(f32[24,24]{1,0:T(8,128)} %refs_10_.3) | copy-start | bytes 6916
  0.0 32.4 %copy-start.8 = (f32[24,24]{1,0:T(8,128)S(1)}, f32[24,24]{1,0:T(8,128)}, u32[]{:S(2)}) copy-start(f32[24,24]{1,0:T(8,128)} %refs_9_.3) | copy-start | bytes 6916
  0.0 32.4 %copy-start = (bf16[24,24,128]{2,1,0:T(8,128)(2,1)S(1)}, bf16[24,24,128]{2,1,0:T(8,128)(2,1)}, u32[]{:S(2)}) copy-start(bf16[24,24,128]{2,1,0:T(8,128)(2,1)} %param.11) | copy-start | bytes 442372
  0.0 32.4 %copy-start.7 = (bf16[128,128]{1,0:T(8,128)(2,1)S(1)}, bf16[128,128]{1,0:T(8,128)(2,1)}, u32[]{:S(2)}) copy-start(bf16[128,128]{1,0:T(8,128)(2,1)} %refs_14_.1) | copy-start | bytes 98308
  0.0 32.4 %copy-start.6 = (bf16[128,128]{1,0:T(8,128)(2,1)S(1)}, bf16[128,128]{1,0:T(8,128)(2,1)}, u32[]{:S(2)}) copy-start(bf16[128,128]{1,0:T(8,128)(2,1)} %refs_19_.1) | copy-start | bytes 98308
  0.0 32.4 %copy-start.1 = (bf16[24,24,128]{2,1,0:T(8,128)(2,1)S(1)}, bf16[24,24,128]{2,1,0:T(8,128)(2,1)}, u32[]{:S(2)}) copy-start(bf16[24,24,128]{2,1,0:T(8,128)(2,1)} %param.15) | copy-start | bytes 442372
  32.7 1.5 %collective-permute-start = (bf16[192,384]{1,0:T(8,128)(2,1)S(1)}, bf16[192,384]{1,0:T(8,128)(2,1)S(1)}, u32[]{:S(2)}, u32[]{:S(2)}) collective-permute-start(bf16[192,384]{1,0:T(8,128)(2,1)S(1)} %get-tuple-element.33.right_ref.own_ref), channel_id=1, source_target_pairs={{0,16},{16,0},{1,17},{17,1},{2,18},{18,2},{3,19},{19,3},{4,20},{20... | collective-permute-start | bytes 442376 | tf_op jit(solution)/shard_map/ppermute | solution.py:374
  34.2 38.7 %copy-start.2 = (bf16[128,128]{1,0:T(8,128)(2,1)S(1)}, bf16[128,128]{1,0:T(8,128)(2,1)}, u32[]{:S(2)}) copy-start(bf16[128,128]{1,0:T(8,128)(2,1)} %lg.1) | copy-start | bytes 98308
  34.2 38.7 %copy-start.3 = (bf16[128,128]{1,0:T(8,128)(2,1)S(1)}, bf16[128,128]{1,0:T(8,128)(2,1)}, u32[]{:S(2)}) copy-start(bf16[128,128]{1,0:T(8,128)(2,1)} %lv.1) | copy-start | bytes 98308
  34.2 38.6 %copy-start.4 = (bf16[128,128]{1,0:T(8,128)(2,1)S(1)}, bf16[128,128]{1,0:T(8,128)(2,1)}, u32[]{:S(2)}) copy-start(bf16[128,128]{1,0:T(8,128)(2,1)} %rg.1) | copy-start | bytes 98308
  34.3 38.6 %copy-start.5 = (bf16[128,128]{1,0:T(8,128)(2,1)S(1)}, bf16[128,128]{1,0:T(8,128)(2,1)}, u32[]{:S(2)}) copy-start(bf16[128,128]{1,0:T(8,128)(2,1)} %rv.1) | copy-start | bytes 98308
  34.3 38.6 %copy-start.10 = (s32[24,24]{1,0:T(8,128)S(1)}, s32[24,24]{1,0:T(8,128)}, u32[]{:S(2)}) copy-start(s32[24,24]{1,0:T(8,128)} %refs_11_.3) | copy-start | bytes 6916
  73.3 1.7 %collective-permute-start.1 = (bf16[192,384]{1,0:T(8,128)(2,1)S(1)}, bf16[192,384]{1,0:T(8,128)(2,1)S(1)}, u32[]{:S(2)}, u32[]{:S(2)}) collective-permute-start(bf16[192,384]{1,0:T(8,128)(2,1)S(1)} %get-tuple-element.56), channel_id=1, source_target_pairs={{0,16},{16,0},{1,17},{17,1},{2,18},{18,2},{3,19},{19,3},{4,20},{20... | collective-permute-start | bytes 442376 | tf_op jit(solution)/shard_map/ppermute | solution.py:374
